TPU v7x, 32 devices: a whole 2x2x4 slice. The times are simulated.
32 devices in a mesh: dp: 4 (over y, x), ctx: 8 (over z, core).
Axes of the slice: x: 2, y: 2, z: 4, core: 2. Of those that a mesh axis runs over, the one named last changes fastest.
Arguments:
- queries: bfloat16 [4, 1024, 2048], P('dp', 'ctx'), may hold values from -5 to 5
- key_rows: bfloat16 [4, 1024, 256], P('dp', 'ctx'), may hold values from -5 to 5
- value_stored_rows: bfloat16 [4, 1024, 256], P('dp', 'ctx'), may hold values from -6 to 6
- out_grad: bfloat16 [4, 1024, 2048], P('dp', 'ctx'), may hold values from -6 to 6
- documents: int32 [4, 1024], P('dp', 'ctx'), may hold values from 0 to 15, never falling along the last dimension, each value on 1 to 512 neighbouring positions
- swapped: int32 [4, 8, 4], P('dp', 'ctx'), may hold values from 0 to 1, as said below
Outputs:
- attended: bfloat16 [4, 1024, 2048], P('dp', 'ctx')
- query_grad: bfloat16 [4, 1024, 2048], P('dp', 'ctx')
- key_gradient_store: bfloat16 [4, 1024, 256], P('dp', 'ctx')
- value_gradient_store: bfloat16 [4, 1024, 256], P('dp', 'ctx')
Inputs may be any that keep to these rules, and one draw needn't show every extreme that they name: swapped[g, r, b] equals swapped[(g + 2) mod 4, r, b]. `documents`: document numbers never fall along a group's sequence; a document has 1 to 512 positions.
All inputs are finite; a program needn't handle non-finite values.
Results may differ from a plain program's by a relative error of at most 0.024.
Values may be sent and summed in bfloat16 or wider, within the bound.
No kernel may reach another device: no remote copies, remote signals or barrier semaphores. Data moves between devices by JAX's collectives and lax.ppermute only.
A program may use at most 64 MiB of HBM per device.

v0:
```python
import math

import jax
import jax.numpy as jnp
from jax import lax
from jax.sharding import PartitionSpec as P

HEAD_SIZE = 128
QUERY_PER_KEY = 8
KEY_VALUE_HEADS = 2
HQ = 16


def shifted_2(block, axis, distance):
    devices = range(lax.axis_size(axis))
    route = [((i - distance) % len(devices), i) for i in devices]
    return lax.ppermute(block, axis, route)


def pick_rows(own_part, their_part, swap_flags):
    row_total, feature_width = own_part.shape
    blocks = swap_flags.shape[0]
    chosen = (swap_flags == 1)[:, None, None]
    merged = jnp.where(
        chosen,
        their_part.reshape(blocks, row_total // blocks, feature_width),
        own_part.reshape(blocks, row_total // blocks, feature_width),
    )
    return merged.reshape(row_total, feature_width)


def attend(query_head, key_head, value_head, grad_head, doc_ids):
    sequence_length, head_width = query_head.shape
    tile_rows = min(512, sequence_length)
    tile_count = sequence_length // tile_rows
    score_scale = 1.0 / math.sqrt(head_width)
    offsets = jnp.arange(tile_rows, dtype=jnp.int32)

    def tile_of(source, index):
        return lax.dynamic_slice_in_dim(source, index * tile_rows, tile_rows, 0)

    def scores(row_tile, col_tile):
        raw_scores = (
            jnp.einsum(
                "qd,kd->qk",
                tile_of(query_head, row_tile),
                tile_of(key_head, col_tile),
                preferred_element_type=jnp.float32,
            )
            * score_scale
        )
        row_pos = row_tile * tile_rows + offsets
        col_pos = col_tile * tile_rows + offsets
        allowed = (col_pos[None, :] <= row_pos[:, None]) & (
            tile_of(doc_ids, col_tile)[None, :] == tile_of(doc_ids, row_tile)[:, None]
        )
        return jnp.where(allowed, raw_scores, -jnp.inf)

    def is_live(row_tile, col_tile):
        return col_tile <= row_tile

    def query_tile(row_tile, carry_state):
        attended, query_grad, key_gradient_store, value_gradient_store = carry_state
        query_part = tile_of(query_head, row_tile)
        grad_part = tile_of(grad_head, row_tile)

        def stats_step(col_tile, running):

            def stats_update(running):
                running_max, running_sum = running
                current = scores(row_tile, col_tile)
                new_max = jnp.maximum(running_max, jnp.max(current, axis=1))
                shifted = jnp.where(new_max == -jnp.inf, 0.0, new_max)
                new_sum = running_sum * jnp.exp(running_max - shifted) + jnp.sum(
                    jnp.exp(current - shifted[:, None]), axis=1
                )
                return (new_max, new_sum)

            return lax.cond(
                is_live(row_tile, col_tile), stats_update, lambda unchanged: unchanged, running
            )

        initial = (
            jnp.full((tile_rows,), -jnp.inf, jnp.float32),
            jnp.zeros((tile_rows,), jnp.float32),
        )
        running_max, running_sum = lax.fori_loop(0, tile_count, stats_step, initial)
        log_total = running_max + jnp.log(running_sum)

        def output_step(col_tile, running):

            def output_update(running):
                weights = jnp.exp(scores(row_tile, col_tile) - log_total[:, None]).astype(
                    jnp.bfloat16
                )
                return running + jnp.dot(
                    weights, tile_of(value_head, col_tile), preferred_element_type=jnp.float32
                )

            return lax.cond(
                is_live(row_tile, col_tile), output_update, lambda unchanged: unchanged, running
            )

        result = lax.fori_loop(
            0, tile_count, output_step, jnp.zeros((tile_rows, head_width), jnp.float32)
        ).astype(jnp.bfloat16)
        row_delta = jnp.sum(grad_part.astype(jnp.float32) * result.astype(jnp.float32), axis=1)

        def backward_step(col_tile, running):

            def backward_update(running):
                row_grad, key_total, value_total = running
                probabilities = jnp.exp(scores(row_tile, col_tile) - log_total[:, None])
                weights = probabilities.astype(jnp.bfloat16)
                value_portion = tile_of(value_head, col_tile)
                prob_grad = jnp.einsum(
                    "qd,kd->qk", grad_part, value_portion, preferred_element_type=jnp.float32
                )
                score_grad = (probabilities * (prob_grad - row_delta[:, None])).astype(jnp.bfloat16)
                row_grad = row_grad + jnp.dot(
                    score_grad, tile_of(key_head, col_tile), preferred_element_type=jnp.float32
                )
                key_add = jnp.einsum(
                    "qk,qd->kd", score_grad, query_part, preferred_element_type=jnp.float32
                )
                value_add = jnp.einsum(
                    "qk,qd->kd", weights, grad_part, preferred_element_type=jnp.float32
                )
                key_total = lax.dynamic_update_slice_in_dim(
                    key_total, tile_of(key_total, col_tile) + key_add, col_tile * tile_rows, 0
                )
                value_total = lax.dynamic_update_slice_in_dim(
                    value_total, tile_of(value_total, col_tile) + value_add, col_tile * tile_rows, 0
                )
                return (row_grad, key_total, value_total)

            return lax.cond(
                is_live(row_tile, col_tile), backward_update, lambda unchanged: unchanged, running
            )

        row_grad, key_gradient_store, value_gradient_store = lax.fori_loop(
            0,
            tile_count,
            backward_step,
            (
                jnp.zeros((tile_rows, head_width), jnp.float32),
                key_gradient_store,
                value_gradient_store,
            ),
        )
        attended = lax.dynamic_update_slice_in_dim(attended, result, row_tile * tile_rows, 0)
        query_grad = lax.dynamic_update_slice_in_dim(
            query_grad, (row_grad * score_scale).astype(jnp.bfloat16), row_tile * tile_rows, 0
        )
        return (attended, query_grad, key_gradient_store, value_gradient_store)

    initial = (
        jnp.zeros((sequence_length, head_width), jnp.bfloat16),
        jnp.zeros((sequence_length, head_width), jnp.bfloat16),
        jnp.zeros((sequence_length, head_width), jnp.float32),
        jnp.zeros((sequence_length, head_width), jnp.float32),
    )
    attended, query_grad, key_gradient_store, value_gradient_store = lax.fori_loop(
        0, tile_count, query_tile, initial
    )
    return (attended, query_grad, key_gradient_store * score_scale, value_gradient_store)


def local(queries, key_rows, value_stored_rows, out_grad, documents, swapped):
    partner_step = lax.axis_size("dp") // 2
    swap_flags = swapped[0, 0]
    own_rows = (queries[0], key_rows[0], value_stored_rows[0], out_grad[0])
    remote = shifted_2((own_rows[0], own_rows[1], own_rows[2], own_rows[3]), "dp", partner_step)
    query_home, key_home, value_home, grad_home = [
        pick_rows(own_part, their_part, swap_flags)
        for own_part, their_part in zip(own_rows, remote)
    ]
    doc_ids = lax.all_gather(documents[0], "ctx", axis=0, tiled=True)
    rank_count = lax.axis_size("ctx")
    heads_local = HQ // rank_count
    token_rows = query_home.shape[0]

    def widen(weight_matrix):
        return jnp.broadcast_to(
            weight_matrix.reshape(token_rows, KEY_VALUE_HEADS, 1, HEAD_SIZE),
            (token_rows, KEY_VALUE_HEADS, QUERY_PER_KEY, HEAD_SIZE),
        ).reshape(token_rows, HQ * HEAD_SIZE)

    query_seq, grad_seq, key_seq, value_seq = (
        lax.all_to_all(query_home, "ctx", split_axis=1, concat_axis=0, tiled=True),
        lax.all_to_all(grad_home, "ctx", split_axis=1, concat_axis=0, tiled=True),
        lax.all_to_all(widen(key_home), "ctx", split_axis=1, concat_axis=0, tiled=True),
        lax.all_to_all(widen(value_home), "ctx", split_axis=1, concat_axis=0, tiled=True),
    )
    key_list = [
        key_seq[:, index * HEAD_SIZE : (index + 1) * HEAD_SIZE] for index in range(heads_local)
    ]
    value_list = [
        value_seq[:, index * HEAD_SIZE : (index + 1) * HEAD_SIZE] for index in range(heads_local)
    ]
    outputs = [
        attend(
            query_seq[:, index * HEAD_SIZE : (index + 1) * HEAD_SIZE],
            key_list[index],
            value_list[index],
            grad_seq[:, index * HEAD_SIZE : (index + 1) * HEAD_SIZE],
            doc_ids,
        )
        for index in range(heads_local)
    ]
    attended_seq = jnp.concatenate([entry[0] for entry in outputs], axis=1)
    query_grad_seq = jnp.concatenate([entry[1] for entry in outputs], axis=1)
    attended_rows, query_grad_rows = (
        lax.all_to_all(attended_seq, "ctx", split_axis=0, concat_axis=1, tiled=True),
        lax.all_to_all(query_grad_seq, "ctx", split_axis=0, concat_axis=1, tiled=True),
    )
    key_grad_seq = jnp.concatenate([entry[2] for entry in outputs], axis=1)
    value_grad_seq = jnp.concatenate([entry[3] for entry in outputs], axis=1)
    key_returned_grad, value_returned_grad = (
        lax.all_to_all(key_grad_seq, "ctx", split_axis=0, concat_axis=1, tiled=True),
        lax.all_to_all(value_grad_seq, "ctx", split_axis=0, concat_axis=1, tiled=True),
    )
    key_gradient_store = (
        key_returned_grad.reshape(token_rows, KEY_VALUE_HEADS, QUERY_PER_KEY, HEAD_SIZE)
        .sum(axis=2)
        .reshape(token_rows, KEY_VALUE_HEADS * HEAD_SIZE)
    )
    value_gradient_store = (
        value_returned_grad.reshape(token_rows, KEY_VALUE_HEADS, QUERY_PER_KEY, HEAD_SIZE)
        .sum(axis=2)
        .reshape(token_rows, KEY_VALUE_HEADS * HEAD_SIZE)
    )
    outgoing = (
        attended_rows,
        query_grad_rows,
        key_gradient_store.astype(jnp.bfloat16),
        value_gradient_store.astype(jnp.bfloat16),
    )
    returned = shifted_2((outgoing[0], outgoing[1], outgoing[2], outgoing[3]), "dp", partner_step)
    finals = [
        pick_rows(own_part, their_part, swap_flags)[None]
        for own_part, their_part in zip(outgoing, returned)
    ]
    return (finals[0], finals[1], finals[2], finals[3])


def solution(mesh):
    in_specs = (
        P("dp", "ctx", None),
        P("dp", "ctx", None),
        P("dp", "ctx", None),
        P("dp", "ctx", None),
        P("dp", "ctx"),
        P("dp", "ctx", None),
    )
    out_specs = (
        P("dp", "ctx", None),
        P("dp", "ctx", None),
        P("dp", "ctx", None),
        P("dp", "ctx", None),
    )
    return jax.shard_map(local, mesh=mesh, in_specs=in_specs, out_specs=out_specs, check_vma=False)
```

profile of v0, /device:TPU:0, one launch (start us, length us, event | category | flops | bytes accessed | tf_op | source)
XLA Modules:
  0.0 239.3 jit_solution(2711447711015158766)
XLA Ops:
  0.6 3.0 %collective-permute-start.2 = (bf16[128,256]{1,0:T(8,128)(2,1)}, bf16[128,256]{1,0:T(8,128)(2,1)S(1)}, u32[]{:S(2)}, u32[]{:S(2)}) collective-permute-start(bf16[128,256]{1,0:T(8,128)(2,1)} %bitcast.99), channel_id=1, source_target_pairs={{16,0},{24,8},{0,16},{8,24},{17,1},{25,9},{1,17},{9,25},{18,2},{26... | collective-permute-start | bytes 196616 | tf_op jit(solution)/shard_map/ppermute | solution.py:17
  5.1 1.2 collective-permute-done.2
  6.4 1.7 collective-permute-done.1
  9.2 5.0 %all-to-all-start.1 = ((bf16[128,8,256]{0,2,1:T(8,128)(2,1)}), bf16[128,8,256]{0,2,1:T(8,128)(2,1)S(1)}, u32[]{:S(2)}, u32[]{:S(2)}) async-start(bf16[128,8,256]{0,2,1:T(8,128)(2,1)} %bitcast.11), calls=%async_computation.1 | async-start | bytes 1048576 | tf_op jit(solution)/shard_map/all_to_all | solution.py:192
  15.8 1.1 collective-permute-start.3
  16.9 12.6 %all-to-all-done.1 = bf16[128,8,256]{0,2,1:T(8,128)(2,1)S(1)} async-done(((bf16[128,8,256]{0,2,1:T(8,128)(2,1)}), bf16[128,8,256]{0,2,1:T(8,128)(2,1)S(1)}, u32[]{:S(2)}, u32[]{:S(2)}) %all-to-all-start.1) | async-done | bytes 524320 | tf_op jit(solution)/shard_map/all_to_all | solution.py:192
  30.5 3.5 %all-to-all-start.2 = ((bf16[128,8,256]{0,2,1:T(8,128)(2,1)}), bf16[128,8,256]{0,2,1:T(8,128)(2,1)S(1)}, u32[]{:S(2)}, u32[]{:S(2)}) async-start(bf16[128,8,256]{0,2,1:T(8,128)(2,1)} %bitcast.17), calls=%async_computation.2 | async-start | bytes 1048576 | tf_op jit(solution)/shard_map/all_to_all | solution.py:193
  34.8 5.5 %collective-permute-done.3 = bf16[128,2048]{0,1:T(8,128)(2,1)} collective-permute-done((bf16[128,2048]{0,1:T(8,128)(2,1)S(1)}, bf16[128,2048]{0,1:T(8,128)(2,1)}, u32[]{:S(2)}, u32[]{:S(2)}) %collective-permute-start.3) | collective-permute-done | bytes 524320 | tf_op jit(solution)/shard_map/ppermute | solution.py:17
  40.2 1.4 broadcast_select_fusion
  42.6 6.6 %all-to-all-done.2 = bf16[128,8,256]{0,2,1:T(8,128)(2,1)S(1)} async-done(((bf16[128,8,256]{0,2,1:T(8,128)(2,1)}), bf16[128,8,256]{0,2,1:T(8,128)(2,1)S(1)}, u32[]{:S(2)}, u32[]{:S(2)}) %all-to-all-start.2) | async-done | bytes 524320 | tf_op jit(solution)/shard_map/all_to_all | solution.py:193
  49.2 3.5 %all-to-all-start = ((bf16[128,8,256]{2,0,1:T(8,128)(2,1)}), bf16[128,8,256]{2,0,1:T(8,128)(2,1)S(1)}, u32[]{:S(2)}, u32[]{:S(2)}) async-start(bf16[128,8,256]{2,0,1:T(8,128)(2,1)} %copy.57), calls=%async_computation | async-start | bytes 1048576 | tf_op jit(solution)/shard_map/all_to_all | solution.py:190
  53.8 14.3 %all-to-all-done = bf16[128,8,256]{2,0,1:T(8,128)(2,1)S(1)} async-done(((bf16[128,8,256]{2,0,1:T(8,128)(2,1)}), bf16[128,8,256]{2,0,1:T(8,128)(2,1)S(1)}, u32[]{:S(2)}, u32[]{:S(2)}) %all-to-all-start) | async-done | bytes 524320 | tf_op jit(solution)/shard_map/all_to_all | solution.py:190
  68.0 3.5 %all-to-all-start.3 = ((bf16[128,8,256]{2,0,1:T(8,128)(2,1)}), bf16[128,8,256]{2,0,1:T(8,128)(2,1)S(1)}, u32[]{:S(2)}, u32[]{:S(2)}) async-start(bf16[128,8,256]{2,0,1:T(8,128)(2,1)} %copy.65), calls=%async_computation.3 | async-start | bytes 1048576 | tf_op jit(solution)/shard_map/all_to_all | solution.py:191
  72.2 15.5 %all-gather = s32[1,1024]{1,0:T(1,128)S(1)} all-gather(s32[1,128]{1,0:T(1,128)S(1)} %copy-done.11), channel_id=2, replica_groups=mesh['dp'=4,'ctx'=8] {'ctx'}, dimensions={1}, use_global_device_ids=true | all-gather | bytes 4608 | tf_op jit(solution)/shard_map/all_gather | solution.py:178
  88.9 1.2 fusion.105
  93.1 12.6 %while.247 = (s32[]{:T(128)}, bf16[1024,128]{1,0:T(8,128)(2,1)}, bf16[1024,128]{1,0:T(8,128)(2,1)}, f32[1024,128]{1,0:T(8,128)S(1)}, f32[1024,128]{1,0:T(8,128)S...) while((s32[]{:T(128)}, bf16[1024,128]{1,0:T(8,128)(2,1)}, ...), condition=%wide.region_16.17_spmd.clone.clone, body=%wide.region_0.16_spmd.clone.clone.sunk | while | flops 544217088 | bytes 12708980 | solution.py:163
  94.9 2.0 while.254
  95.0 1.9 conditional.23
  97.7 1.5 while.252
  99.3 1.5 while.253
  101.0 3.9 %while.254 = (s32[]{:T(128)}, f32[512,128]{1,0:T(8,128)S(1)}, f32[1024,128]{1,0:T(8,128)S(1)}, f32[1024,128]{1,0:T(8,128)S(1)}, s32[]{:T(128)}, /*index=5*/s32[5...) while((s32[]{:T(128)}, f32[512,128]{1,0:T(8,128)S(1)}, ...), condition=%wide.region_15.15_spmd.clone, body=%wide.region_12.14_spmd.clone.sunk | while | flops 338363392 | bytes 7238095 | solution.py:141
  101.0 1.9 conditional.23
  103.0 1.9 conditional.23
  107.3 24.3 %while.251 = (s32[]{:T(128)}, bf16[1024,128]{1,0:T(8,128)(2,1)}, bf16[1024,128]{1,0:T(8,128)(2,1)}, f32[1024,128]{1,0:T(8,128)S(1)}, f32[1024,128]{1,0:T(8,128)S...) while((s32[]{:T(128)}, bf16[1024,128]{1,0:T(8,128)(2,1)}, ...), condition=%wide.region_33.34_spmd.clone.clone, body=%wide.region_17.33_spmd.clone.clone.sunk | while | flops 544217088 | bytes 12708980 | solution.py:163
  107.3 1.6 while.255
  107.3 1.6 conditional.18
  107.4 1.3 fusion.101
  109.0 1.7 while.256
  109.0 1.6 conditional.19
  109.1 1.5 fusion.58
  112.7 2.9 %while.257 = (s32[]{:T(128)}, f32[512,128]{1,0:T(8,128)S(1)}, f32[1024,128]{1,0:T(8,128)S(1)}, f32[1024,128]{1,0:T(8,128)S(1)}, s32[]{:T(128)}, /*index=5*/s32[5...) while((s32[]{:T(128)}, f32[512,128]{1,0:T(8,128)S(1)}, ...), condition=%wide.region_32.32_spmd.clone, body=%wide.region_29.31_spmd.clone.sunk | while | flops 338363392 | bytes 7238095 | solution.py:141
  112.8 2.9 %conditional.20 = ((f32[512,128]{1,0:T(8,128)S(1)}, f32[1024,128]{1,0:T(8,128)S(1)}, f32[1024,128]{1,0:T(8,128)S(1)})) conditional(s32[]{:T(128)} %convert_element_type.214, (f32[512,128]{1,0:T(8,128)S(1)}, f32[1024,128]{1,0:T(8,128)S(1)}, f32[1024,128]{1,0:T(8,128)S(1)}) %tuple.372, (s32[]{:T(128)}, s32[512]{0:T(512)S(1)}, s32[]{:T(128)}, ...), branch_computations={%region_30.29_spmd, %region_31.30_spmd} | conditional | flops 338363392 | bytes 7237796 | solution.py:137
  112.9 1.4 fusion.82
  116.4 3.3 %while.255 = (s32[]{:T(128)}, f32[512]{0:T(512)S(1)}, f32[512]{0:T(512)S(1)}, s32[]{:T(128)}, s32[512]{0:T(512)S(1)}, /*index=5*/s32[1024]{0:T(1024)S(1)}, bf16[...) while((s32[]{:T(128)}, f32[512]{0:T(512)S(1)}, f32[512]{0:T(512)S(1)}, s32[]{:T(128)}, ...), condition=%wide.region_23.23_spmd.clone, body=%wide.region_18.22_spmd.clone.sunk | while | flops 69210120 | bytes 2412879 | solution.py:87
  116.4 1.6 conditional.18
  116.6 1.3 fusion.101
  118.1 1.6 conditional.18
  118.2 1.3 fusion.101
  119.8 3.3 %while.256 = (s32[]{:T(128)}, f32[512,128]{1,0:T(8,128)S(1)}, s32[]{:T(128)}, s32[512]{0:T(512)S(1)}, s32[1024]{0:T(1024)S(1)}, /*index=5*/bf16[1024,128]{1,0:T(...) while((s32[]{:T(128)}, f32[512,128]{1,0:T(8,128)S(1)}, ...), condition=%wide.region_27.27_spmd.clone, body=%wide.region_24.26_spmd.clone.sunk | while | flops 136119296 | bytes 945975 | solution.py:104
  119.8 1.6 conditional.19
  119.9 1.5 fusion.58
  121.5 1.6 conditional.19
  121.6 1.5 fusion.58
  125.1 5.8 %while.257 = (s32[]{:T(128)}, f32[512,128]{1,0:T(8,128)S(1)}, f32[1024,128]{1,0:T(8,128)S(1)}, f32[1024,128]{1,0:T(8,128)S(1)}, s32[]{:T(128)}, /*index=5*/s32[5...) while((s32[]{:T(128)}, f32[512,128]{1,0:T(8,128)S(1)}, ...), condition=%wide.region_32.32_spmd.clone, body=%wide.region_29.31_spmd.clone.sunk | while | flops 338363392 | bytes 7238095 | solution.py:141
  125.2 2.8 %conditional.20 = ((f32[512,128]{1,0:T(8,128)S(1)}, f32[1024,128]{1,0:T(8,128)S(1)}, f32[1024,128]{1,0:T(8,128)S(1)})) conditional(s32[]{:T(128)} %convert_element_type.214, (f32[512,128]{1,0:T(8,128)S(1)}, f32[1024,128]{1,0:T(8,128)S(1)}, f32[1024,128]{1,0:T(8,128)S(1)}) %tuple.372, (s32[]{:T(128)}, s32[512]{0:T(512)S(1)}, s32[]{:T(128)}, ...), branch_computations={%region_30.29_spmd, %region_31.30_spmd} | conditional | flops 338363392 | bytes 7237796 | solution.py:137
  125.3 1.4 fusion.82
  128.0 2.9 %conditional.20 = ((f32[512,128]{1,0:T(8,128)S(1)}, f32[1024,128]{1,0:T(8,128)S(1)}, f32[1024,128]{1,0:T(8,128)S(1)})) conditional(s32[]{:T(128)} %convert_element_type.214, (f32[512,128]{1,0:T(8,128)S(1)}, f32[1024,128]{1,0:T(8,128)S(1)}, f32[1024,128]{1,0:T(8,128)S(1)}) %tuple.372, (s32[]{:T(128)}, s32[512]{0:T(512)S(1)}, s32[]{:T(128)}, ...), branch_computations={%region_30.29_spmd, %region_31.30_spmd} | conditional | flops 338363392 | bytes 7237796 | solution.py:137
  128.1 1.4 fusion.82
  131.7 1.9 pad_maximum_fusion.2
  133.5 4.9 %all-to-all-start.4 = ((bf16[8,128,256]{2,1,0:T(8,128)(2,1)}), bf16[8,128,256]{2,1,0:T(8,128)(2,1)S(1)}, u32[]{:S(2)}, u32[]{:S(2)}) async-start(bf16[8,128,256]{2,1,0:T(8,128)(2,1)} %bitcast.26), calls=%async_computation.4 | async-start | bytes 1048576 | tf_op jit(solution)/shard_map/all_to_all | solution.py:214
  139.3 14.5 %all-to-all-done.4 = bf16[8,128,256]{2,1,0:T(8,128)(2,1)S(1)} async-done(((bf16[8,128,256]{2,1,0:T(8,128)(2,1)}), bf16[8,128,256]{2,1,0:T(8,128)(2,1)S(1)}, u32[]{:S(2)}, u32[]{:S(2)}) %all-to-all-start.4) | async-done | bytes 524320 | tf_op jit(solution)/shard_map/all_to_all | solution.py:214
  153.8 3.5 %all-to-all-start.5 = ((bf16[8,128,256]{2,1,0:T(8,128)(2,1)}), bf16[8,128,256]{2,1,0:T(8,128)(2,1)S(1)}, u32[]{:S(2)}, u32[]{:S(2)}) async-start(bf16[8,128,256]{2,1,0:T(8,128)(2,1)} %bitcast.84), calls=%async_computation.5 | async-start | bytes 1048576 | tf_op jit(solution)/shard_map/all_to_all | solution.py:215
  157.4 1.1 pad_maximum_fusion
  158.5 14.1 %all-to-all-done.5 = bf16[8,128,256]{2,1,0:T(8,128)(2,1)S(1)} async-done(((bf16[8,128,256]{2,1,0:T(8,128)(2,1)}), bf16[8,128,256]{2,1,0:T(8,128)(2,1)S(1)}, u32[]{:S(2)}, u32[]{:S(2)}) %all-to-all-start.5) | async-done | bytes 524320 | tf_op jit(solution)/shard_map/all_to_all | solution.py:215
  173.4 3.6 %all-to-all-start.6 = ((f32[8,128,256]{2,1,0:T(8,128)}), f32[8,128,256]{2,1,0:T(8,128)S(1)}, u32[]{:S(2)}, u32[]{:S(2)}) async-start(f32[8,128,256]{2,1,0:T(8,128)} %bitcast.34), calls=%async_computation.6 | async-start | bytes 2097152 | tf_op jit(solution)/shard_map/all_to_all | solution.py:220
  177.0 1.2 pad_maximum_fusion.1
  178.1 25.3 %all-to-all-done.6 = f32[8,128,256]{2,1,0:T(8,128)S(1)} async-done(((f32[8,128,256]{2,1,0:T(8,128)}), f32[8,128,256]{2,1,0:T(8,128)S(1)}, u32[]{:S(2)}, u32[]{:S(2)}) %all-to-all-start.6) | async-done | bytes 1048608 | tf_op jit(solution)/shard_map/all_to_all | solution.py:220
  203.5 3.6 %all-to-all-start.7 = ((f32[8,128,256]{2,1,0:T(8,128)}), f32[8,128,256]{2,1,0:T(8,128)S(1)}, u32[]{:S(2)}, u32[]{:S(2)}) async-start(f32[8,128,256]{2,1,0:T(8,128)} %bitcast.39), calls=%async_computation.7 | async-start | bytes 2097152 | tf_op jit(solution)/shard_map/all_to_all | solution.py:221
  209.4 1.1 collective-permute-start.5
  210.5 1.3 copy.68
  211.8 1.3 reduce_sum.62
  213.2 1.1 collective-permute-start.6
  214.3 19.3 %all-to-all-done.7 = f32[8,128,256]{2,1,0:T(8,128)S(1)} async-done(((f32[8,128,256]{2,1,0:T(8,128)}), f32[8,128,256]{2,1,0:T(8,128)S(1)}, u32[]{:S(2)}, u32[]{:S(2)}) %all-to-all-start.7) | async-done | bytes 1048608 | tf_op jit(solution)/shard_map/all_to_all | solution.py:221
  235.2 1.3 select_bitcast_fusion
  (217 shorter events, 51.5 us)
Async XLA Ops:
  0.6 3.1 %copy-start.12 = (s32[1,1,4]{2,1,0:T(1,128)S(1)}, s32[1,1,4]{2,1,0:T(1,128)}, u32[]{:S(2)}) copy-start(s32[1,1,4]{2,1,0:T(1,128)} %param.39) | copy-start | bytes 52
  0.6 5.6 %collective-permute-start.2 = (bf16[128,256]{1,0:T(8,128)(2,1)}, bf16[128,256]{1,0:T(8,128)(2,1)S(1)}, u32[]{:S(2)}, u32[]{:S(2)}) collective-permute-start(bf16[128,256]{1,0:T(8,128)(2,1)} %bitcast.99), channel_id=1, source_target_pairs={{16,0},{24,8},{0,16},{8,24},{17,1},{25,9},{1,17},{9,25},{18,2},{26... | collective-permute-start | bytes 196616 | tf_op jit(solution)/shard_map/ppermute | solution.py:17
  3.7 4.5 %collective-permute-start.1 = (bf16[128,256]{1,0:T(8,128)(2,1)}, bf16[128,256]{1,0:T(8,128)(2,1)S(1)}, u32[]{:S(2)}, u32[]{:S(2)}) collective-permute-start(bf16[128,256]{1,0:T(8,128)(2,1)} %bitcast.100), channel_id=1, source_target_pairs={{16,0},{24,8},{0,16},{8,24},{17,1},{25,9},{1,17},{9,25},{18,2},{26... | collective-permute-start | bytes 196616 | tf_op jit(solution)/shard_map/ppermute | solution.py:17
  3.8 1.0 copy-start.8
  5.1 35.2 %copy-start.9 = (pred[128]{0:T(512)(128)(4,1)}, pred[128]{0:T(512)(128)(4,1)S(1)}, u32[]{:S(2)}) copy-start(pred[128]{0:T(512)(128)(4,1)S(1)} %broadcast_in_dim.117) | copy-start | bytes 388
  9.2 5.0 %copy-start.5 = (bf16[1,128,2048]{2,1,0:T(8,128)(2,1)S(1)}, bf16[1,128,2048]{2,1,0:T(8,128)(2,1)}, u32[]{:S(2)}) copy-start(bf16[1,128,2048]{2,1,0:T(8,128)(2,1)} %param.34) | copy-start | bytes 1572868
  9.2 20.4 %all-to-all-start.1 = ((bf16[128,8,256]{0,2,1:T(8,128)(2,1)}), bf16[128,8,256]{0,2,1:T(8,128)(2,1)S(1)}, u32[]{:S(2)}, u32[]{:S(2)}) async-start(bf16[128,8,256]{0,2,1:T(8,128)(2,1)} %bitcast.11), calls=%async_computation.1 | async-start | bytes 1048576 | tf_op jit(solution)/shard_map/all_to_all | solution.py:192
  14.2 1.3 copy-start.6
  14.5 19.5 %collective-permute-start = (bf16[128,2048]{0,1:T(8,128)(2,1)S(1)}, bf16[128,2048]{0,1:T(8,128)(2,1)S(1)}, u32[]{:S(2)}, u32[]{:S(2)}) collective-permute-start(bf16[128,2048]{0,1:T(8,128)(2,1)S(1)} %bitcast.87), channel_id=1, source_target_pairs={{16,0},{24,8},{0,16},{8,24},{17,1},{25,9},{1,17},{9,25},{18,2},{26... | collective-permute-start | bytes 1572872 | tf_op jit(solution)/shard_map/ppermute | solution.py:17
  15.8 24.4 %collective-permute-start.3 = (bf16[128,2048]{0,1:T(8,128)(2,1)S(1)}, bf16[128,2048]{0,1:T(8,128)(2,1)}, u32[]{:S(2)}, u32[]{:S(2)}) collective-permute-start(bf16[128,2048]{0,1:T(8,128)(2,1)S(1)} %bitcast.88), channel_id=1, source_target_pairs={{16,0},{24,8},{0,16},{8,24},{17,1},{25,9},{1,17},{9,25},{18,2},{26... | collective-permute-start | bytes 1572872 | tf_op jit(solution)/shard_map/ppermute | solution.py:17
  30.5 18.8 %all-to-all-start.2 = ((bf16[128,8,256]{0,2,1:T(8,128)(2,1)}), bf16[128,8,256]{0,2,1:T(8,128)(2,1)S(1)}, u32[]{:S(2)}, u32[]{:S(2)}) async-start(bf16[128,8,256]{0,2,1:T(8,128)(2,1)} %bitcast.17), calls=%async_computation.2 | async-start | bytes 1048576 | tf_op jit(solution)/shard_map/all_to_all | solution.py:193
  34.0 0.8 copy-start.7
  49.2 18.8 %all-to-all-start = ((bf16[128,8,256]{2,0,1:T(8,128)(2,1)}), bf16[128,8,256]{2,0,1:T(8,128)(2,1)S(1)}, u32[]{:S(2)}, u32[]{:S(2)}) async-start(bf16[128,8,256]{2,0,1:T(8,128)(2,1)} %copy.57), calls=%async_computation | async-start | bytes 1048576 | tf_op jit(solution)/shard_map/all_to_all | solution.py:190
  68.0 22.8 %all-to-all-start.3 = ((bf16[128,8,256]{2,0,1:T(8,128)(2,1)}), bf16[128,8,256]{2,0,1:T(8,128)(2,1)S(1)}, u32[]{:S(2)}, u32[]{:S(2)}) async-start(bf16[128,8,256]{2,0,1:T(8,128)(2,1)} %copy.65), calls=%async_computation.3 | async-start | bytes 1048576 | tf_op jit(solution)/shard_map/all_to_all | solution.py:191
  71.5 0.7 copy-start.11
  133.5 4.9 %copy-start.3 = (bf16[1024,128]{1,0:T(8,128)(2,1)S(1)}, bf16[1024,128]{1,0:T(8,128)(2,1)}, u32[]{:S(2)}) copy-start(bf16[1024,128]{1,0:T(8,128)(2,1)} %get-tuple-element.1899) | copy-start | bytes 786436
  133.5 4.9 %copy-start.4 = (bf16[1024,128]{1,0:T(8,128)(2,1)S(1)}, bf16[1024,128]{1,0:T(8,128)(2,1)}, u32[]{:S(2)}) copy-start(bf16[1024,128]{1,0:T(8,128)(2,1)} %get-tuple-element.1898) | copy-start | bytes 786436
  133.5 20.3 %all-to-all-start.4 = ((bf16[8,128,256]{2,1,0:T(8,128)(2,1)}), bf16[8,128,256]{2,1,0:T(8,128)(2,1)S(1)}, u32[]{:S(2)}, u32[]{:S(2)}) async-start(bf16[8,128,256]{2,1,0:T(8,128)(2,1)} %bitcast.26), calls=%async_computation.4 | async-start | bytes 1048576 | tf_op jit(solution)/shard_map/all_to_all | solution.py:214
  153.8 18.8 %all-to-all-start.5 = ((bf16[8,128,256]{2,1,0:T(8,128)(2,1)}), bf16[8,128,256]{2,1,0:T(8,128)(2,1)S(1)}, u32[]{:S(2)}, u32[]{:S(2)}) async-start(bf16[8,128,256]{2,1,0:T(8,128)(2,1)} %bitcast.84), calls=%async_computation.5 | async-start | bytes 1048576 | tf_op jit(solution)/shard_map/all_to_all | solution.py:215
  172.6 0.8 copy-start
  173.4 30.1 %all-to-all-start.6 = ((f32[8,128,256]{2,1,0:T(8,128)}), f32[8,128,256]{2,1,0:T(8,128)S(1)}, u32[]{:S(2)}, u32[]{:S(2)}) async-start(f32[8,128,256]{2,1,0:T(8,128)} %bitcast.34), calls=%async_computation.6 | async-start | bytes 2097152 | tf_op jit(solution)/shard_map/all_to_all | solution.py:220
  203.5 30.1 %all-to-all-start.7 = ((f32[8,128,256]{2,1,0:T(8,128)}), f32[8,128,256]{2,1,0:T(8,128)S(1)}, u32[]{:S(2)}, u32[]{:S(2)}) async-start(f32[8,128,256]{2,1,0:T(8,128)} %bitcast.39), calls=%async_computation.7 | async-start | bytes 2097152 | tf_op jit(solution)/shard_map/all_to_all | solution.py:221
  207.0 2.0 copy-start.1
  208.1 27.1 %collective-permute-start.4 = (bf16[128,2048]{0,1:T(8,128)(2,1)}, bf16[128,2048]{0,1:T(8,128)(2,1)}, u32[]{:S(2)}, u32[]{:S(2)}) collective-permute-start(bf16[128,2048]{0,1:T(8,128)(2,1)} %bitcast.85), channel_id=1, source_target_pairs={{16,0},{24,8},{0,16},{8,24},{17,1},{25,9},{1,17},{9,25},{18,2},{26... | collective-permute-start | bytes 1572872 | tf_op jit(solution)/shard_map/ppermute | solution.py:17
  209.4 25.8 %collective-permute-start.5 = (bf16[128,2048]{0,1:T(8,128)(2,1)S(1)}, bf16[128,2048]{0,1:T(8,128)(2,1)}, u32[]{:S(2)}, u32[]{:S(2)}) collective-permute-start(bf16[128,2048]{0,1:T(8,128)(2,1)S(1)} %bitcast.86), channel_id=1, source_target_pairs={{16,0},{24,8},{0,16},{8,24},{17,1},{25,9},{1,17},{9,25},{18,2},{26... | collective-permute-start | bytes 1572872 | tf_op jit(solution)/shard_map/ppermute | solution.py:17
  213.2 25.3 %collective-permute-start.6 = (bf16[128,256]{1,0:T(8,128)(2,1)S(1)}, bf16[128,256]{1,0:T(8,128)(2,1)S(1)}, u32[]{:S(2)}, u32[]{:S(2)}) collective-permute-start(bf16[128,256]{1,0:T(8,128)(2,1)S(1)} %copy.69), channel_id=1, source_target_pairs={{16,0},{24,8},{0,16},{8,24},{17,1},{25,9},{1,17},{9,25},{18,2},{26... | collective-permute-start | bytes 196616 | tf_op jit(solution)/shard_map/ppermute | solution.py:17
  233.9 1.3 copy-start.2
  234.0 1.2 copy-start.10
  234.1 4.4 %collective-permute-start.7 = (bf16[128,256]{1,0:T(8,128)(2,1)S(1)}, bf16[128,256]{1,0:T(8,128)(2,1)S(1)}, u32[]{:S(2)}, u32[]{:S(2)}) collective-permute-start(bf16[128,256]{1,0:T(8,128)(2,1)S(1)} %copy.72), channel_id=1, source_target_pairs={{16,0},{24,8},{0,16},{8,24},{17,1},{25,9},{1,17},{9,25},{18,2},{26... | collective-permute-start | bytes 196616 | tf_op jit(solution)/shard_map/ppermute | solution.py:17
where the time goes:
time: 240 us; the launch traced here: 239 us
  waiting for transfers between devices  115 us (48%)
  starting transfers between devices  40.5 us (17%)
  matrix products  24.9 us (10%)
  local copies, waits for them, and re-layouts  23.8 us (10%)
  other arithmetic  16.7 us (7%)
  blocking collectives  15.5 us (6%)
    all_to_all x1, waiting for transfers between devices, local(): lax.all_to_all(key_grad_seq, 'ctx', split_axis=0, concat_axis=1, tiled=True)  25.3 us
    all_to_all x1, waiting for transfers between devices, local(): lax.all_to_all(value_grad_seq, 'ctx', split_axis=0, concat_axis=1, tiled=...  19.3 us
    all_gather x1, blocking collectives, local(): doc_ids = lax.all_gather(documents[0], 'ctx', axis=0, tiled=True)  15.5 us
    all_to_all x1, waiting for transfers between devices, local(): lax.all_to_all(attended_seq, 'ctx', split_axis=0, concat_axis=1, tiled=True)  14.5 us
    all_to_all x1, waiting for transfers between devices, local(): lax.all_to_all(query_home, 'ctx', split_axis=1, concat_axis=0, tiled=True)  14.3 us
    all_to_all x1, waiting for transfers between devices, local(): lax.all_to_all(query_grad_seq, 'ctx', split_axis=0, concat_axis=1, tiled=...  14.1 us
    all_to_all x1, waiting for transfers between devices, local(): lax.all_to_all(widen(key_home), 'ctx', split_axis=1, concat_axis=0, tiled...  12.6 us
    dot_general x12, matrix products, scores(): jnp.einsum('qd,kd->qk', tile_of(query_head, row_tile), tile_of(key_head,...  10.5 us
  transfers between devices with their start and end apart: 16, of which 10 were waited for; matrix products, arithmetic and copies ran while one was open for 9% of the time, Pallas kernels for 0%

commit v1 on v0

v1 whole, which is shorter than its diff:
```python
import functools
import math

import jax
import jax.numpy as jnp
from jax import lax
from jax.experimental import pallas as pl
from jax.experimental.pallas import tpu as pltpu
from jax.sharding import Mesh
from jax.sharding import PartitionSpec as P

HEAD_SIZE = 128
QUERY_PER_KEY = 8
KEY_VALUE_HEADS = 2
NBLK = 4
META = 16
FLAG_ROW, TILED_ROW, DOC_ROW = 0, 4, 8
NEG = -1e30
F32, BF16 = jnp.float32, jnp.bfloat16
NT = (((1,), (1,)), ((), ()))


def payload_of(key_rows, value_rows, docs, flags):
    rows, width = key_rows.shape
    per_block = rows // NBLK
    flag_rows = jnp.broadcast_to(flags.astype(BF16)[:, None], (NBLK, width))
    docs = docs.astype(BF16)
    tiled = jnp.tile(docs.reshape(NBLK, per_block), (1, width // per_block))
    doc_row = jnp.tile(docs.reshape(1, rows), (1, width // rows))
    meta = jnp.concatenate(
        [flag_rows, tiled, doc_row, jnp.zeros((META - 2 * NBLK - 1, width), BF16)], axis=0
    )
    return jnp.concatenate([key_rows, value_rows, meta], axis=0)


def attention_kernel(
    window,
    place_ref,
    swap_ref,
    query_ref,
    grad_ref,
    gathered_ref,
    out_ref,
    query_grad_ref,
    partial_ref,
    key_log,
    value_log,
    key_turned,
    value_turned,
    doc_column,
    doc_row,
    key_total,
    value_total,
):
    rows = query_ref.shape[0]
    per_block = rows // NBLK
    lanes = QUERY_PER_KEY * per_block
    half, rank = place_ref[0], place_ref[1]
    ranks = gathered_ref.shape[1]
    scale = 1.0 / math.sqrt(HEAD_SIZE)
    factor = scale * math.log2(math.e)

    key_total[...] = jnp.zeros_like(key_total)
    value_total[...] = jnp.zeros_like(value_total)
    partial_ref[...] = jnp.zeros_like(partial_ref)
    doc_row[...] = jnp.full_like(doc_row, 1e4)

    for slot in range(window):
        source = rank - (window - 1) + slot
        valid = source >= 0
        index = jnp.maximum(source, 0)
        for stored in range(2):
            docs = gathered_ref[stored, index, pl.ds(2 * rows, META), :].astype(F32)
            docs = docs[DOC_ROW : DOC_ROW + 1, :rows]
            docs = jnp.where(valid, docs, -1.0)
            doc_row[stored, slot : slot + 1, :] = docs
            doc_column[stored, slot * rows : (slot + 1) * rows, :] = jnp.broadcast_to(
                docs, (rows, rows)
            ).T
        flags = gathered_ref[0, index, pl.ds(2 * rows, META), :].astype(F32)
        for block in range(NBLK):
            flag = flags[FLAG_ROW + block : FLAG_ROW + block + 1, :]
            mask = jnp.broadcast_to(flag, (per_block, flag.shape[1])) > 0.5
            at = slot * rows + block * per_block
            for which, log in ((0, key_log), (1, value_log)):
                part = pl.ds(which * rows + block * per_block, per_block)
                first = gathered_ref[0, index, part, :].astype(F32)
                second = gathered_ref[1, index, part, :].astype(F32)
                for own, other, logical in ((first, second, 0), (second, first, 1)):
                    merged = jnp.where(mask, other, own).astype(BF16)
                    for head in range(KEY_VALUE_HEADS):
                        log[logical, head, at : at + per_block, :] = merged[
                            :, head * HEAD_SIZE : (head + 1) * HEAD_SIZE
                        ]
    for logical in range(2):
        for head in range(KEY_VALUE_HEADS):
            key_turned[logical, head] = key_log[logical, head].T
            value_turned[logical, head] = value_log[logical, head].T

    def unit(block, logical, head, chunks, doc_lanes):
        first = (window - chunks) * rows
        span = pl.ds(first, chunks * rows)
        at = pl.ds(pl.multiple_of(block * per_block, per_block), per_block)
        columns = [
            slice((head * QUERY_PER_KEY + h) * HEAD_SIZE, (head * QUERY_PER_KEY + h + 1) * HEAD_SIZE)
            for h in range(QUERY_PER_KEY)
        ]
        query = jnp.concatenate([query_ref[at, column] for column in columns], axis=0)
        grad = jnp.concatenate([grad_ref[at, column] for column in columns], axis=0)
        keys = key_log[logical, head, span, :]
        values = value_log[logical, head, span, :]
        scores = lax.dot_general(keys, query, NT, preferred_element_type=F32)
        same = doc_column[logical, span, :] == doc_lanes
        key_place = lax.broadcasted_iota(jnp.int32, same.shape, 0) - (chunks - 1) * rows
        row_place = block * per_block + lax.rem(
            lax.broadcasted_iota(jnp.int32, same.shape, 1), per_block
        )
        allowed = same & (key_place <= row_place)
        width = same.shape[1]
        scores = jnp.concatenate(
            [
                jnp.where(allowed, scores[:, lane : lane + width], NEG)
                for lane in range(0, lanes, width)
            ],
            axis=1,
        )
        peak = jnp.max(scores, axis=0, keepdims=True)
        powers = jnp.exp2((scores - peak) * factor)
        inverse = 1.0 / jnp.sum(powers, axis=0, keepdims=True)
        probs = powers * inverse
        weights = probs.astype(BF16)
        out_turned = jnp.dot(
            value_turned[logical, head, :, span], weights, preferred_element_type=F32
        ).astype(BF16)
        delta = jnp.sum(
            grad.T.astype(F32) * out_turned.astype(F32), axis=0, keepdims=True
        )
        prob_grad = lax.dot_general(values, grad, NT, preferred_element_type=F32)
        score_grad = (probs * (prob_grad - delta)).astype(BF16)
        query_grad_turned = jnp.dot(
            key_turned[logical, head, :, span], score_grad, preferred_element_type=F32
        )
        key_total[logical, head, span, :] += jnp.dot(
            score_grad, query, preferred_element_type=F32
        )
        value_total[logical, head, span, :] += jnp.dot(
            weights, grad, preferred_element_type=F32
        )
        out = out_turned.T
        query_grad = (query_grad_turned * scale).astype(BF16).T
        for h, column in enumerate(columns):
            out_ref[at, column] = out[h * per_block : (h + 1) * per_block, :]
            query_grad_ref[at, column] = query_grad[h * per_block : (h + 1) * per_block, :]

    def row_block(block, carry):
        logical = half ^ swap_ref[block]
        meta = gathered_ref[logical, rank, pl.ds(2 * rows, META), :].astype(F32)
        pick = lax.broadcasted_iota(jnp.int32, meta.shape, 0) == TILED_ROW + block
        doc_lanes = jnp.max(jnp.where(pick, meta, -1.0), axis=0, keepdims=True)
        lowest = jnp.min(doc_lanes)
        skipped = jnp.sum((doc_row[logical] < lowest).astype(F32)).astype(jnp.int32)
        needed = window - skipped // rows
        doc_lanes = doc_lanes[:, :HEAD_SIZE]
        for chunks in range(1, window + 1):

            @pl.when(needed == chunks)
            def _():
                for head in range(KEY_VALUE_HEADS):
                    unit(block, logical, head, chunks, doc_lanes)

        return carry

    lax.fori_loop(0, NBLK, row_block, 0)

    for slot in range(window):
        source = rank - (window - 1) + slot

        @pl.when(source >= 0)
        def _(slot=slot, source=source):
            flags = gathered_ref[0, source, pl.ds(2 * rows, META), :].astype(F32)
            for block in range(NBLK):
                at = slot * rows + block * per_block
                for head in range(KEY_VALUE_HEADS):
                    side = slice(head * HEAD_SIZE, (head + 1) * HEAD_SIZE)
                    flag = flags[FLAG_ROW + block : FLAG_ROW + block + 1, side]
                    mask = jnp.broadcast_to(flag, (per_block, HEAD_SIZE)) > 0.5
                    for which, total, gain in ((0, key_total, scale), (1, value_total, 1.0)):
                        part = pl.ds(which * rows + block * per_block, per_block)
                        first = total[0, head, at : at + per_block, :] * gain
                        second = total[1, head, at : at + per_block, :] * gain
                        partial_ref[0, source, part, side] = jnp.where(
                            mask, second, first
                        ).astype(BF16)
                        partial_ref[1, source, part, side] = jnp.where(
                            mask, first, second
                        ).astype(BF16)


def local(queries, key_rows, value_rows, out_grad, documents, swapped):
    ranks = lax.axis_size("ctx")
    window = ranks // 2 + 1
    rows, width = key_rows.shape[1:]
    payload = payload_of(key_rows[0], value_rows[0], documents[0], swapped[0, 0])
    gathered = lax.all_gather(payload, ("half", "ctx"), axis=0, tiled=False)
    gathered = gathered.reshape(2, ranks, *payload.shape)
    place = jnp.stack([lax.axis_index("half"), lax.axis_index("ctx")]).astype(jnp.int32)
    vmem = pl.BlockSpec(memory_space=pltpu.VMEM)
    smem = pl.BlockSpec(memory_space=pltpu.SMEM)
    heads = KEY_VALUE_HEADS
    keys = window * rows
    out, query_grad, partial = pl.pallas_call(
        functools.partial(attention_kernel, window),
        out_shape=[
            jax.ShapeDtypeStruct(queries.shape[1:], BF16),
            jax.ShapeDtypeStruct(queries.shape[1:], BF16),
            jax.ShapeDtypeStruct((2, ranks, 2 * rows, width), BF16),
        ],
        in_specs=[smem, smem, vmem, vmem, vmem],
        out_specs=[vmem] * 3,
        scratch_shapes=[
            pltpu.VMEM((2, heads, keys, HEAD_SIZE), BF16),
            pltpu.VMEM((2, heads, keys, HEAD_SIZE), BF16),
            pltpu.VMEM((2, heads, HEAD_SIZE, keys), BF16),
            pltpu.VMEM((2, heads, HEAD_SIZE, keys), BF16),
            pltpu.VMEM((2, keys, rows), F32),
            pltpu.VMEM((2, 16, rows), F32),
            pltpu.VMEM((2, heads, keys, HEAD_SIZE), F32),
            pltpu.VMEM((2, heads, keys, HEAD_SIZE), F32),
        ],
        compiler_params=pltpu.CompilerParams(vmem_limit_bytes=48 * 1024 * 1024),
        cost_estimate=pl.CostEstimate(
            flops=12 * rows * keys * 2048, bytes_accessed=8 * 1024 * 1024, transcendentals=rows * keys * 16
        ),
    )(place, swapped[0, 0], queries[0], out_grad[0], gathered)
    summed = lax.psum_scatter(
        partial.reshape(2 * ranks, 2 * rows, width), ("half", "ctx"), scatter_dimension=0, tiled=False
    )
    return (out[None], query_grad[None], summed[None, :rows], summed[None, rows:])


def solution(mesh):
    groups, ranks = mesh.devices.shape
    wide = Mesh(mesh.devices.reshape(2, groups // 2, ranks), ("half", "pair", "ctx"))
    spec3 = P(("half", "pair"), "ctx", None)
    in_specs = (spec3, spec3, spec3, spec3, P(("half", "pair"), "ctx"), spec3)
    return jax.shard_map(
        local, mesh=wide, in_specs=in_specs, out_specs=(spec3,) * 4, check_vma=False
    )
```

time: 240 us -> 144 us (0.60)
  starting transfers between devices: 40.5 us -> 0.08 us
  matrix products: 24.9 us -> 0 us
  blocking collectives: 15.5 us -> 0 us
  other arithmetic: 16.7 us -> 2.07 us
  local copies, waits for them, and re-layouts: 23.8 us -> 10.3 us
  between operations: 0.95 us -> 14.1 us
  Pallas kernels: 0 us -> 8.68 us
  waiting for transfers between devices: 115 us -> 109 us
    all_to_all x8 -> x0, waiting for transfers between devices: 107 us -> none  [the longest x1 25.3 us: local(): lax.all_to_all(key_grad_seq, 'ctx', split_axis=0, concat_axis=1, tiled=True)]
    reduce_scatter x0 -> x1, waiting for transfers between devices: none -> 64.5 us  [local(): lax.psum_scatter(partial.reshape(2 * ranks, 2 * rows, width), ('half', 'c...]
    all_gather x0 -> x1, waiting for transfers between devices: none -> 44.6 us  [local(): gathered = lax.all_gather(payload, ('half', 'ctx'), axis=0, tiled=False)]
    all_to_all x8 -> x0, starting transfers between devices: 31 us -> none  [the longest x1 5.01 us: local(): lax.all_to_all(widen(key_home), 'ctx', split_axis=1, concat_axis=0, tiled...]
    dot_general x42 -> x0, matrix products: 24.9 us -> none  [the longest x12 10.5 us: scores(): jnp.einsum('qd,kd->qk', tile_of(query_head, row_tile), tile_of(key_head,...]
    all_gather x1 -> x0, blocking collectives: 15.5 us -> none  [local(): doc_ids = lax.all_gather(documents[0], 'ctx', axis=0, tiled=True)]
    ppermute x8 -> x0, starting transfers between devices: 9.51 us -> none  [shifted_2(): return lax.ppermute(block, axis, route)]
    pallas_call x0 -> x1, Pallas kernels: none -> 8.68 us  [local(): pl.pallas_call(functools.partial(attention_kernel, window), out_shape=[ja...]
  transfers between devices with their start and end apart: 16 -> 2, of which waited for: 10 -> 2; matrix products, arithmetic and copies ran while one was open for 9% -> 0% of each run, Pallas kernels for 0% -> 0%
where the time goes in v1:
time: 144 us
  waiting for transfers between devices  109 us (76%)
  between operations  14.1 us (10%)
  local copies, waits for them, and re-layouts  10.3 us (7%)
  Pallas kernels  8.68 us (6%)
  other arithmetic  2.07 us (1%)
    reduce_scatter x1, waiting for transfers between devices, local(): lax.psum_scatter(partial.reshape(2 * ranks, 2 * rows, width), ('half', 'c...  64.5 us
    all_gather x1, waiting for transfers between devices, local(): gathered = lax.all_gather(payload, ('half', 'ctx'), axis=0, tiled=False)  44.6 us
    pallas_call x1, Pallas kernels, local(): pl.pallas_call(functools.partial(attention_kernel, window), out_shape=[ja...  8.68 us
    unnamed x10, local copies, waits for them, and re-layouts  4.37 us
    concatenate x1, local copies, waits for them, and re-layouts, payload_of(): return jnp.concatenate([key_rows, value_rows, meta], axis=0)  4.17 us
  transfers between devices with their start and end apart: 2, of which 2 were waited for; matrix products, arithmetic and copies ran while one was open for 0% of the time, Pallas kernels for 0%

profile of v1, /device:TPU:0, one launch (start us, length us, event | category | flops | bytes accessed | tf_op | source)
XLA Modules:
  0.0 144.2 jit_solution(17977243527521192194)
XLA Ops:
  7.2 0.0 all-gather.3.cloned.1.call-start
  7.2 0.7 convert_bitcast_fusion
  7.9 0.7 convert_reduce_fusion
  8.6 0.1 convert_element_type.26
  8.6 0.7 bitcast_convert_fusion
  9.3 0.1 tile.17
  9.4 0.1 broadcast_in_dim.8
  9.5 4.2 %concatenate.3 = bf16[272,256]{1,0:T(8,128)(2,1)} concatenate(bf16[128,256]{1,0:T(8,128)(2,1)} %bitcast.24, bf16[128,256]{1,0:T(8,128)(2,1)} %bitcast.25, bf16[4,256]{1,0:T(4,128)(2,1)S(1)} %broadcast_in_dim.8, bf16[4,256]{1,0:T(4,128)(2,1)S(1)} %tile.17, bf16[1,256]{1,0:T(2,128)(2,1)S(1)} %bitcast.26, bf16[7,256]{1,0:T(8,128)(2,1)S(1)} %broadcast_in_dim.18), dimensions={0} | concatenate | bytes 278528 | tf_op jit(solution)/shard_map/concatenate | solution.py:33
  13.6 0.0 all-gather.3.cloned.1.call-update
  13.7 0.0 reduce-scatter.2.cloned.1.call-start
  13.7 0.1 pad_add_fusion.place_ref
  13.8 44.6 %all-gather.3.cloned.1.call-done = bf16[4352,256]{1,0:T(8,128)(2,1)} async-done(((bf16[272,256]{1,0:T(8,128)(2,1)}), bf16[4352,256]{1,0:T(8,128)(2,1)}) %all-gather.3.cloned.1.call-update) | async-done | bytes 2228240 | tf_op jit(solution)/shard_map/all_gather | solution.py:204
  58.4 0.0 copy-start
  58.4 1.6 %copy-done = bf16[4352,256]{1,0:T(8,128)(2,1)S(1)} copy-done((bf16[4352,256]{1,0:T(8,128)(2,1)S(1)}, bf16[4352,256]{1,0:T(8,128)(2,1)}, u32[]{:S(2)}) %copy-start) | copy-done | bytes 2228248
  60.0 0.0 copy-start.1
  60.0 1.0 copy-done.1
  61.0 0.0 copy-start.2
  61.0 1.0 copy-done.2
  62.1 0.0 copy-start.3
  62.1 0.7 copy-done.3
  62.7 8.7 %shard_map.93 = (bf16[128,2048]{1,0:T(8,128)(2,1)}, bf16[128,2048]{1,0:T(8,128)(2,1)}, bf16[2,8,256,256]{3,2,1,0:T(8,128)(2,1)}) custom-call(s32[2]{0:T(128)S(1)} %pad_add_fusion.place_ref, s32[4]{0:T(128)S(1)} %bitcast.23, bf16[128,2048]{1,0:T(8,128)(2,1)S(1)} %bitcast.21, bf16[128,2048]{1,0:T(8,128)(2,1)S(1)} %bitcast.22, bf16[2,8,272,256]{3,2,1,0:T(8,128)(2,1)S(1)} %bitcast.20), custom_call_target="tpu_custom_call" | custom-call | flops 2013265920 | bytes 8388608 | tf_op jit(solution)/shard_map/pallas_call | solution.py:211
  71.4 0.0 reduce-scatter.2.cloned.1.call-update
  71.4 64.5 %reduce-scatter.2.cloned.1.call-done = bf16[1,256,256]{2,1,0:T(8,128)(2,1)} async-done(((bf16[16,256,256]{2,1,0:T(8,128)(2,1)}), bf16[1,256,256]{2,1,0:T(8,128)(2,1)}) %reduce-scatter.2.cloned.1.call-update) | async-done | bytes 131088 | tf_op jit(solution)/shard_map/reduce_scatter | solution.py:235
  135.9 1.5 %fusion = (bf16[1,128,256]{2,1,0:T(8,128)(2,1)}, bf16[1,128,256]{2,1,0:T(8,128)(2,1)}) fusion(bf16[1,256,256]{2,1,0:T(8,128)(2,1)} %reduce-scatter.2.cloned.1.call-done), kind=kLoop, calls=%fused_computation.6 | loop fusion | bytes 262144 | tf_op jit(solution)/shard_map/slice | solution.py:238
  (4 shorter events, 0.0 us)
Async XLA Ops:
  7.2 51.2 %all-gather.3.cloned.1.call-start = ((), (), s32[]{:S(2)}) async-start(), calls=%async_computation.2 | async-start | bytes 2367488 | tf_op jit(solution)/shard_map/all_gather | solution.py:204
  13.7 122.2 %reduce-scatter.2.cloned.1.call-start = ((), (), s32[]{:S(2)}) async-start(), calls=%async_computation.1 | async-start | bytes 2228224 | tf_op jit(solution)/shard_map/reduce_scatter | solution.py:235
  58.4 1.6 %copy-start = (bf16[4352,256]{1,0:T(8,128)(2,1)S(1)}, bf16[4352,256]{1,0:T(8,128)(2,1)}, u32[]{:S(2)}) copy-start(bf16[4352,256]{1,0:T(8,128)(2,1)} %all-gather.3.cloned.1.call-done) | copy-start | bytes 6684676
  60.0 1.0 copy-start.1
  61.0 1.0 copy-start.2
  62.1 0.7 copy-start.3
Sparse Core Ops, SparseCore 0:
  13.8 44.5 all-gather.2
  71.5 64.2 reduce-scatter.1

commit v2 on v1

v2 whole, which is shorter than its diff:
```python
import functools
import math

import jax
import jax.numpy as jnp
from jax import lax
from jax.experimental import pallas as pl
from jax.experimental.pallas import tpu as pltpu
from jax.sharding import Mesh
from jax.sharding import PartitionSpec as P

HEAD_SIZE = 128
QUERY_PER_KEY = 8
KEY_VALUE_HEADS = 2
NBLK = 4
META = 16
DOC_ROW = NBLK
NEG = -1e30
F32, BF16 = jnp.float32, jnp.bfloat16
NT = (((1,), (1,)), ((), ()))


def payload_kernel(swap_ref, key_ref, value_ref, docs_ref, payload_ref):
    rows, width = key_ref.shape
    payload_ref[:rows, :] = key_ref[...]
    payload_ref[rows : 2 * rows, :] = value_ref[...]
    docs = jnp.broadcast_to(docs_ref[...].astype(F32), (META, rows))
    docs = jnp.concatenate([docs] * (width // rows), axis=1)
    place = lax.broadcasted_iota(jnp.int32, docs.shape, 0)
    meta = jnp.where(place == DOC_ROW, docs, 0.0)
    for block in range(NBLK):
        meta = jnp.where(place == block, swap_ref[block].astype(F32), meta)
    payload_ref[2 * rows :, :] = meta.astype(BF16)


def attention_kernel(
    hops,
    place_ref,
    swap_ref,
    query_ref,
    grad_ref,
    *refs,
):
    window = 2 * hops + 1
    count = hops + 1
    blocks = refs[: 4 * count]
    out_ref, query_grad_ref, home_ref, home_side_ref, away_ref, away_side_ref = refs[
        4 * count : 4 * count + 6
    ]
    (
        key_log,
        value_log,
        key_turned,
        value_turned,
        doc_column,
        doc_row,
        doc_tiled,
        key_total,
        value_total,
    ) = refs[4 * count + 6 :]
    rows = query_ref.shape[0]
    per_block = rows // NBLK
    lanes = QUERY_PER_KEY * per_block
    core, chip = place_ref[0], place_ref[1]
    scale = 1.0 / math.sqrt(HEAD_SIZE)
    factor = scale * math.log2(math.e)

    key_total[...] = jnp.zeros_like(key_total)
    value_total[...] = jnp.zeros_like(value_total)
    doc_row[...] = jnp.full_like(doc_row, 1e4)

    def place_slot(home, away, valid, slot):
        base = pl.multiple_of(slot * rows, rows)
        for logical, ref in ((0, home), (1, away)):
            meta = ref[2 * rows :, :rows].astype(F32)
            docs = jnp.where(valid, meta[DOC_ROW : DOC_ROW + 1, :], -1.0)
            doc_row[logical, pl.ds(slot, 1), :] = docs
            doc_column[logical, pl.ds(base, rows), :] = jnp.broadcast_to(
                docs, (rows, rows)
            ).T
        flags = home[2 * rows :, :].astype(F32)
        for block in range(NBLK):
            mask = jnp.broadcast_to(flags[block : block + 1, :], (per_block, flags.shape[1])) > 0.5
            at = pl.ds(base + block * per_block, per_block)
            for which, log in ((0, key_log), (1, value_log)):
                part = slice(which * rows + block * per_block, which * rows + (block + 1) * per_block)
                first = home[part, :].astype(F32)
                second = away[part, :].astype(F32)
                for own, other, logical in ((first, second, 0), (second, first, 1)):
                    merged = jnp.where(mask, other, own).astype(BF16)
                    for head in range(KEY_VALUE_HEADS):
                        log[logical, head, at, :] = merged[
                            :, head * HEAD_SIZE : (head + 1) * HEAD_SIZE
                        ]

    for k in range(count):
        home, away, home_side, away_side = (blocks[kind * count + k] for kind in range(4))
        slot = window - 1 - 2 * k
        side_slot = slot + 1 - 2 * core
        place_slot(home, away, chip >= k, slot)

        @pl.when((side_slot >= 0) & (side_slot < window))
        def _(home_side=home_side, away_side=away_side, k=k, side_slot=side_slot):
            place_slot(home_side, away_side, chip >= k, side_slot)

    for logical in range(2):
        for head in range(KEY_VALUE_HEADS):
            key_turned[logical, head] = key_log[logical, head].T
            value_turned[logical, head] = value_log[logical, head].T
        docs = jnp.broadcast_to(doc_row[logical, window - 1 : window, :], (8, rows))
        turns = [docs] + [
            pltpu.roll(docs, t * per_block, 1) for t in range(1, NBLK)
        ]
        group = lax.broadcasted_iota(jnp.int32, docs.shape, 1) // per_block
        for block in range(NBLK):
            tiled = turns[0]
            for t in range(1, NBLK):
                tiled = jnp.where(group == (block + t) % NBLK, turns[t], tiled)
            doc_tiled[logical, block : block + 1, :] = tiled[:1]

    def unit(block, logical, head, chunks, doc_lanes):
        first = (window - chunks) * rows
        span = pl.ds(first, chunks * rows)
        at = pl.ds(pl.multiple_of(block * per_block, per_block), per_block)
        columns = [
            slice((head * QUERY_PER_KEY + h) * HEAD_SIZE, (head * QUERY_PER_KEY + h + 1) * HEAD_SIZE)
            for h in range(QUERY_PER_KEY)
        ]
        query = jnp.concatenate([query_ref[at, column] for column in columns], axis=0)
        grad = jnp.concatenate([grad_ref[at, column] for column in columns], axis=0)
        keys = key_log[logical, head, span, :]
        values = value_log[logical, head, span, :]
        scores = lax.dot_general(keys, query, NT, preferred_element_type=F32)
        same = doc_column[logical, span, :] == doc_lanes
        key_place = lax.broadcasted_iota(jnp.int32, same.shape, 0) - (chunks - 1) * rows
        row_place = block * per_block + lax.rem(
            lax.broadcasted_iota(jnp.int32, same.shape, 1), per_block
        )
        allowed = same & (key_place <= row_place)
        width = same.shape[1]
        scores = jnp.concatenate(
            [
                jnp.where(allowed, scores[:, lane : lane + width], NEG)
                for lane in range(0, lanes, width)
            ],
            axis=1,
        )
        peak = jnp.max(scores, axis=0, keepdims=True)
        powers = jnp.exp2((scores - peak) * factor)
        inverse = 1.0 / jnp.sum(powers, axis=0, keepdims=True)
        probs = powers * inverse
        weights = probs.astype(BF16)
        out_turned = jnp.dot(
            value_turned[logical, head, :, span], weights, preferred_element_type=F32
        ).astype(BF16)
        delta = jnp.sum(
            grad.T.astype(F32) * out_turned.astype(F32), axis=0, keepdims=True
        )
        prob_grad = lax.dot_general(values, grad, NT, preferred_element_type=F32)
        score_grad = (probs * (prob_grad - delta)).astype(BF16)
        query_grad_turned = jnp.dot(
            key_turned[logical, head, :, span], score_grad, preferred_element_type=F32
        )
        key_total[logical, head, span, :] += jnp.dot(
            score_grad, query, preferred_element_type=F32
        )
        value_total[logical, head, span, :] += jnp.dot(
            weights, grad, preferred_element_type=F32
        )
        out = out_turned.T
        query_grad = (query_grad_turned * scale).astype(BF16).T
        for h, column in enumerate(columns):
            out_ref[at, column] = out[h * per_block : (h + 1) * per_block, :]
            query_grad_ref[at, column] = query_grad[h * per_block : (h + 1) * per_block, :]

    def row_block(block, carry):
        logical = swap_ref[block]
        doc_lanes = doc_tiled[logical, pl.ds(block, 1), :]
        lowest = jnp.min(doc_lanes)
        skipped = jnp.sum((doc_row[logical] < lowest).astype(F32)).astype(jnp.int32)
        needed = window - skipped // rows
        for chunks in range(1, window + 1):

            @pl.when(needed == chunks)
            def _():
                for head in range(KEY_VALUE_HEADS):
                    unit(block, logical, head, chunks, doc_lanes)

        return carry

    lax.fori_loop(0, NBLK, row_block, 0)

    def give(slot, k, meta_ref, home_out, away_out):
        base = pl.multiple_of(slot * rows, rows)
        flags = meta_ref[2 * rows :, :].astype(F32)
        for block in range(NBLK):
            at = pl.ds(base + block * per_block, per_block)
            for head in range(KEY_VALUE_HEADS):
                side = slice(head * HEAD_SIZE, (head + 1) * HEAD_SIZE)
                mask = jnp.broadcast_to(flags[block : block + 1, side], (per_block, HEAD_SIZE)) > 0.5
                for which, total, gain in ((0, key_total, scale), (1, value_total, 1.0)):
                    part = slice(
                        which * rows + block * per_block, which * rows + (block + 1) * per_block
                    )
                    first = total[0, head, at, :] * gain
                    second = total[1, head, at, :] * gain
                    home_out[k, part, side] = jnp.where(mask, second, first).astype(BF16)
                    away_out[k, part, side] = jnp.where(mask, first, second).astype(BF16)

    for k in range(count):
        slot = window - 1 - 2 * k
        side_slot = slot + 1 - 2 * core
        give(slot, k, blocks[k], home_ref, away_ref)
        inside = (side_slot >= 0) & (side_slot < window)

        @pl.when(inside)
        def _(k=k, side_slot=side_slot):
            give(side_slot, k, blocks[2 * count + k], home_side_ref, away_side_ref)

        @pl.when(jnp.logical_not(inside))
        def _(k=k):
            home_side_ref[k] = jnp.zeros_like(home_side_ref[k])
            away_side_ref[k] = jnp.zeros_like(away_side_ref[k])


def local(queries, key_rows, value_rows, out_grad, documents, swapped):
    ranks = lax.axis_size("ctx")
    hops = ranks // 4
    count = hops + 1
    window = 2 * hops + 1
    rows, width = key_rows.shape[1:]
    vmem = pl.BlockSpec(memory_space=pltpu.VMEM)
    smem = pl.BlockSpec(memory_space=pltpu.SMEM)
    heads = KEY_VALUE_HEADS
    keys = window * rows
    swap_flags = swapped[0, 0]

    up = [(i, i + 2) for i in range(ranks - 2)]
    down = [(i + 2, i) for i in range(ranks - 2)]
    side = [(i, i ^ 1) for i in range(ranks)]

    def to_partner(block):
        return lax.ppermute(block, "half", [(0, 1), (1, 0)])

    def to_side(block):
        return lax.ppermute(block, "ctx", side)

    payload = pl.pallas_call(
        payload_kernel,
        out_shape=jax.ShapeDtypeStruct((2 * rows + META, width), BF16),
        in_specs=[smem, vmem, vmem, vmem],
        out_specs=vmem,
    )(swap_flags, key_rows[0], value_rows[0], documents)
    home = [payload]
    for _ in range(hops):
        home.append(lax.ppermute(home[-1], "ctx", up))
    away = [to_partner(block) for block in home]
    home_side = [to_side(block) for block in home]
    away_side = [to_side(block) for block in away]
    chunk = jax.ShapeDtypeStruct((count, 2 * rows, width), BF16)
    index = lax.axis_index("ctx")
    place = jnp.stack([lax.rem(index, 2), index // 2]).astype(jnp.int32)
    out, query_grad, home_sum, home_sum_side, away_sum, away_sum_side = pl.pallas_call(
        functools.partial(attention_kernel, hops),
        out_shape=[
            jax.ShapeDtypeStruct(queries.shape[1:], BF16),
            jax.ShapeDtypeStruct(queries.shape[1:], BF16),
            chunk,
            chunk,
            chunk,
            chunk,
        ],
        in_specs=[smem, smem] + [vmem] * (2 + 4 * count),
        out_specs=[vmem] * 6,
        scratch_shapes=[
            pltpu.VMEM((2, heads, keys, HEAD_SIZE), BF16),
            pltpu.VMEM((2, heads, keys, HEAD_SIZE), BF16),
            pltpu.VMEM((2, heads, HEAD_SIZE, keys), BF16),
            pltpu.VMEM((2, heads, HEAD_SIZE, keys), BF16),
            pltpu.VMEM((2, keys, rows), F32),
            pltpu.VMEM((2, 16, rows), F32),
            pltpu.VMEM((2, 8, rows), F32),
            pltpu.VMEM((2, heads, keys, HEAD_SIZE), F32),
            pltpu.VMEM((2, heads, keys, HEAD_SIZE), F32),
        ],
        compiler_params=pltpu.CompilerParams(vmem_limit_bytes=40 * 1024 * 1024),
        cost_estimate=pl.CostEstimate(
            flops=12 * rows * keys * 2048,
            bytes_accessed=8 * 1024 * 1024,
            transcendentals=rows * keys * 16,
        ),
    )(place, swap_flags, queries[0], out_grad[0], *home, *away, *home_side, *away_side)

    away_got = to_side(away_sum_side)
    home_got = to_side(home_sum_side)
    added = [
        (away_sum[k].astype(F32) + away_got[k].astype(F32)).astype(BF16) for k in range(count)
    ]
    crossed = [None] * count
    for k in reversed(range(count)):
        crossed[k] = to_partner(added[k])
    moving = None
    for k in reversed(range(count)):
        total = home_sum[k].astype(F32) + home_got[k].astype(F32) + crossed[k].astype(F32)
        if moving is not None:
            total = total + moving.astype(F32)
        moving = total.astype(BF16)
        if k:
            moving = lax.ppermute(moving, "ctx", down)
    return (out[None], query_grad[None], moving[None, :rows], moving[None, rows:])


def solution(mesh):
    groups, ranks = mesh.devices.shape
    wide = Mesh(mesh.devices.reshape(2, groups // 2, ranks), ("half", "pair", "ctx"))
    spec3 = P(("half", "pair"), "ctx", None)
    in_specs = (spec3, spec3, spec3, spec3, P(("half", "pair"), "ctx"), spec3)
    return jax.shard_map(
        local, mesh=wide, in_specs=in_specs, out_specs=(spec3,) * 4, check_vma=False
    )
```

time: 144 us -> 64.3 us (0.45)
  waiting for transfers between devices: 109 us -> 27.5 us
  starting transfers between devices: 0.08 us -> 20.7 us
  between operations: 14.1 us -> 0.72 us
  local copies, waits for them, and re-layouts: 10.3 us -> 4.3 us
  other arithmetic: 2.07 us -> 0.35 us
    reduce_scatter x1 -> x0, waiting for transfers between devices: 64.5 us -> none  [local(): lax.psum_scatter(partial.reshape(2 * ranks, 2 * rows, width), ('half', 'c...]
    all_gather x1 -> x0, waiting for transfers between devices: 44.6 us -> none  [local(): gathered = lax.all_gather(payload, ('half', 'ctx'), axis=0, tiled=False)]
    ppermute x0 -> x18, waiting for transfers between devices: none -> 27.5 us  [the longest x6 10.9 us: to_partner(): return lax.ppermute(block, 'half', [(0, 1), (1, 0)])]
    ppermute x0 -> x18, starting transfers between devices: none -> 20.7 us  [the longest x2 9.2 us: local(): home.append(lax.ppermute(home[-1], 'ctx', up))]
    concatenate x1 -> x0, local copies, waits for them, and re-layouts: 4.17 us -> none  [payload_of(): return jnp.concatenate([key_rows, value_rows, meta], axis=0)]
    convert_element_type x3 -> x4, other arithmetic: 1.99 us -> 0.28 us  [the longest x3 0.19 us: local(): moving = total.astype(BF16)]
    slice x1 -> x0, local copies, waits for them, and re-layouts: 1.53 us -> none  [local(): summed[None, rows:]]
    pallas_call x1 -> x2, Pallas kernels: 8.68 us -> 9.77 us  [the longest x1 8.21 us: local(): pl.pallas_call(functools.partial(attention_kernel, hops), out_shape=[jax....]
  transfers between devices with their start and end apart: 2 -> 18, of which waited for: 2 -> 10; matrix products, arithmetic and copies ran while one was open for 0% -> 0% of each run, Pallas kernels for 0% -> 0%
where the time goes in v2:
time: 64.3 us; the launch traced here: 63.3 us
  waiting for transfers between devices  27.5 us (43%)
  starting transfers between devices  20.7 us (32%)
  Pallas kernels  9.77 us (15%)
  local copies, waits for them, and re-layouts  4.3 us (7%)
  between operations  0.72 us (1%)
    ppermute x6, waiting for transfers between devices, to_partner(): return lax.ppermute(block, 'half', [(0, 1), (1, 0)])  10.9 us
    ppermute x2, waiting for transfers between devices, local(): moving = lax.ppermute(moving, 'ctx', down)  10.4 us
    ppermute x2, starting transfers between devices, local(): home.append(lax.ppermute(home[-1], 'ctx', up))  9.2 us
    pallas_call x1, Pallas kernels, local(): pl.pallas_call(functools.partial(attention_kernel, hops), out_shape=[jax....  8.21 us
    ppermute x6, starting transfers between devices, to_partner(): return lax.ppermute(block, 'half', [(0, 1), (1, 0)])  7.84 us
    ppermute x2, waiting for transfers between devices, local(): home.append(lax.ppermute(home[-1], 'ctx', up))  3.7 us
    unnamed x8, local copies, waits for them, and re-layouts  3.64 us
    ppermute x2, starting transfers between devices, local(): moving = lax.ppermute(moving, 'ctx', down)  2.58 us
  transfers between devices with their start and end apart: 18, of which 10 were waited for; matrix products, arithmetic and copies ran while one was open for 0% of the time, Pallas kernels for 0%

profile of v2, /device:TPU:0, one launch (start us, length us, event | category | flops | bytes accessed | tf_op | source)
XLA Modules:
  0.0 63.3 jit_solution(1985936560869832852)
XLA Ops:
  0.6 1.6 %shard_map.93.refs_0_ = bf16[272,256]{1,0:T(8,128)(2,1)} custom-call(s32[4]{0:T(128)} %bitcast.35, bf16[128,256]{1,0:T(8,128)(2,1)} %bitcast.39, bf16[128,256]{1,0:T(8,128)(2,1)} %bitcast.40, s32[1,128]{1,0:T(1,128)} %docs_ref.1), custom_call_target="tpu_custom_call" | custom-call | tf_op jit(solution)/shard_map/pallas_call | solution.py:248
  2.2 4.9 %collective-permute-start = (bf16[272,256]{1,0:T(8,128)(2,1)}, bf16[272,256]{1,0:T(8,128)(2,1)S(1)}, u32[]{:S(2)}, u32[]{:S(2)}) collective-permute-start(bf16[272,256]{1,0:T(8,128)(2,1)} %shard_map.93.refs_0_), channel_id=1, source_target_pairs={{0,2},{1,3},{2,4},{3,5},{4,6},{5,7},{8,10},{9,11},{10,12},{11,13},... | collective-permute-start | bytes 417800 | tf_op jit(solution)/shard_map/ppermute | solution.py:256
  7.1 3.2 %collective-permute-done.refs_1_ = bf16[272,256]{1,0:T(8,128)(2,1)S(1)} collective-permute-done((bf16[272,256]{1,0:T(8,128)(2,1)}, bf16[272,256]{1,0:T(8,128)(2,1)S(1)}, u32[]{:S(2)}, u32[]{:S(2)}) %collective-permute-start) | collective-permute-done | bytes 139296 | tf_op jit(solution)/shard_map/ppermute | solution.py:256
  10.3 4.3 %collective-permute-start.1 = (bf16[272,256]{1,0:T(8,128)(2,1)S(1)}, bf16[272,256]{1,0:T(8,128)(2,1)S(1)}, u32[]{:S(2)}, u32[]{:S(2)}) collective-permute-start(bf16[272,256]{1,0:T(8,128)(2,1)S(1)} %collective-permute-done.refs_1_), channel_id=1, source_target_pairs={{0,2},{1,3},{2,4},{3,5},{4,6},{5,7},{8,10},{9,11},{10,12},{11,13},... | collective-permute-start | bytes 417800 | tf_op jit(solution)/shard_map/ppermute | solution.py:256
  14.6 1.6 %collective-permute-start.2 = (bf16[272,256]{1,0:T(8,128)(2,1)}, bf16[272,256]{1,0:T(8,128)(2,1)S(1)}, u32[]{:S(2)}, u32[]{:S(2)}) collective-permute-start(bf16[272,256]{1,0:T(8,128)(2,1)} %shard_map.93.refs_0_), channel_id=1, source_target_pairs={{0,16},{16,0},{1,17},{17,1},{2,18},{18,2},{3,19},{19,3},{4,20},{20... | collective-permute-start | bytes 417800 | tf_op jit(solution)/shard_map/ppermute | solution.py:243
  16.2 0.0 collective-permute-start.5
  16.2 0.5 collective-permute-start.3
  16.7 0.5 collective-permute-done.1.refs_2_
  17.2 1.5 %collective-permute-start.4 = (bf16[272,256]{1,0:T(8,128)(2,1)S(1)}, bf16[272,256]{1,0:T(8,128)(2,1)S(1)}, u32[]{:S(2)}, u32[]{:S(2)}) collective-permute-start(bf16[272,256]{1,0:T(8,128)(2,1)S(1)} %collective-permute-done.1.refs_2_), channel_id=1, source_target_pairs={{0,16},{16,0},{1,17},{17,1},{2,18},{18,2},{3,19},{19,3},{4,20},{20... | collective-permute-start | bytes 417800 | tf_op jit(solution)/shard_map/ppermute | solution.py:243
  18.7 0.0 collective-permute-start.6
  18.7 1.9 %collective-permute-done.2.refs_3_ = bf16[272,256]{1,0:T(8,128)(2,1)S(1)} collective-permute-done((bf16[272,256]{1,0:T(8,128)(2,1)}, bf16[272,256]{1,0:T(8,128)(2,1)S(1)}, u32[]{:S(2)}, u32[]{:S(2)}) %collective-permute-start.2) | collective-permute-done | bytes 139296 | tf_op jit(solution)/shard_map/ppermute | solution.py:243
  20.6 0.0 collective-permute-start.8
  20.6 0.0 collective-permute-done.5.refs_6_
  20.6 0.5 collective-permute-start.7
  21.1 2.5 %collective-permute-done.3.refs_4_ = bf16[272,256]{1,0:T(8,128)(2,1)S(1)} collective-permute-done((bf16[272,256]{1,0:T(8,128)(2,1)S(1)}, bf16[272,256]{1,0:T(8,128)(2,1)S(1)}, u32[]{:S(2)}, u32[]{:S(2)}) %collective-permute-start.3) | collective-permute-done | bytes 139296 | tf_op jit(solution)/shard_map/ppermute | solution.py:243
  23.6 0.0 collective-permute-start.9
  23.6 2.3 %collective-permute-done.4.refs_5_ = bf16[272,256]{1,0:T(8,128)(2,1)S(1)} collective-permute-done((bf16[272,256]{1,0:T(8,128)(2,1)S(1)}, bf16[272,256]{1,0:T(8,128)(2,1)S(1)}, u32[]{:S(2)}, u32[]{:S(2)}) %collective-permute-start.4) | collective-permute-done | bytes 139296 | tf_op jit(solution)/shard_map/ppermute | solution.py:243
  25.9 0.0 collective-permute-start.10
  25.9 0.1 pad_add_fusion.place_ref
  26.0 0.0 collective-permute-done.8.refs_9_
  26.0 0.0 collective-permute-done.6.refs_7_
  26.0 0.0 collective-permute-done.9.refs_10_
  26.0 0.0 collective-permute-done.7.refs_8_
  26.0 1.3 %collective-permute-done.10.refs_11_ = bf16[272,256]{1,0:T(8,128)(2,1)S(1)} collective-permute-done((bf16[272,256]{1,0:T(8,128)(2,1)S(1)}, bf16[272,256]{1,0:T(8,128)(2,1)S(1)}, u32[]{:S(2)}, u32[]{:S(2)}) %collective-permute-start.10) | collective-permute-done | bytes 139296 | tf_op jit(solution)/shard_map/ppermute | solution.py:246
  27.3 0.0 copy-start.1
  27.3 0.7 %copy-done.1 = s32[1,1,4]{2,1,0:T(1,128)S(1)} copy-done((s32[1,1,4]{2,1,0:T(1,128)S(1)}, s32[1,1,4]{2,1,0:T(1,128)}, u32[]{:S(2)}) %copy-start.1) | copy-done | bytes 40
  27.9 0.0 copy-start
  27.9 0.9 %copy-done = bf16[272,256]{1,0:T(8,128)(2,1)S(1)} copy-done((bf16[272,256]{1,0:T(8,128)(2,1)S(1)}, bf16[272,256]{1,0:T(8,128)(2,1)}, u32[]{:S(2)}) %copy-start) | copy-done | bytes 139288
  28.8 0.0 copy-start.2
  28.9 1.0 %copy-done.2 = bf16[1,128,2048]{2,1,0:T(8,128)(2,1)S(1)} copy-done((bf16[1,128,2048]{2,1,0:T(8,128)(2,1)S(1)}, bf16[1,128,2048]{2,1,0:T(8,128)(2,1)}, u32[]{:S(2)}) %copy-start.2) | copy-done | bytes 524312
  29.9 0.0 copy-start.3
  29.9 1.0 %copy-done.3 = bf16[1,128,2048]{2,1,0:T(8,128)(2,1)S(1)} copy-done((bf16[1,128,2048]{2,1,0:T(8,128)(2,1)S(1)}, bf16[1,128,2048]{2,1,0:T(8,128)(2,1)}, u32[]{:S(2)}) %copy-start.3) | copy-done | bytes 524312
  30.9 8.2 %shard_map.94 = (bf16[128,2048]{1,0:T(8,128)(2,1)}, bf16[128,2048]{1,0:T(8,128)(2,1)}, bf16[3,256,256]{2,1,0:T(8,128)(2,1)S(1)}, bf16[3,256,256]{2,1,0:T(8,128)(...) custom-call(s32[2]{0:T(128)S(1)} %pad_add_fusion.place_ref, s32[4]{0:T(128)S(1)} %bitcast.36, ...), custom_call_target="tpu_custom_call" | custom-call | flops 2013265920 | bytes 8388608 | tf_op jit(solution)/shard_map/pallas_call | solution.py:263
  39.1 0.5 collective-permute-start.12
  39.6 0.0 collective-permute-start.11
  39.7 1.3 %collective-permute-done.12 = bf16[3,256,256]{2,1,0:T(8,128)(2,1)S(1)} collective-permute-done((bf16[3,256,256]{2,1,0:T(8,128)(2,1)S(1)}, bf16[3,256,256]{2,1,0:T(8,128)(2,1)S(1)}, u32[]{:S(2)}, u32[]{:S(2)}) %collective-permute-start.12) | collective-permute-done | bytes 393248 | tf_op jit(solution)/shard_map/ppermute | solution.py:246
  41.0 0.1 fusion.5
  41.1 2.1 %collective-permute-start.15 = (bf16[256,256]{1,0:T(8,128)(2,1)S(1)}, bf16[256,256]{1,0:T(8,128)(2,1)S(1)}, u32[]{:S(2)}, u32[]{:S(2)}) collective-permute-start(bf16[256,256]{1,0:T(8,128)(2,1)S(1)} %get-tuple-element.17), channel_id=1, source_target_pairs={{0,16},{16,0},{1,17},{17,1},{2,18},{18,2},{3,19},{19,3},{4,20},{20... | collective-permute-start | bytes 393224 | tf_op jit(solution)/shard_map/ppermute | solution.py:243
  43.1 0.1 collective-permute-start.14
  43.2 0.0 collective-permute-done.11
  43.2 4.2 %collective-permute-done.15 = bf16[256,256]{1,0:T(8,128)(2,1)S(1)} collective-permute-done((bf16[256,256]{1,0:T(8,128)(2,1)S(1)}, bf16[256,256]{1,0:T(8,128)(2,1)S(1)}, u32[]{:S(2)}, u32[]{:S(2)}) %collective-permute-start.15) | collective-permute-done | bytes 131104 | tf_op jit(solution)/shard_map/ppermute | solution.py:243
  47.4 0.1 fusion
  47.5 1.3 %collective-permute-start.16 = (bf16[256,256]{1,0:T(8,128)(2,1)S(1)}, bf16[256,256]{1,0:T(8,128)(2,1)S(1)}, u32[]{:S(2)}, u32[]{:S(2)}) collective-permute-start(bf16[256,256]{1,0:T(8,128)(2,1)S(1)} %fusion), channel_id=1, source_target_pairs={{2,0},{3,1},{4,2},{5,3},{6,4},{7,5},{10,8},{11,9},{12,10},{13,11},... | collective-permute-start | bytes 393224 | tf_op jit(solution)/shard_map/ppermute | solution.py:309
  48.8 2.1 %collective-permute-start.13 = (bf16[256,256]{1,0:T(8,128)(2,1)S(1)}, bf16[256,256]{1,0:T(8,128)(2,1)S(1)}, u32[]{:S(2)}, u32[]{:S(2)}) collective-permute-start(bf16[256,256]{1,0:T(8,128)(2,1)S(1)} %get-tuple-element.16), channel_id=1, source_target_pairs={{0,16},{16,0},{1,17},{17,1},{2,18},{18,2},{3,19},{19,3},{4,20},{20... | collective-permute-start | bytes 393224 | tf_op jit(solution)/shard_map/ppermute | solution.py:243
  50.9 0.0 collective-permute-done.14
  50.9 3.5 %collective-permute-done.16 = bf16[256,256]{1,0:T(8,128)(2,1)S(1)} collective-permute-done((bf16[256,256]{1,0:T(8,128)(2,1)S(1)}, bf16[256,256]{1,0:T(8,128)(2,1)S(1)}, u32[]{:S(2)}, u32[]{:S(2)}) %collective-permute-start.16) | collective-permute-done | bytes 131104 | tf_op jit(solution)/shard_map/ppermute | solution.py:309
  54.3 0.1 fusion.2
  54.4 1.3 %collective-permute-start.17 = (bf16[256,256]{1,0:T(8,128)(2,1)S(1)}, bf16[256,256]{1,0:T(8,128)(2,1)S(1)}, u32[]{:S(2)}, u32[]{:S(2)}) collective-permute-start(bf16[256,256]{1,0:T(8,128)(2,1)S(1)} %fusion.2), channel_id=1, source_target_pairs={{2,0},{3,1},{4,2},{5,3},{6,4},{7,5},{10,8},{11,9},{12,10},{13,11},... | collective-permute-start | bytes 393224 | tf_op jit(solution)/shard_map/ppermute | solution.py:309
  55.7 0.0 collective-permute-done.13
  55.7 6.9 %collective-permute-done.17 = bf16[256,256]{1,0:T(8,128)(2,1)S(1)} collective-permute-done((bf16[256,256]{1,0:T(8,128)(2,1)S(1)}, bf16[256,256]{1,0:T(8,128)(2,1)S(1)}, u32[]{:S(2)}, u32[]{:S(2)}) %collective-permute-start.17) | collective-permute-done | bytes 131104 | tf_op jit(solution)/shard_map/ppermute | solution.py:309
  62.6 0.1 fusion.4
  62.7 0.7 %slice_bitcast_fusion = (bf16[1,128,256]{2,1,0:T(8,128)(2,1)}, bf16[1,128,256]{2,1,0:T(8,128)(2,1)}) fusion(bf16[256,256]{1,0:T(8,128)(2,1)S(1)} %fusion.4), kind=kLoop, calls=%fused_computation.14 | loop fusion | bytes 262144 | tf_op jit(solution)/shard_map/broadcast_in_dim | solution.py:310
Async XLA Ops:
  2.2 8.2 %collective-permute-start = (bf16[272,256]{1,0:T(8,128)(2,1)}, bf16[272,256]{1,0:T(8,128)(2,1)S(1)}, u32[]{:S(2)}, u32[]{:S(2)}) collective-permute-start(bf16[272,256]{1,0:T(8,128)(2,1)} %shard_map.93.refs_0_), channel_id=1, source_target_pairs={{0,2},{1,3},{2,4},{3,5},{4,6},{5,7},{8,10},{9,11},{10,12},{11,13},... | collective-permute-start | bytes 417800 | tf_op jit(solution)/shard_map/ppermute | solution.py:256
  10.3 6.9 %collective-permute-start.1 = (bf16[272,256]{1,0:T(8,128)(2,1)S(1)}, bf16[272,256]{1,0:T(8,128)(2,1)S(1)}, u32[]{:S(2)}, u32[]{:S(2)}) collective-permute-start(bf16[272,256]{1,0:T(8,128)(2,1)S(1)} %collective-permute-done.refs_1_), channel_id=1, source_target_pairs={{0,2},{1,3},{2,4},{3,5},{4,6},{5,7},{8,10},{9,11},{10,12},{11,13},... | collective-permute-start | bytes 417800 | tf_op jit(solution)/shard_map/ppermute | solution.py:256
  14.6 6.0 %collective-permute-start.2 = (bf16[272,256]{1,0:T(8,128)(2,1)}, bf16[272,256]{1,0:T(8,128)(2,1)S(1)}, u32[]{:S(2)}, u32[]{:S(2)}) collective-permute-start(bf16[272,256]{1,0:T(8,128)(2,1)} %shard_map.93.refs_0_), channel_id=1, source_target_pairs={{0,16},{16,0},{1,17},{17,1},{2,18},{18,2},{3,19},{19,3},{4,20},{20... | collective-permute-start | bytes 417800 | tf_op jit(solution)/shard_map/ppermute | solution.py:243
  16.2 4.4 %collective-permute-start.5 = (bf16[272,256]{1,0:T(8,128)(2,1)}, bf16[272,256]{1,0:T(8,128)(2,1)S(1)}, u32[]{:S(2)}, u32[]{:S(2)}) collective-permute-start(bf16[272,256]{1,0:T(8,128)(2,1)} %shard_map.93.refs_0_), channel_id=1, source_target_pairs={{0,1},{1,0},{2,3},{3,2},{4,5},{5,4},{6,7},{7,6},{8,9},{9,8},{10,11... | collective-permute-start | bytes 417800 | tf_op jit(solution)/shard_map/ppermute | solution.py:246
  16.2 7.4 %collective-permute-start.3 = (bf16[272,256]{1,0:T(8,128)(2,1)S(1)}, bf16[272,256]{1,0:T(8,128)(2,1)S(1)}, u32[]{:S(2)}, u32[]{:S(2)}) collective-permute-start(bf16[272,256]{1,0:T(8,128)(2,1)S(1)} %collective-permute-done.refs_1_), channel_id=1, source_target_pairs={{0,16},{16,0},{1,17},{17,1},{2,18},{18,2},{3,19},{19,3},{4,20},{20... | collective-permute-start | bytes 417800 | tf_op jit(solution)/shard_map/ppermute | solution.py:243
  17.2 8.7 %collective-permute-start.4 = (bf16[272,256]{1,0:T(8,128)(2,1)S(1)}, bf16[272,256]{1,0:T(8,128)(2,1)S(1)}, u32[]{:S(2)}, u32[]{:S(2)}) collective-permute-start(bf16[272,256]{1,0:T(8,128)(2,1)S(1)} %collective-permute-done.1.refs_2_), channel_id=1, source_target_pairs={{0,16},{16,0},{1,17},{17,1},{2,18},{18,2},{3,19},{19,3},{4,20},{20... | collective-permute-start | bytes 417800 | tf_op jit(solution)/shard_map/ppermute | solution.py:243
  18.7 7.3 %collective-permute-start.6 = (bf16[272,256]{1,0:T(8,128)(2,1)S(1)}, bf16[272,256]{1,0:T(8,128)(2,1)S(1)}, u32[]{:S(2)}, u32[]{:S(2)}) collective-permute-start(bf16[272,256]{1,0:T(8,128)(2,1)S(1)} %collective-permute-done.refs_1_), channel_id=1, source_target_pairs={{0,1},{1,0},{2,3},{3,2},{4,5},{5,4},{6,7},{7,6},{8,9},{9,8},{10,11... | collective-permute-start | bytes 417800 | tf_op jit(solution)/shard_map/ppermute | solution.py:246
  20.6 5.4 %collective-permute-start.8 = (bf16[272,256]{1,0:T(8,128)(2,1)S(1)}, bf16[272,256]{1,0:T(8,128)(2,1)S(1)}, u32[]{:S(2)}, u32[]{:S(2)}) collective-permute-start(bf16[272,256]{1,0:T(8,128)(2,1)S(1)} %collective-permute-done.2.refs_3_), channel_id=1, source_target_pairs={{0,1},{1,0},{2,3},{3,2},{4,5},{5,4},{6,7},{7,6},{8,9},{9,8},{10,11... | collective-permute-start | bytes 417800 | tf_op jit(solution)/shard_map/ppermute | solution.py:246
  20.6 5.4 %collective-permute-start.7 = (bf16[272,256]{1,0:T(8,128)(2,1)S(1)}, bf16[272,256]{1,0:T(8,128)(2,1)S(1)}, u32[]{:S(2)}, u32[]{:S(2)}) collective-permute-start(bf16[272,256]{1,0:T(8,128)(2,1)S(1)} %collective-permute-done.1.refs_2_), channel_id=1, source_target_pairs={{0,1},{1,0},{2,3},{3,2},{4,5},{5,4},{6,7},{7,6},{8,9},{9,8},{10,11... | collective-permute-start | bytes 417800 | tf_op jit(solution)/shard_map/ppermute | solution.py:246
  23.6 2.4 %collective-permute-start.9 = (bf16[272,256]{1,0:T(8,128)(2,1)S(1)}, bf16[272,256]{1,0:T(8,128)(2,1)S(1)}, u32[]{:S(2)}, u32[]{:S(2)}) collective-permute-start(bf16[272,256]{1,0:T(8,128)(2,1)S(1)} %collective-permute-done.3.refs_4_), channel_id=1, source_target_pairs={{0,1},{1,0},{2,3},{3,2},{4,5},{5,4},{6,7},{7,6},{8,9},{9,8},{10,11... | collective-permute-start | bytes 417800 | tf_op jit(solution)/shard_map/ppermute | solution.py:246
  25.9 1.4 %collective-permute-start.10 = (bf16[272,256]{1,0:T(8,128)(2,1)S(1)}, bf16[272,256]{1,0:T(8,128)(2,1)S(1)}, u32[]{:S(2)}, u32[]{:S(2)}) collective-permute-start(bf16[272,256]{1,0:T(8,128)(2,1)S(1)} %collective-permute-done.4.refs_5_), channel_id=1, source_target_pairs={{0,1},{1,0},{2,3},{3,2},{4,5},{5,4},{6,7},{7,6},{8,9},{9,8},{10,11... | collective-permute-start | bytes 417800 | tf_op jit(solution)/shard_map/ppermute | solution.py:246
  27.3 0.7 %copy-start.1 = (s32[1,1,4]{2,1,0:T(1,128)S(1)}, s32[1,1,4]{2,1,0:T(1,128)}, u32[]{:S(2)}) copy-start(s32[1,1,4]{2,1,0:T(1,128)} %param.11) | copy-start | bytes 52
  27.9 0.9 %copy-start = (bf16[272,256]{1,0:T(8,128)(2,1)S(1)}, bf16[272,256]{1,0:T(8,128)(2,1)}, u32[]{:S(2)}) copy-start(bf16[272,256]{1,0:T(8,128)(2,1)} %shard_map.93.refs_0_) | copy-start | bytes 417796
  28.8 1.0 %copy-start.2 = (bf16[1,128,2048]{2,1,0:T(8,128)(2,1)S(1)}, bf16[1,128,2048]{2,1,0:T(8,128)(2,1)}, u32[]{:S(2)}) copy-start(bf16[1,128,2048]{2,1,0:T(8,128)(2,1)} %param.6) | copy-start | bytes 1572868
  29.9 1.0 %copy-start.3 = (bf16[1,128,2048]{2,1,0:T(8,128)(2,1)S(1)}, bf16[1,128,2048]{2,1,0:T(8,128)(2,1)}, u32[]{:S(2)}) copy-start(bf16[1,128,2048]{2,1,0:T(8,128)(2,1)} %param.9) | copy-start | bytes 1572868
  39.1 1.8 %collective-permute-start.12 = (bf16[3,256,256]{2,1,0:T(8,128)(2,1)S(1)}, bf16[3,256,256]{2,1,0:T(8,128)(2,1)S(1)}, u32[]{:S(2)}, u32[]{:S(2)}) collective-permute-start(bf16[3,256,256]{2,1,0:T(8,128)(2,1)S(1)} %get-tuple-element.15), channel_id=1, source_target_pairs={{0,1},{1,0},{2,3},{3,2},{4,5},{5,4},{6,7},{7,6},{8,9},{9,8},{10,11... | collective-permute-start | bytes 1179656 | tf_op jit(solution)/shard_map/ppermute | solution.py:246
  39.6 3.6 %collective-permute-start.11 = (bf16[3,256,256]{2,1,0:T(8,128)(2,1)S(1)}, bf16[3,256,256]{2,1,0:T(8,128)(2,1)S(1)}, u32[]{:S(2)}, u32[]{:S(2)}) collective-permute-start(bf16[3,256,256]{2,1,0:T(8,128)(2,1)S(1)} %get-tuple-element.13), channel_id=1, source_target_pairs={{0,1},{1,0},{2,3},{3,2},{4,5},{5,4},{6,7},{7,6},{8,9},{9,8},{10,11... | collective-permute-start | bytes 1179656 | tf_op jit(solution)/shard_map/ppermute | solution.py:246
  41.1 6.4 %collective-permute-start.15 = (bf16[256,256]{1,0:T(8,128)(2,1)S(1)}, bf16[256,256]{1,0:T(8,128)(2,1)S(1)}, u32[]{:S(2)}, u32[]{:S(2)}) collective-permute-start(bf16[256,256]{1,0:T(8,128)(2,1)S(1)} %get-tuple-element.17), channel_id=1, source_target_pairs={{0,16},{16,0},{1,17},{17,1},{2,18},{18,2},{3,19},{19,3},{4,20},{20... | collective-permute-start | bytes 393224 | tf_op jit(solution)/shard_map/ppermute | solution.py:243
  43.1 7.7 %collective-permute-start.14 = (bf16[256,256]{1,0:T(8,128)(2,1)S(1)}, bf16[256,256]{1,0:T(8,128)(2,1)S(1)}, u32[]{:S(2)}, u32[]{:S(2)}) collective-permute-start(bf16[256,256]{1,0:T(8,128)(2,1)S(1)} %get-tuple-element.18), channel_id=1, source_target_pairs={{0,16},{16,0},{1,17},{17,1},{2,18},{18,2},{3,19},{19,3},{4,20},{20... | collective-permute-start | bytes 393224 | tf_op jit(solution)/shard_map/ppermute | solution.py:243
  47.5 6.9 %collective-permute-start.16 = (bf16[256,256]{1,0:T(8,128)(2,1)S(1)}, bf16[256,256]{1,0:T(8,128)(2,1)S(1)}, u32[]{:S(2)}, u32[]{:S(2)}) collective-permute-start(bf16[256,256]{1,0:T(8,128)(2,1)S(1)} %fusion), channel_id=1, source_target_pairs={{2,0},{3,1},{4,2},{5,3},{6,4},{7,5},{10,8},{11,9},{12,10},{13,11},... | collective-permute-start | bytes 393224 | tf_op jit(solution)/shard_map/ppermute | solution.py:309
  48.8 6.9 %collective-permute-start.13 = (bf16[256,256]{1,0:T(8,128)(2,1)S(1)}, bf16[256,256]{1,0:T(8,128)(2,1)S(1)}, u32[]{:S(2)}, u32[]{:S(2)}) collective-permute-start(bf16[256,256]{1,0:T(8,128)(2,1)S(1)} %get-tuple-element.16), channel_id=1, source_target_pairs={{0,16},{16,0},{1,17},{17,1},{2,18},{18,2},{3,19},{19,3},{4,20},{20... | collective-permute-start | bytes 393224 | tf_op jit(solution)/shard_map/ppermute | solution.py:243
  54.4 8.2 %collective-permute-start.17 = (bf16[256,256]{1,0:T(8,128)(2,1)S(1)}, bf16[256,256]{1,0:T(8,128)(2,1)S(1)}, u32[]{:S(2)}, u32[]{:S(2)}) collective-permute-start(bf16[256,256]{1,0:T(8,128)(2,1)S(1)} %fusion.2), channel_id=1, source_target_pairs={{2,0},{3,1},{4,2},{5,3},{6,4},{7,5},{10,8},{11,9},{12,10},{13,11},... | collective-permute-start | bytes 393224 | tf_op jit(solution)/shard_map/ppermute | solution.py:309

commit v3 on v1

v3 whole, which is shorter than its diff:
```python
import functools
import math

import jax
import jax.numpy as jnp
from jax import lax
from jax.experimental import pallas as pl
from jax.experimental.pallas import tpu as pltpu
from jax.sharding import Mesh
from jax.sharding import PartitionSpec as P

HEAD_SIZE = 128
QUERY_PER_KEY = 8
NBLK = 4
META = 16
DOC_ROW = NBLK
DOC_VALUES = 16
GROUPED = 2
HALF = QUERY_PER_KEY * HEAD_SIZE
NEG = -1e30
F32, BF16, I32 = jnp.float32, jnp.bfloat16, jnp.int32
NT = (((1,), (1,)), ((), ()))
VMEM = pl.BlockSpec(memory_space=pltpu.VMEM)
SMEM = pl.BlockSpec(memory_space=pltpu.SMEM)
HBM = pl.BlockSpec(memory_space=pltpu.HBM)


def core_index():
    return lax.rem(lax.axis_index("ctx"), 2)


def payload_kernel(
    swap_ref, key_ref, value_ref, docs_ref, query_ref, grad_ref, own_ref, side_ref, rows_ref, sems
):
    rows = key_ref.shape[0]
    core = core_index()
    away = pl.ds(pl.multiple_of((1 - core) * HALF, HALF), HALF)
    copies = [
        pltpu.make_async_copy(query_ref.at[:, away], rows_ref.at[pl.ds(0, rows), :], sems.at[0]),
        pltpu.make_async_copy(grad_ref.at[:, away], rows_ref.at[pl.ds(rows, rows), :], sems.at[1]),
    ]
    for copy in copies:
        copy.start()
    docs = jnp.broadcast_to(docs_ref[...].astype(F32), (META, rows))
    place = lax.broadcasted_iota(I32, docs.shape, 0)
    meta = jnp.where(place == DOC_ROW, docs, 0.0)
    for block in range(NBLK):
        meta = jnp.where(place == block, swap_ref[block].astype(F32), meta)
    meta = meta.astype(BF16)
    for ref, head in ((own_ref, core), (side_ref, 1 - core)):
        lane = pl.ds(pl.multiple_of(head * HEAD_SIZE, HEAD_SIZE), HEAD_SIZE)
        ref[:rows, :] = key_ref[:, lane]
        ref[rows : 2 * rows, :] = value_ref[:, lane]
        ref[2 * rows :, :] = meta
    for copy in copies:
        copy.wait()


def join_kernel(first_ref, second_ref, both_ref):
    size = first_ref.shape[0]
    both_ref[:size, :] = first_ref[...]
    both_ref[size:, :] = second_ref[...]


def finish_kernel(own_ref, side_ref, out_ref, query_grad_ref, sems):
    rows = out_ref.shape[0]
    core = core_index()
    copies = []
    for at, (source, head) in enumerate(((own_ref, core), (side_ref, 1 - core))):
        lanes = pl.ds(pl.multiple_of(head * HALF, HALF), HALF)
        for part, target in enumerate((out_ref, query_grad_ref)):
            copies.append(
                pltpu.make_async_copy(
                    source.at[pl.ds(part * rows, rows), :], target.at[:, lanes], sems.at[2 * at + part]
                )
            )
    for copy in copies:
        copy.start()
    for copy in copies:
        copy.wait()


def attention_kernel(hops, query_ref, grad_ref, side_rows_ref, *refs):
    count = hops + 1
    slots = 2 * count
    window = slots - 1
    homes, aways = refs[:count], refs[count : 2 * count]
    own_out_ref, side_out_ref = refs[2 * count : 2 * count + 2]
    home_outs = refs[2 * count + 2 : 3 * count + 2]
    away_outs = refs[3 * count + 2 : 4 * count + 2]
    (
        query_all,
        grad_all,
        out_all,
        key_log,
        value_log,
        key_turned,
        value_turned,
        doc_window,
        starts,
        key_total,
        value_total,
        logical_of,
        needed_of,
        sems,
    ) = refs[4 * count + 2 :]
    rows = query_ref.shape[0]
    per_block = rows // NBLK
    lanes = QUERY_PER_KEY * per_block
    size = 2 * rows + META
    core = core_index()
    chip = lax.axis_index("ctx") // 2
    parity = (core, 1 - core)
    scale = 1.0 / math.sqrt(HEAD_SIZE)
    factor = scale * math.log2(math.e)

    mine = pl.ds(pl.multiple_of(core * HALF, HALF), HALF)
    copies = [
        pltpu.make_async_copy(query_ref.at[:, mine], query_all.at[0], sems.at[0]),
        pltpu.make_async_copy(grad_ref.at[:, mine], grad_all.at[0], sems.at[1]),
        pltpu.make_async_copy(side_rows_ref.at[pl.ds(0, rows), :], query_all.at[1], sems.at[2]),
        pltpu.make_async_copy(side_rows_ref.at[pl.ds(rows, rows), :], grad_all.at[1], sems.at[3]),
    ]
    for copy in copies:
        copy.start()

    key_total[...] = jnp.zeros_like(key_total)
    value_total[...] = jnp.zeros_like(value_total)
    doc_window[...] = jnp.full_like(doc_window, 1e4)

    def meta_of(ref, who):
        return ref[who * size + 2 * rows : (who + 1) * size, :].astype(F32)

    for k in range(count):
        for who in range(2):
            slot = 2 * (hops - k) + parity[who]
            base = pl.multiple_of(slot * rows, rows)
            for logical, ref in ((0, homes[k]), (1, aways[k])):
                docs = meta_of(ref, who)[DOC_ROW : DOC_ROW + 1, :]
                doc_window[logical, pl.ds(slot, 1), :] = jnp.where(chip >= k, docs, -1.0)
            flags = meta_of(homes[k], who)
            for block in range(NBLK):
                mask = (
                    jnp.broadcast_to(flags[block : block + 1, :], (per_block, HEAD_SIZE)).astype(BF16)
                    > 0.5
                )
                at = pl.ds(base + block * per_block, per_block)
                for which, log in ((0, key_log), (1, value_log)):
                    first = who * size + which * rows + block * per_block
                    own = homes[k][first : first + per_block, :]
                    other = aways[k][first : first + per_block, :]
                    log[0, at, :] = jnp.where(mask, other, own)
                    log[1, at, :] = jnp.where(mask, own, other)

    for logical in range(2):
        key_turned[logical] = key_log[logical].T
        value_turned[logical] = value_log[logical].T

    values_down = lax.broadcasted_iota(I32, (DOC_VALUES, rows), 0).astype(F32)
    group = lax.broadcasted_iota(I32, (8, rows), 1) // per_block
    meta_rows = [meta_of(homes[0], who) for who in range(2)]
    for logical in range(2):
        lower = jnp.zeros((DOC_VALUES, rows), F32)
        for slot in range(slots):
            docs = jnp.broadcast_to(doc_window[logical, slot : slot + 1, :], lower.shape)
            lower = lower + jnp.where(docs < values_down, 1.0, 0.0)
        lower = jnp.broadcast_to(jnp.sum(lower, axis=1, keepdims=True), lower.shape)
        for who in range(2):
            docs = meta_of((homes, aways)[logical][0], who)[DOC_ROW : DOC_ROW + 1, :]
            docs = jnp.broadcast_to(docs, (8, rows))
            turns = [docs] + [pltpu.roll(docs, t * per_block, 1) for t in range(1, NBLK)]
            for block in range(NBLK):
                tiled = turns[0]
                for t in range(1, NBLK):
                    tiled = jnp.where(group == (block + t) % NBLK, turns[t], tiled)
                tiled = jnp.broadcast_to(tiled[:1], lower.shape)
                start = jnp.sum(jnp.where(tiled == values_down, lower, 0.0), axis=0, keepdims=True)
                starts[logical, who * NBLK + block : who * NBLK + block + 1, :] = start.astype(I32)
    for unit_index in range(2 * NBLK):
        who, block = unit_index // NBLK, unit_index % NBLK
        flag = jnp.max(meta_rows[who][block : block + 1, :]).astype(I32)
        logical_of[unit_index] = flag
        first = jnp.min(starts[flag, unit_index : unit_index + 1, :].astype(F32)).astype(I32)
        needed_of[unit_index] = window + parity[who] - first // rows
    for copy in copies:
        copy.wait()

    def unit(unit_index, chunks):
        who, block = unit_index // NBLK, lax.rem(unit_index, NBLK)
        logical = logical_of[unit_index]
        row_parity = jnp.where(who == 0, core, 1 - core)
        first_slot = window + row_parity - chunks
        first = pl.multiple_of(first_slot * rows, rows)
        span = pl.ds(first, chunks * rows)
        at = pl.ds(pl.multiple_of(block * per_block, per_block), per_block)
        columns = [slice(h * HEAD_SIZE, (h + 1) * HEAD_SIZE) for h in range(QUERY_PER_KEY)]
        query = jnp.concatenate([query_all[who, at, column] for column in columns], axis=0)
        grad = jnp.concatenate([grad_all[who, at, column] for column in columns], axis=0)
        scores = lax.dot_general(key_log[logical, span, :], query, NT, preferred_element_type=F32)
        shape = (chunks * rows, HEAD_SIZE)
        key_place = lax.broadcasted_iota(I32, shape, 0)
        row_first = starts[logical, pl.ds(unit_index, 1), :] - first
        row_last = (
            (chunks - 1) * rows
            + block * per_block
            + lax.rem(lax.broadcasted_iota(I32, (1, HEAD_SIZE), 1), per_block)
        )
        allowed = (key_place >= row_first) & (key_place <= row_last)
        scores = jnp.concatenate(
            [
                jnp.where(allowed, scores[:, lane : lane + HEAD_SIZE], NEG)
                for lane in range(0, lanes, HEAD_SIZE)
            ],
            axis=1,
        )
        peak = jnp.max(scores, axis=0, keepdims=True)
        powers = jnp.exp2((scores - peak) * factor)
        inverse = 1.0 / jnp.sum(powers, axis=0, keepdims=True)
        probs = powers * inverse
        weights = probs.astype(BF16)
        out_turned = jnp.dot(
            value_turned[logical, :, span], weights, preferred_element_type=F32
        ).astype(BF16)
        delta = jnp.sum(grad.T.astype(F32) * out_turned.astype(F32), axis=0, keepdims=True)
        prob_grad = lax.dot_general(
            value_log[logical, span, :], grad, NT, preferred_element_type=F32
        )
        score_grad = (probs * (prob_grad - delta)).astype(BF16)
        query_grad_turned = jnp.dot(
            key_turned[logical, :, span], score_grad, preferred_element_type=F32
        )
        key_add = jnp.dot(score_grad, query, preferred_element_type=F32)
        value_add = jnp.dot(weights, grad, preferred_element_type=F32)
        out = out_turned.T
        query_grad = (query_grad_turned * scale).astype(BF16).T
        return who, at, logical, span, out, query_grad, key_add, value_add

    def step(pair, carry):
        members = [pair * GROUPED + m for m in range(GROUPED)]
        needed = needed_of[members[0]]
        for member in members[1:]:
            needed = jnp.maximum(needed, needed_of[member])
        for chunks in range(1, window + 1):

            @pl.when(needed == chunks)
            def _(chunks=chunks):
                results = [unit(member, chunks) for member in members]
                for who, at, logical, span, out, query_grad, key_add, value_add in results:
                    key_total[logical, span, :] += key_add
                    value_total[logical, span, :] += value_add
                    for h in range(QUERY_PER_KEY):
                        column = slice(h * HEAD_SIZE, (h + 1) * HEAD_SIZE)
                        part = slice(h * per_block, (h + 1) * per_block)
                        out_all[who, 0, at, column] = out[part, :]
                        out_all[who, 1, at, column] = query_grad[part, :]

        return carry

    lax.fori_loop(0, 2 * NBLK // GROUPED, step, 0)
    copies = [
        pltpu.make_async_copy(
            out_all.at[who, which], target.at[pl.ds(which * rows, rows), :], sems.at[2 * who + which]
        )
        for who, target in enumerate((own_out_ref, side_out_ref))
        for which in range(2)
    ]
    for copy in copies:
        copy.start()

    for k in range(count):
        for who in range(2):
            base = pl.multiple_of((2 * (hops - k) + parity[who]) * rows, rows)
            flags = meta_of(homes[k], who)
            for block in range(NBLK):
                at = pl.ds(base + block * per_block, per_block)
                mask = jnp.broadcast_to(flags[block : block + 1, :], (per_block, HEAD_SIZE)) > 0.5
                for which, total, gain in ((0, key_total, scale), (1, value_total, 1.0)):
                    part = (2 * who + which) * rows + block * per_block
                    first = total[0, at, :] * gain
                    second = total[1, at, :] * gain
                    home_outs[k][part : part + per_block, :] = jnp.where(mask, second, first).astype(BF16)
                    away_outs[k][part : part + per_block, :] = jnp.where(mask, first, second).astype(BF16)
    for copy in copies:
        copy.wait()


def local(queries, key_rows, value_rows, out_grad, documents, swapped):
    ranks = lax.axis_size("ctx")
    hops = ranks // 4
    count = hops + 1
    slots = 2 * count
    rows, width = key_rows.shape[1:]
    keys = slots * rows
    size = 2 * rows + META
    queries, out_grad = queries[0], out_grad[0]

    def up(block, k):
        return lax.ppermute(block, "ctx", [(i, i + 2 * k) for i in range(ranks - 2 * k)])

    def down(block, k):
        return lax.ppermute(block, "ctx", [(i + 2 * k, i) for i in range(ranks - 2 * k)])

    def to_partner(block):
        return lax.ppermute(block, "half", [(0, 1), (1, 0)])

    def to_side(block):
        return lax.ppermute(block, "ctx", [(i, i ^ 1) for i in range(ranks)])

    payload, payload_side, rows_side = pl.pallas_call(
        payload_kernel,
        out_shape=[
            jax.ShapeDtypeStruct((size, HEAD_SIZE), BF16),
            jax.ShapeDtypeStruct((size, HEAD_SIZE), BF16),
            jax.ShapeDtypeStruct((2 * rows, HALF), BF16),
        ],
        in_specs=[SMEM, VMEM, VMEM, VMEM, HBM, HBM],
        out_specs=[VMEM, VMEM, HBM],
        scratch_shapes=[pltpu.SemaphoreType.DMA((2,))],
    )(swapped[0, 0], key_rows[0], value_rows[0], documents, queries, out_grad)
    from_side = to_side(payload_side)
    rows_got = to_side(rows_side)
    both = pl.pallas_call(
        join_kernel,
        out_shape=jax.ShapeDtypeStruct((2 * size, HEAD_SIZE), BF16),
        in_specs=[VMEM, VMEM],
        out_specs=VMEM,
    )(payload, from_side)
    home = [both] + [up(both, k) for k in range(1, count)]
    away = [to_partner(block) for block in home]
    chunk = jax.ShapeDtypeStruct((4 * rows, HEAD_SIZE), BF16)
    outs = pl.pallas_call(
        functools.partial(attention_kernel, hops),
        out_shape=[jax.ShapeDtypeStruct((2 * rows, HALF), BF16)] * 2 + [chunk] * (2 * count),
        in_specs=[HBM, HBM, pl.BlockSpec(memory_space=pl.ANY)] + [VMEM] * (2 * count),
        out_specs=[HBM] * 2 + [VMEM] * (2 * count),
        scratch_shapes=[
            pltpu.VMEM((2, rows, HALF), BF16),
            pltpu.VMEM((2, rows, HALF), BF16),
            pltpu.VMEM((2, 2, rows, HALF), BF16),
            pltpu.VMEM((2, keys, HEAD_SIZE), BF16),
            pltpu.VMEM((2, keys, HEAD_SIZE), BF16),
            pltpu.VMEM((2, HEAD_SIZE, keys), BF16),
            pltpu.VMEM((2, HEAD_SIZE, keys), BF16),
            pltpu.VMEM((2, 16, rows), F32),
            pltpu.VMEM((2, 8, rows), I32),
            pltpu.VMEM((2, keys, HEAD_SIZE), F32),
            pltpu.VMEM((2, keys, HEAD_SIZE), F32),
            pltpu.SMEM((2 * NBLK,), I32),
            pltpu.SMEM((2 * NBLK,), I32),
            pltpu.SemaphoreType.DMA((4,)),
        ],
        compiler_params=pltpu.CompilerParams(vmem_limit_bytes=40 * 1024 * 1024),
        cost_estimate=pl.CostEstimate(
            flops=12 * rows * keys * 2048,
            bytes_accessed=4 * 1024 * 1024,
            transcendentals=rows * keys * 16,
        ),
    )(queries, out_grad, rows_got, *home, *away)
    own_out, side_out = outs[:2]
    home_sum, away_sum = outs[2 : 2 + count], outs[2 + count :]

    crossed = [None] * count
    for k in reversed(range(count)):
        crossed[k] = to_partner(away_sum[k])
    parts = []
    for k in reversed(range(count)):
        part = home_sum[k].astype(F32) + crossed[k].astype(F32)
        parts.append(down(part.astype(BF16), k) if k else part)
    out_got = to_side(side_out)
    out, query_grad = pl.pallas_call(
        finish_kernel,
        out_shape=[jax.ShapeDtypeStruct(queries.shape, BF16)] * 2,
        in_specs=[pl.BlockSpec(memory_space=pl.ANY)] * 2,
        out_specs=[HBM] * 2,
        scratch_shapes=[pltpu.SemaphoreType.DMA((4,))],
    )(own_out, out_got)
    parts[0], out, query_grad = lax.optimization_barrier((parts[0], out, query_grad))
    total = sum(part.astype(F32) for part in parts).astype(BF16)
    grads_got = to_side(total[2 * rows :])
    grads = total[: 2 * rows]
    first = core_index() == 0
    grads = jnp.concatenate(
        [jnp.where(first, grads, grads_got), jnp.where(first, grads_got, grads)], axis=1
    )
    return (out[None], query_grad[None], grads[None, :rows], grads[None, rows:])


def solution(mesh):
    groups, ranks = mesh.devices.shape
    wide = Mesh(mesh.devices.reshape(2, groups // 2, ranks), ("half", "pair", "ctx"))
    spec3 = P(("half", "pair"), "ctx", None)
    in_specs = (spec3, spec3, spec3, spec3, P(("half", "pair"), "ctx"), spec3)
    return jax.shard_map(
        local, mesh=wide, in_specs=in_specs, out_specs=(spec3,) * 4, check_vma=False
    )
```

time: 144 us -> 99.8 us (0.69); the launches traced: 144 us -> 98.4 us
  waiting for transfers between devices: 109 us -> 14 us
  Pallas kernels: 8.68 us -> 59.5 us
  starting transfers between devices: 0.08 us -> 20.1 us
  between operations: 14.1 us -> 0.82 us
  local copies, waits for them, and re-layouts: 10.3 us -> 3.15 us
    reduce_scatter x1 -> x0, waiting for transfers between devices: 64.5 us -> none  [local(): lax.psum_scatter(partial.reshape(2 * ranks, 2 * rows, width), ('half', 'c...]
    pallas_call x1 -> x4, Pallas kernels: 8.68 us -> 59.5 us  [the longest x1 32.9 us: local(): pl.pallas_call(finish_kernel, out_shape=[jax.ShapeDtypeStruct(queries.sha...]
    all_gather x1 -> x0, waiting for transfers between devices: 44.6 us -> none  [local(): gathered = lax.all_gather(payload, ('half', 'ctx'), axis=0, tiled=False)]
    ppermute x0 -> x14, starting transfers between devices: none -> 20.1 us  [the longest x2 9.34 us: up(): lax.ppermute(block, 'ctx', [(i, i + 2 * k) for i in range(ranks - 2 * k)])]
    ppermute x0 -> x14, waiting for transfers between devices: none -> 14 us  [the longest x6 9.81 us: to_partner(): return lax.ppermute(block, 'half', [(0, 1), (1, 0)])]
    concatenate x1 -> x0, local copies, waits for them, and re-layouts: 4.17 us -> none  [payload_of(): return jnp.concatenate([key_rows, value_rows, meta], axis=0)]
    convert_element_type x3, other arithmetic: 1.99 us -> 0.15 us  [the longest x2 0.08 us: local(): parts.append(down(part.astype(BF16), k) if k else part)]
    slice x1, local copies, waits for them, and re-layouts: 1.53 us -> 0.01 us  [local(): grads_got = to_side(total[2 * rows:])]
  transfers between devices with their start and end apart: 2 -> 14, of which waited for: 2 -> 8; matrix products, arithmetic and copies ran while one was open for 0% -> 0% of each run, Pallas kernels for 0% -> 35%
where the time goes in v3:
time: 99.8 us; the launch traced here: 98.4 us
  Pallas kernels  59.5 us (60%)
  starting transfers between devices  20.1 us (20%)
  waiting for transfers between devices  14 us (14%)
  local copies, waits for them, and re-layouts  3.15 us (3%)
    pallas_call x1, Pallas kernels, local(): pl.pallas_call(finish_kernel, out_shape=[jax.ShapeDtypeStruct(queries.sha...  32.9 us
    pallas_call x1, Pallas kernels, local(): pl.pallas_call(payload_kernel, out_shape=[jax.ShapeDtypeStruct((size, HEA...  18.6 us
    ppermute x6, waiting for transfers between devices, to_partner(): return lax.ppermute(block, 'half', [(0, 1), (1, 0)])  9.81 us
    ppermute x2, starting transfers between devices, up(): lax.ppermute(block, 'ctx', [(i, i + 2 * k) for i in range(ranks - 2 * k)])  9.34 us
    ppermute x6, starting transfers between devices, to_partner(): return lax.ppermute(block, 'half', [(0, 1), (1, 0)])  7.47 us
    pallas_call x1, Pallas kernels, local(): pl.pallas_call(functools.partial(attention_kernel, hops), out_shape=[jax....  6.4 us
    unnamed x12, local copies, waits for them, and re-layouts  3.14 us
    ppermute x4, waiting for transfers between devices, to_side(): return lax.ppermute(block, 'ctx', [(i, i ^ 1) for i in range(ranks)])  3.01 us
  transfers between devices with their start and end apart: 14, of which 8 were waited for; matrix products, arithmetic and copies ran while one was open for 0% of the time, Pallas kernels for 35%

profile of v3, /device:TPU:0, one launch (start us, length us, event | category | flops | bytes accessed | tf_op | source)
XLA Modules:
  0.0 98.4 jit_solution(1540948560602545012)
XLA Ops:
  0.6 0.0 copy-start.1
  0.6 0.0 copy-start.2
  0.7 18.6 %shard_map.93 = (bf16[272,128]{1,0:T(8,128)(2,1)}, bf16[272,128]{1,0:T(8,128)(2,1)}, bf16[256,1024]{1,0:T(8,128)(2,1)}) custom-call(s32[4]{0:T(128)} %bitcast.17, bf16[128,256]{1,0:T(8,128)(2,1)} %bitcast.15, bf16[128,256]{1,0:T(8,128)(2,1)} %bitcast.16, s32[1,128]{1,0:T(1,128)} %docs_ref.1, bf16[128,2048]{1,0:T(8,128)(2,1)} %bitcast.11, ...), custom_call_target="tpu_custom_call" | custom-call | tf_op jit(solution)/shard_map/pallas_call | solution.py:309
  19.3 0.5 collective-permute-start
  19.8 0.1 collective-permute-start.1
  19.9 1.8 %collective-permute-done.1.second_ref = bf16[272,128]{1,0:T(8,128)(2,1)S(1)} collective-permute-done((bf16[272,128]{1,0:T(8,128)(2,1)}, bf16[272,128]{1,0:T(8,128)(2,1)S(1)}, u32[]{:S(2)}, u32[]{:S(2)}) %collective-permute-start.1) | collective-permute-done | bytes 69664 | tf_op jit(solution)/shard_map/ppermute | solution.py:307
  21.7 0.0 copy-start.5
  21.7 0.6 copy-done.5
  22.3 1.6 %shard_map.94.refs_0_ = bf16[544,128]{1,0:T(8,128)(2,1)} custom-call(bf16[272,128]{1,0:T(8,128)(2,1)} %get-tuple-element.21.first_ref, bf16[272,128]{1,0:T(8,128)(2,1)} %copy-done.5), custom_call_target="tpu_custom_call" | custom-call | tf_op jit(solution)/shard_map/pallas_call | solution.py:322
  23.9 4.8 %collective-permute-start.2 = (bf16[544,128]{1,0:T(8,128)(2,1)}, bf16[544,128]{1,0:T(8,128)(2,1)S(1)}, u32[]{:S(2)}, u32[]{:S(2)}) collective-permute-start(bf16[544,128]{1,0:T(8,128)(2,1)} %shard_map.94.refs_0_), channel_id=1, source_target_pairs={{0,2},{1,3},{2,4},{3,5},{4,6},{5,7},{8,10},{9,11},{10,12},{11,13},... | collective-permute-start | bytes 417800 | tf_op jit(solution)/shard_map/ppermute | solution.py:298
  28.7 4.5 %collective-permute-start.3 = (bf16[544,128]{1,0:T(8,128)(2,1)}, bf16[544,128]{1,0:T(8,128)(2,1)S(1)}, u32[]{:S(2)}, u32[]{:S(2)}) collective-permute-start(bf16[544,128]{1,0:T(8,128)(2,1)} %shard_map.94.refs_0_), channel_id=1, source_target_pairs={{0,4},{1,5},{2,6},{3,7},{8,12},{9,13},{10,14},{11,15},{16,20},{17,... | collective-permute-start | bytes 417800 | tf_op jit(solution)/shard_map/ppermute | solution.py:298
  33.2 1.6 %collective-permute-start.4 = (bf16[544,128]{1,0:T(8,128)(2,1)}, bf16[544,128]{1,0:T(8,128)(2,1)S(1)}, u32[]{:S(2)}, u32[]{:S(2)}) collective-permute-start(bf16[544,128]{1,0:T(8,128)(2,1)} %shard_map.94.refs_0_), channel_id=1, source_target_pairs={{0,16},{16,0},{1,17},{17,1},{2,18},{18,2},{3,19},{19,3},{4,20},{20... | collective-permute-start | bytes 417800 | tf_op jit(solution)/shard_map/ppermute | solution.py:304
  34.8 0.0 collective-permute-done.2.refs_1_
  34.8 0.5 collective-permute-start.5
  35.3 1.2 %collective-permute-done.3.refs_2_ = bf16[544,128]{1,0:T(8,128)(2,1)S(1)} collective-permute-done((bf16[544,128]{1,0:T(8,128)(2,1)}, bf16[544,128]{1,0:T(8,128)(2,1)S(1)}, u32[]{:S(2)}, u32[]{:S(2)}) %collective-permute-start.3) | collective-permute-done | bytes 139296 | tf_op jit(solution)/shard_map/ppermute | solution.py:298
  36.5 1.5 %collective-permute-start.6 = (bf16[544,128]{1,0:T(8,128)(2,1)S(1)}, bf16[544,128]{1,0:T(8,128)(2,1)S(1)}, u32[]{:S(2)}, u32[]{:S(2)}) collective-permute-start(bf16[544,128]{1,0:T(8,128)(2,1)S(1)} %collective-permute-done.3.refs_2_), channel_id=1, source_target_pairs={{0,16},{16,0},{1,17},{17,1},{2,18},{18,2},{3,19},{19,3},{4,20},{20... | collective-permute-start | bytes 417800 | tf_op jit(solution)/shard_map/ppermute | solution.py:304
  38.0 2.1 %collective-permute-done.4.refs_3_ = bf16[544,128]{1,0:T(8,128)(2,1)S(1)} collective-permute-done((bf16[544,128]{1,0:T(8,128)(2,1)}, bf16[544,128]{1,0:T(8,128)(2,1)S(1)}, u32[]{:S(2)}, u32[]{:S(2)}) %collective-permute-start.4) | collective-permute-done | bytes 139296 | tf_op jit(solution)/shard_map/ppermute | solution.py:304
  40.1 3.0 %collective-permute-done.5.refs_4_ = bf16[544,128]{1,0:T(8,128)(2,1)S(1)} collective-permute-done((bf16[544,128]{1,0:T(8,128)(2,1)S(1)}, bf16[544,128]{1,0:T(8,128)(2,1)S(1)}, u32[]{:S(2)}, u32[]{:S(2)}) %collective-permute-start.5) | collective-permute-done | bytes 139296 | tf_op jit(solution)/shard_map/ppermute | solution.py:304
  43.1 1.5 %collective-permute-done.6.refs_5_ = bf16[544,128]{1,0:T(8,128)(2,1)S(1)} collective-permute-done((bf16[544,128]{1,0:T(8,128)(2,1)S(1)}, bf16[544,128]{1,0:T(8,128)(2,1)S(1)}, u32[]{:S(2)}, u32[]{:S(2)}) %collective-permute-start.6) | collective-permute-done | bytes 139296 | tf_op jit(solution)/shard_map/ppermute | solution.py:304
  44.6 0.0 collective-permute-done.side_rows_ref
  44.6 0.0 copy-done.1
  44.6 0.0 copy-done.2
  44.6 0.0 copy-start.3
  44.6 0.9 copy-done.3
  45.5 6.4 %shard_map.95 = (bf16[256,1024]{1,0:T(8,128)(2,1)S(1)}, bf16[256,1024]{1,0:T(8,128)(2,1)S(1)}, bf16[512,128]{1,0:T(8,128)(2,1)S(1)}, bf16[512,128]{1,0:T(8,128)(...) custom-call(bf16[128,2048]{1,0:T(8,128)(2,1)S(1)} %bitcast.12, ...), custom_call_target="tpu_custom_call" | custom-call | flops 2415919104 | bytes 4194304 | tf_op jit(solution)/shard_map/pallas_call | solution.py:331
  52.0 0.0 copy-start
  52.0 0.8 copy-done
  52.8 1.8 %collective-permute-start.7 = (bf16[512,128]{1,0:T(8,128)(2,1)S(1)}, bf16[512,128]{1,0:T(8,128)(2,1)S(1)}, u32[]{:S(2)}, u32[]{:S(2)}) collective-permute-start(bf16[512,128]{1,0:T(8,128)(2,1)S(1)} %get-tuple-element.24), channel_id=1, source_target_pairs={{0,16},{16,0},{1,17},{17,1},{2,18},{18,2},{3,19},{19,3},{4,20},{20... | collective-permute-start | bytes 393224 | tf_op jit(solution)/shard_map/ppermute | solution.py:304
  54.6 0.2 collective-permute-start.10
  54.8 0.0 collective-permute-start.9
  54.8 1.8 %collective-permute-start.12 = (bf16[512,128]{1,0:T(8,128)(2,1)S(1)}, bf16[512,128]{1,0:T(8,128)(2,1)S(1)}, u32[]{:S(2)}, u32[]{:S(2)}) collective-permute-start(bf16[512,128]{1,0:T(8,128)(2,1)S(1)} %get-tuple-element.35), channel_id=1, source_target_pairs={{0,16},{16,0},{1,17},{17,1},{2,18},{18,2},{3,19},{19,3},{4,20},{20... | collective-permute-start | bytes 393224 | tf_op jit(solution)/shard_map/ppermute | solution.py:304
  56.6 2.1 %collective-permute-done.7 = bf16[512,128]{1,0:T(8,128)(2,1)S(1)} collective-permute-done((bf16[512,128]{1,0:T(8,128)(2,1)S(1)}, bf16[512,128]{1,0:T(8,128)(2,1)S(1)}, u32[]{:S(2)}, u32[]{:S(2)}) %collective-permute-start.7) | collective-permute-done | bytes 131104 | tf_op jit(solution)/shard_map/ppermute | solution.py:304
  58.7 1.3 %collective-permute-start.8 = (bf16[512,128]{1,0:T(8,128)(2,1)S(1)}, bf16[512,128]{1,0:T(8,128)(2,1)S(1)}, u32[]{:S(2)}, u32[]{:S(2)}) collective-permute-start(bf16[512,128]{1,0:T(8,128)(2,1)S(1)} %add_convert_fusion.2), channel_id=1, source_target_pairs={{4,0},{5,1},{6,2},{7,3},{12,8},{13,9},{14,10},{15,11},{20,16},{21,... | collective-permute-start | bytes 393224 | tf_op jit(solution)/shard_map/ppermute | solution.py:301
  60.0 1.1 %collective-permute-done.10 = bf16[512,128]{1,0:T(8,128)(2,1)S(1)} collective-permute-done((bf16[512,128]{1,0:T(8,128)(2,1)S(1)}, bf16[512,128]{1,0:T(8,128)(2,1)S(1)}, u32[]{:S(2)}, u32[]{:S(2)}) %collective-permute-start.10) | collective-permute-done | bytes 131104 | tf_op jit(solution)/shard_map/ppermute | solution.py:304
  61.2 1.3 %collective-permute-start.11 = (bf16[512,128]{1,0:T(8,128)(2,1)S(1)}, bf16[512,128]{1,0:T(8,128)(2,1)S(1)}, u32[]{:S(2)}, u32[]{:S(2)}) collective-permute-start(bf16[512,128]{1,0:T(8,128)(2,1)S(1)} %add_convert_fusion.1), channel_id=1, source_target_pairs={{2,0},{3,1},{4,2},{5,3},{6,4},{7,5},{10,8},{11,9},{12,10},{13,11},... | collective-permute-start | bytes 393224 | tf_op jit(solution)/shard_map/ppermute | solution.py:301
  62.5 0.0 collective-permute-done.9.side_ref
  62.5 0.0 copy-start.4
  62.5 0.8 copy-done.4
  63.3 32.9 %shard_map.96 = (bf16[128,2048]{1,0:T(8,128)(2,1)}, bf16[128,2048]{1,0:T(8,128)(2,1)}) custom-call(bf16[256,1024]{1,0:T(8,128)(2,1)} %copy-done, bf16[256,1024]{1,0:T(8,128)(2,1)} %copy-done.4), custom_call_target="tpu_custom_call" | custom-call | tf_op jit(solution)/shard_map/pallas_call | solution.py:370
  96.3 0.0 collective-permute-done.8
  96.3 0.0 collective-permute-done.12
  96.3 0.0 collective-permute-done.11
  96.3 0.1 add_convert_fusion
  96.4 0.1 collective-permute-start.13
  96.5 1.2 %collective-permute-done.13 = bf16[256,128]{1,0:T(8,128)(2,1)S(1)} collective-permute-done((bf16[256,128]{1,0:T(8,128)(2,1)S(1)}, bf16[256,128]{1,0:T(8,128)(2,1)S(1)}, u32[]{:S(2)}, u32[]{:S(2)}) %collective-permute-start.13) | collective-permute-done | bytes 65568 | tf_op jit(solution)/shard_map/ppermute | solution.py:307
  97.7 0.7 fusion.2
  (4 shorter events, 0.1 us)
Async XLA Ops:
  0.6 44.0 %copy-start.1 = (bf16[1,128,2048]{2,1,0:T(8,128)(2,1)S(1)}, bf16[1,128,2048]{2,1,0:T(8,128)(2,1)}, u32[]{:S(2)}) copy-start(bf16[1,128,2048]{2,1,0:T(8,128)(2,1)} %param.6) | copy-start | bytes 1572868
  0.6 44.0 %copy-start.2 = (bf16[1,128,2048]{2,1,0:T(8,128)(2,1)S(1)}, bf16[1,128,2048]{2,1,0:T(8,128)(2,1)}, u32[]{:S(2)}) copy-start(bf16[1,128,2048]{2,1,0:T(8,128)(2,1)} %param.9) | copy-start | bytes 1572868
  19.3 25.3 %collective-permute-start = (bf16[256,1024]{1,0:T(8,128)(2,1)}, bf16[256,1024]{1,0:T(8,128)(2,1)S(1)}, u32[]{:S(2)}, u32[]{:S(2)}) collective-permute-start(bf16[256,1024]{1,0:T(8,128)(2,1)} %get-tuple-element.20), channel_id=1, source_target_pairs={{0,1},{1,0},{2,3},{3,2},{4,5},{5,4},{6,7},{7,6},{8,9},{9,8},{10,11... | collective-permute-start | bytes 1572872 | tf_op jit(solution)/shard_map/ppermute | solution.py:307
  19.8 1.8 %collective-permute-start.1 = (bf16[272,128]{1,0:T(8,128)(2,1)}, bf16[272,128]{1,0:T(8,128)(2,1)S(1)}, u32[]{:S(2)}, u32[]{:S(2)}) collective-permute-start(bf16[272,128]{1,0:T(8,128)(2,1)} %get-tuple-element.22), channel_id=1, source_target_pairs={{0,1},{1,0},{2,3},{3,2},{4,5},{5,4},{6,7},{7,6},{8,9},{9,8},{10,11... | collective-permute-start | bytes 208904 | tf_op jit(solution)/shard_map/ppermute | solution.py:307
  21.7 0.6 copy-start.5
  23.9 10.9 %collective-permute-start.2 = (bf16[544,128]{1,0:T(8,128)(2,1)}, bf16[544,128]{1,0:T(8,128)(2,1)S(1)}, u32[]{:S(2)}, u32[]{:S(2)}) collective-permute-start(bf16[544,128]{1,0:T(8,128)(2,1)} %shard_map.94.refs_0_), channel_id=1, source_target_pairs={{0,2},{1,3},{2,4},{3,5},{4,6},{5,7},{8,10},{9,11},{10,12},{11,13},... | collective-permute-start | bytes 417800 | tf_op jit(solution)/shard_map/ppermute | solution.py:298
  28.7 7.8 %collective-permute-start.3 = (bf16[544,128]{1,0:T(8,128)(2,1)}, bf16[544,128]{1,0:T(8,128)(2,1)S(1)}, u32[]{:S(2)}, u32[]{:S(2)}) collective-permute-start(bf16[544,128]{1,0:T(8,128)(2,1)} %shard_map.94.refs_0_), channel_id=1, source_target_pairs={{0,4},{1,5},{2,6},{3,7},{8,12},{9,13},{10,14},{11,15},{16,20},{17,... | collective-permute-start | bytes 417800 | tf_op jit(solution)/shard_map/ppermute | solution.py:298
  33.2 6.9 %collective-permute-start.4 = (bf16[544,128]{1,0:T(8,128)(2,1)}, bf16[544,128]{1,0:T(8,128)(2,1)S(1)}, u32[]{:S(2)}, u32[]{:S(2)}) collective-permute-start(bf16[544,128]{1,0:T(8,128)(2,1)} %shard_map.94.refs_0_), channel_id=1, source_target_pairs={{0,16},{16,0},{1,17},{17,1},{2,18},{18,2},{3,19},{19,3},{4,20},{20... | collective-permute-start | bytes 417800 | tf_op jit(solution)/shard_map/ppermute | solution.py:304
  34.8 8.3 %collective-permute-start.5 = (bf16[544,128]{1,0:T(8,128)(2,1)S(1)}, bf16[544,128]{1,0:T(8,128)(2,1)S(1)}, u32[]{:S(2)}, u32[]{:S(2)}) collective-permute-start(bf16[544,128]{1,0:T(8,128)(2,1)S(1)} %collective-permute-done.2.refs_1_), channel_id=1, source_target_pairs={{0,16},{16,0},{1,17},{17,1},{2,18},{18,2},{3,19},{19,3},{4,20},{20... | collective-permute-start | bytes 417800 | tf_op jit(solution)/shard_map/ppermute | solution.py:304
  36.5 8.1 %collective-permute-start.6 = (bf16[544,128]{1,0:T(8,128)(2,1)S(1)}, bf16[544,128]{1,0:T(8,128)(2,1)S(1)}, u32[]{:S(2)}, u32[]{:S(2)}) collective-permute-start(bf16[544,128]{1,0:T(8,128)(2,1)S(1)} %collective-permute-done.3.refs_2_), channel_id=1, source_target_pairs={{0,16},{16,0},{1,17},{17,1},{2,18},{18,2},{3,19},{19,3},{4,20},{20... | collective-permute-start | bytes 417800 | tf_op jit(solution)/shard_map/ppermute | solution.py:304
  44.6 0.9 copy-start.3
  52.0 0.8 copy-start
  52.8 5.9 %collective-permute-start.7 = (bf16[512,128]{1,0:T(8,128)(2,1)S(1)}, bf16[512,128]{1,0:T(8,128)(2,1)S(1)}, u32[]{:S(2)}, u32[]{:S(2)}) collective-permute-start(bf16[512,128]{1,0:T(8,128)(2,1)S(1)} %get-tuple-element.24), channel_id=1, source_target_pairs={{0,16},{16,0},{1,17},{17,1},{2,18},{18,2},{3,19},{19,3},{4,20},{20... | collective-permute-start | bytes 393224 | tf_op jit(solution)/shard_map/ppermute | solution.py:304
  54.6 6.6 %collective-permute-start.10 = (bf16[512,128]{1,0:T(8,128)(2,1)S(1)}, bf16[512,128]{1,0:T(8,128)(2,1)S(1)}, u32[]{:S(2)}, u32[]{:S(2)}) collective-permute-start(bf16[512,128]{1,0:T(8,128)(2,1)S(1)} %get-tuple-element.33), channel_id=1, source_target_pairs={{0,16},{16,0},{1,17},{17,1},{2,18},{18,2},{3,19},{19,3},{4,20},{20... | collective-permute-start | bytes 393224 | tf_op jit(solution)/shard_map/ppermute | solution.py:304
  54.8 7.7 %collective-permute-start.9 = (bf16[256,1024]{1,0:T(8,128)(2,1)S(1)}, bf16[256,1024]{1,0:T(8,128)(2,1)S(1)}, u32[]{:S(2)}, u32[]{:S(2)}) collective-permute-start(bf16[256,1024]{1,0:T(8,128)(2,1)S(1)} %get-tuple-element.26), channel_id=1, source_target_pairs={{0,1},{1,0},{2,3},{3,2},{4,5},{5,4},{6,7},{7,6},{8,9},{9,8},{10,11... | collective-permute-start | bytes 1572872 | tf_op jit(solution)/shard_map/ppermute | solution.py:307
  54.8 41.5 %collective-permute-start.12 = (bf16[512,128]{1,0:T(8,128)(2,1)S(1)}, bf16[512,128]{1,0:T(8,128)(2,1)S(1)}, u32[]{:S(2)}, u32[]{:S(2)}) collective-permute-start(bf16[512,128]{1,0:T(8,128)(2,1)S(1)} %get-tuple-element.35), channel_id=1, source_target_pairs={{0,16},{16,0},{1,17},{17,1},{2,18},{18,2},{3,19},{19,3},{4,20},{20... | collective-permute-start | bytes 393224 | tf_op jit(solution)/shard_map/ppermute | solution.py:304
  58.7 37.5 %collective-permute-start.8 = (bf16[512,128]{1,0:T(8,128)(2,1)S(1)}, bf16[512,128]{1,0:T(8,128)(2,1)S(1)}, u32[]{:S(2)}, u32[]{:S(2)}) collective-permute-start(bf16[512,128]{1,0:T(8,128)(2,1)S(1)} %add_convert_fusion.2), channel_id=1, source_target_pairs={{4,0},{5,1},{6,2},{7,3},{12,8},{13,9},{14,10},{15,11},{20,16},{21,... | collective-permute-start | bytes 393224 | tf_op jit(solution)/shard_map/ppermute | solution.py:301
  61.2 35.1 %collective-permute-start.11 = (bf16[512,128]{1,0:T(8,128)(2,1)S(1)}, bf16[512,128]{1,0:T(8,128)(2,1)S(1)}, u32[]{:S(2)}, u32[]{:S(2)}) collective-permute-start(bf16[512,128]{1,0:T(8,128)(2,1)S(1)} %add_convert_fusion.1), channel_id=1, source_target_pairs={{2,0},{3,1},{4,2},{5,3},{6,4},{7,5},{10,8},{11,9},{12,10},{13,11},... | collective-permute-start | bytes 393224 | tf_op jit(solution)/shard_map/ppermute | solution.py:301
  62.5 0.8 copy-start.4
  96.4 1.3 %collective-permute-start.13 = (bf16[256,128]{1,0:T(8,128)(2,1)S(1)}, bf16[256,128]{1,0:T(8,128)(2,1)S(1)}, u32[]{:S(2)}, u32[]{:S(2)}) collective-permute-start(bf16[256,128]{1,0:T(8,128)(2,1)S(1)} %slice.17), channel_id=1, source_target_pairs={{0,1},{1,0},{2,3},{3,2},{4,5},{5,4},{6,7},{7,6},{8,9},{9,8},{10,11... | collective-permute-start | bytes 196616 | tf_op jit(solution)/shard_map/ppermute | solution.py:307

commit v4 on v3

--- a/solution.py
+++ b/solution.py
@@ -15,7 +15,7 @@
 META = 16
 DOC_ROW = NBLK
 DOC_VALUES = 16
-GROUPED = 2
+GROUPED = 4
 HALF = QUERY_PER_KEY * HEAD_SIZE
 NEG = -1e30
 F32, BF16, I32 = jnp.float32, jnp.bfloat16, jnp.int32
@@ -29,18 +29,9 @@
     return lax.rem(lax.axis_index("ctx"), 2)
 
 
-def payload_kernel(
-    swap_ref, key_ref, value_ref, docs_ref, query_ref, grad_ref, own_ref, side_ref, rows_ref, sems
-):
+def payload_kernel(swap_ref, key_ref, value_ref, docs_ref, own_ref, side_ref):
     rows = key_ref.shape[0]
     core = core_index()
-    away = pl.ds(pl.multiple_of((1 - core) * HALF, HALF), HALF)
-    copies = [
-        pltpu.make_async_copy(query_ref.at[:, away], rows_ref.at[pl.ds(0, rows), :], sems.at[0]),
-        pltpu.make_async_copy(grad_ref.at[:, away], rows_ref.at[pl.ds(rows, rows), :], sems.at[1]),
-    ]
-    for copy in copies:
-        copy.start()
     docs = jnp.broadcast_to(docs_ref[...].astype(F32), (META, rows))
     place = lax.broadcasted_iota(I32, docs.shape, 0)
     meta = jnp.where(place == DOC_ROW, docs, 0.0)
@@ -52,32 +43,30 @@
         ref[:rows, :] = key_ref[:, lane]
         ref[rows : 2 * rows, :] = value_ref[:, lane]
         ref[2 * rows :, :] = meta
+
+
+def rows_kernel(query_ref, grad_ref, rows_ref, sems):
+    rows = query_ref.shape[0]
+    away = pl.ds(pl.multiple_of((1 - core_index()) * HALF, HALF), HALF)
+    copies = [
+        pltpu.make_async_copy(
+            source.at[:, away], rows_ref.at[pl.ds(part * rows, rows), :], sems.at[part]
+        )
+        for part, source in enumerate((query_ref, grad_ref))
+    ]
+    for copy in copies:
+        copy.start()
     for copy in copies:
         copy.wait()
 
 
-def join_kernel(first_ref, second_ref, both_ref):
-    size = first_ref.shape[0]
-    both_ref[:size, :] = first_ref[...]
-    both_ref[size:, :] = second_ref[...]
-
-
-def finish_kernel(own_ref, side_ref, out_ref, query_grad_ref, sems):
+def finish_kernel(own_ref, side_ref, out_ref, query_grad_ref):
     rows = out_ref.shape[0]
     core = core_index()
-    copies = []
-    for at, (source, head) in enumerate(((own_ref, core), (side_ref, 1 - core))):
+    for source, head in ((own_ref, core), (side_ref, 1 - core)):
         lanes = pl.ds(pl.multiple_of(head * HALF, HALF), HALF)
-        for part, target in enumerate((out_ref, query_grad_ref)):
-            copies.append(
-                pltpu.make_async_copy(
-                    source.at[pl.ds(part * rows, rows), :], target.at[:, lanes], sems.at[2 * at + part]
-                )
-            )
-    for copy in copies:
-        copy.start()
-    for copy in copies:
-        copy.wait()
+        out_ref[:, lanes] = source[:rows, :]
+        query_grad_ref[:, lanes] = source[rows:, :]
 
 
 def attention_kernel(hops, query_ref, grad_ref, side_rows_ref, *refs):
@@ -306,28 +295,26 @@
     def to_side(block):
         return lax.ppermute(block, "ctx", [(i, i ^ 1) for i in range(ranks)])
 
-    payload, payload_side, rows_side = pl.pallas_call(
+    payload, payload_side = pl.pallas_call(
         payload_kernel,
-        out_shape=[
-            jax.ShapeDtypeStruct((size, HEAD_SIZE), BF16),
-            jax.ShapeDtypeStruct((size, HEAD_SIZE), BF16),
-            jax.ShapeDtypeStruct((2 * rows, HALF), BF16),
-        ],
-        in_specs=[SMEM, VMEM, VMEM, VMEM, HBM, HBM],
-        out_specs=[VMEM, VMEM, HBM],
+        out_shape=[pltpu.VMEM((size, HEAD_SIZE), BF16)] * 2,
+        in_specs=[SMEM, VMEM, VMEM, VMEM],
+        out_specs=[VMEM, VMEM],
+    )(swapped[0, 0], key_rows[0], value_rows[0], documents)
+    from_side = to_side(payload_side)
+    rows_side = pl.pallas_call(
+        rows_kernel,
+        out_shape=pltpu.VMEM((2 * rows, HALF), BF16),
+        in_specs=[HBM, HBM],
+        out_specs=VMEM,
         scratch_shapes=[pltpu.SemaphoreType.DMA((2,))],
-    )(swapped[0, 0], key_rows[0], value_rows[0], documents, queries, out_grad)
-    from_side = to_side(payload_side)
+    )(queries, out_grad)
+    both = jnp.concatenate([payload, from_side], axis=0)
+    both, rows_side = lax.optimization_barrier((both, rows_side))
     rows_got = to_side(rows_side)
-    both = pl.pallas_call(
-        join_kernel,
-        out_shape=jax.ShapeDtypeStruct((2 * size, HEAD_SIZE), BF16),
-        in_specs=[VMEM, VMEM],
-        out_specs=VMEM,
-    )(payload, from_side)
     home = [both] + [up(both, k) for k in range(1, count)]
     away = [to_partner(block) for block in home]
-    chunk = jax.ShapeDtypeStruct((4 * rows, HEAD_SIZE), BF16)
+    chunk = pltpu.VMEM((4 * rows, HEAD_SIZE), BF16)
     outs = pl.pallas_call(
         functools.partial(attention_kernel, hops),
         out_shape=[jax.ShapeDtypeStruct((2 * rows, HALF), BF16)] * 2 + [chunk] * (2 * count),
@@ -365,14 +352,18 @@
     parts = []
     for k in reversed(range(count)):
         part = home_sum[k].astype(F32) + crossed[k].astype(F32)
-        parts.append(down(part.astype(BF16), k) if k else part)
+        if k:
+            part = part.astype(BF16)
+            if k == hops:
+                part, side_out = lax.optimization_barrier((part, side_out))
+            part = down(part, k)
+        parts.append(part)
     out_got = to_side(side_out)
     out, query_grad = pl.pallas_call(
         finish_kernel,
         out_shape=[jax.ShapeDtypeStruct(queries.shape, BF16)] * 2,
-        in_specs=[pl.BlockSpec(memory_space=pl.ANY)] * 2,
-        out_specs=[HBM] * 2,
-        scratch_shapes=[pltpu.SemaphoreType.DMA((4,))],
+        in_specs=[VMEM] * 2,
+        out_specs=[VMEM] * 2,
     )(own_out, out_got)
     parts[0], out, query_grad = lax.optimization_barrier((parts[0], out, query_grad))
     total = sum(part.astype(F32) for part in parts).astype(BF16)

time: 99.8 us -> 53.2 us (0.53); the launches traced: 98.4 us -> 53.1 us
  Pallas kernels: 59.5 us -> 10.6 us
  waiting for transfers between devices: 14 us -> 19.3 us
  local copies, waits for them, and re-layouts: 3.15 us -> 1.6 us
    pallas_call x1, Pallas kernels: 32.9 us -> 2.24 us  [local(): pl.pallas_call(finish_kernel, out_shape=[jax.ShapeDtypeStruct(queries.sha...]
    pallas_call x2, Pallas kernels: 20.2 us -> 2.05 us  [the longest x1 1.13 us: local(): pl.pallas_call(rows_kernel, out_shape=pltpu.VMEM((2 * rows, HALF), BF16),...]
    ppermute x2, waiting for transfers between devices: 0.01 us -> 4.05 us  [down(): lax.ppermute(block, 'ctx', [(i + 2 * k, i) for i in range(ranks - 2 * k)])]
    ppermute x6, waiting for transfers between devices: 9.81 us -> 13.1 us  [to_partner(): return lax.ppermute(block, 'half', [(0, 1), (1, 0)])]
    ppermute x4, waiting for transfers between devices: 3.01 us -> 1.24 us  [to_side(): return lax.ppermute(block, 'ctx', [(i, i ^ 1) for i in range(ranks)])]
    unnamed x12 -> x8, local copies, waits for them, and re-layouts: 3.14 us -> 1.6 us
  transfers between devices with their start and end apart: 14 -> 14, of which waited for: 8 -> 9; matrix products, arithmetic and copies ran while one was open for 0% -> 0% of each run, Pallas kernels for 35% -> 6%
where the time goes in v4:
time: 53.2 us; the launch traced here: 53.1 us
  starting transfers between devices  20 us (38%)
  waiting for transfers between devices  19.3 us (36%)
  Pallas kernels  10.6 us (20%)
  local copies, waits for them, and re-layouts  1.6 us (3%)
  other arithmetic  0.84 us (2%)
  between operations  0.79 us (1%)
    ppermute x6, waiting for transfers between devices, to_partner(): return lax.ppermute(block, 'half', [(0, 1), (1, 0)])  13.1 us
    ppermute x2, starting transfers between devices, up(): lax.ppermute(block, 'ctx', [(i, i + 2 * k) for i in range(ranks - 2 * k)])  9.38 us
    ppermute x6, starting transfers between devices, to_partner(): return lax.ppermute(block, 'half', [(0, 1), (1, 0)])  7.22 us
    pallas_call x1, Pallas kernels, local(): pl.pallas_call(functools.partial(attention_kernel, hops), out_shape=[jax....  6.33 us
    ppermute x2, waiting for transfers between devices, down(): lax.ppermute(block, 'ctx', [(i + 2 * k, i) for i in range(ranks - 2 * k)])  4.05 us
    ppermute x2, starting transfers between devices, down(): lax.ppermute(block, 'ctx', [(i + 2 * k, i) for i in range(ranks - 2 * k)])  2.57 us
    pallas_call x1, Pallas kernels, local(): pl.pallas_call(finish_kernel, out_shape=[jax.ShapeDtypeStruct(queries.sha...  2.24 us
    unnamed x8, local copies, waits for them, and re-layouts  1.6 us
  transfers between devices with their start and end apart: 14, of which 9 were waited for; matrix products, arithmetic and copies ran while one was open for 0% of the time, Pallas kernels for 6%

profile of v4, /device:TPU:0, one launch (start us, length us, event | category | flops | bytes accessed | tf_op | source)
XLA Modules:
  0.0 53.1 jit_solution(1648984710610272835)
XLA Ops:
  0.6 0.9 %shard_map.93 = (bf16[272,128]{1,0:T(8,128)(2,1)S(1)}, bf16[272,128]{1,0:T(8,128)(2,1)S(1)}) custom-call(s32[4]{0:T(128)} %bitcast.17, bf16[128,256]{1,0:T(8,128)(2,1)} %bitcast.15, bf16[128,256]{1,0:T(8,128)(2,1)} %bitcast.16, s32[1,128]{1,0:T(1,128)} %docs_ref.1), custom_call_target="tpu_custom_call" | custom-call | tf_op jit(solution)/shard_map/pallas_call | solution.py:298
  1.6 0.5 collective-permute-start
  2.1 0.0 copy-start
  2.1 0.0 copy-start.1
  2.1 1.1 %shard_map.94 = bf16[256,1024]{1,0:T(8,128)(2,1)S(1)} custom-call(bf16[128,2048]{1,0:T(8,128)(2,1)} %bitcast.11, bf16[128,2048]{1,0:T(8,128)(2,1)} %bitcast.13), custom_call_target="tpu_custom_call" | custom-call | tf_op jit(solution)/shard_map/pallas_call | solution.py:305
  3.2 0.0 collective-permute-done
  3.3 0.2 collective-permute-start.1
  3.4 4.9 %collective-permute-start.2 = (bf16[544,128]{1,0:T(8,128)(2,1)S(1)}, bf16[544,128]{1,0:T(8,128)(2,1)S(1)}, u32[]{:S(2)}, u32[]{:S(2)}) collective-permute-start(bf16[544,128]{1,0:T(8,128)(2,1)S(1)} %pad_maximum_fusion.refs_0_), channel_id=1, source_target_pairs={{0,2},{1,3},{2,4},{3,5},{4,6},{5,7},{8,10},{9,11},{10,12},{11,13},... | collective-permute-start | bytes 417800 | tf_op jit(solution)/shard_map/ppermute | solution.py:287
  8.3 4.5 %collective-permute-start.3 = (bf16[544,128]{1,0:T(8,128)(2,1)S(1)}, bf16[544,128]{1,0:T(8,128)(2,1)S(1)}, u32[]{:S(2)}, u32[]{:S(2)}) collective-permute-start(bf16[544,128]{1,0:T(8,128)(2,1)S(1)} %pad_maximum_fusion.refs_0_), channel_id=1, source_target_pairs={{0,4},{1,5},{2,6},{3,7},{8,12},{9,13},{10,14},{11,15},{16,20},{17,... | collective-permute-start | bytes 417800 | tf_op jit(solution)/shard_map/ppermute | solution.py:287
  12.8 1.6 %collective-permute-start.4 = (bf16[544,128]{1,0:T(8,128)(2,1)S(1)}, bf16[544,128]{1,0:T(8,128)(2,1)S(1)}, u32[]{:S(2)}, u32[]{:S(2)}) collective-permute-start(bf16[544,128]{1,0:T(8,128)(2,1)S(1)} %pad_maximum_fusion.refs_0_), channel_id=1, source_target_pairs={{0,16},{16,0},{1,17},{17,1},{2,18},{18,2},{3,19},{19,3},{4,20},{20... | collective-permute-start | bytes 417800 | tf_op jit(solution)/shard_map/ppermute | solution.py:293
  14.4 0.0 collective-permute-done.2.refs_1_
  14.4 0.5 collective-permute-start.5
  14.9 0.8 %collective-permute-done.3.refs_2_ = bf16[544,128]{1,0:T(8,128)(2,1)S(1)} collective-permute-done((bf16[544,128]{1,0:T(8,128)(2,1)S(1)}, bf16[544,128]{1,0:T(8,128)(2,1)S(1)}, u32[]{:S(2)}, u32[]{:S(2)}) %collective-permute-start.3) | collective-permute-done | bytes 139296 | tf_op jit(solution)/shard_map/ppermute | solution.py:287
  15.7 1.5 %collective-permute-start.6 = (bf16[544,128]{1,0:T(8,128)(2,1)S(1)}, bf16[544,128]{1,0:T(8,128)(2,1)S(1)}, u32[]{:S(2)}, u32[]{:S(2)}) collective-permute-start(bf16[544,128]{1,0:T(8,128)(2,1)S(1)} %collective-permute-done.3.refs_2_), channel_id=1, source_target_pairs={{0,16},{16,0},{1,17},{17,1},{2,18},{18,2},{3,19},{19,3},{4,20},{20... | collective-permute-start | bytes 417800 | tf_op jit(solution)/shard_map/ppermute | solution.py:293
  17.3 2.2 %collective-permute-done.4.refs_3_ = bf16[544,128]{1,0:T(8,128)(2,1)S(1)} collective-permute-done((bf16[544,128]{1,0:T(8,128)(2,1)S(1)}, bf16[544,128]{1,0:T(8,128)(2,1)S(1)}, u32[]{:S(2)}, u32[]{:S(2)}) %collective-permute-start.4) | collective-permute-done | bytes 139296 | tf_op jit(solution)/shard_map/ppermute | solution.py:293
  19.5 3.0 %collective-permute-done.5.refs_4_ = bf16[544,128]{1,0:T(8,128)(2,1)S(1)} collective-permute-done((bf16[544,128]{1,0:T(8,128)(2,1)S(1)}, bf16[544,128]{1,0:T(8,128)(2,1)S(1)}, u32[]{:S(2)}, u32[]{:S(2)}) %collective-permute-start.5) | collective-permute-done | bytes 139296 | tf_op jit(solution)/shard_map/ppermute | solution.py:293
  22.5 1.5 %collective-permute-done.6.refs_5_ = bf16[544,128]{1,0:T(8,128)(2,1)S(1)} collective-permute-done((bf16[544,128]{1,0:T(8,128)(2,1)S(1)}, bf16[544,128]{1,0:T(8,128)(2,1)S(1)}, u32[]{:S(2)}, u32[]{:S(2)}) %collective-permute-start.6) | collective-permute-done | bytes 139296 | tf_op jit(solution)/shard_map/ppermute | solution.py:293
  24.0 0.0 collective-permute-done.1.side_rows_ref
  24.0 0.0 copy-done
  24.0 0.0 copy-done.1
  24.0 6.3 %shard_map.95 = (bf16[256,1024]{1,0:T(8,128)(2,1)S(1)}, bf16[256,1024]{1,0:T(8,128)(2,1)S(1)}, bf16[512,128]{1,0:T(8,128)(2,1)S(1)}, bf16[512,128]{1,0:T(8,128)(...) custom-call(bf16[128,2048]{1,0:T(8,128)(2,1)S(1)} %bitcast.12, ...), custom_call_target="tpu_custom_call" | custom-call | flops 2415919104 | bytes 4194304 | tf_op jit(solution)/shard_map/pallas_call | solution.py:318
  30.3 0.0 copy-start.2
  30.3 0.8 %copy-done.2 = bf16[256,1024]{1,0:T(8,128)(2,1)} copy-done((bf16[256,1024]{1,0:T(8,128)(2,1)}, bf16[256,1024]{1,0:T(8,128)(2,1)S(1)}, u32[]{:S(2)}) %copy-start.2) | copy-done | bytes 524312
  31.1 1.5 %collective-permute-start.7 = (bf16[512,128]{1,0:T(8,128)(2,1)S(1)}, bf16[512,128]{1,0:T(8,128)(2,1)S(1)}, u32[]{:S(2)}, u32[]{:S(2)}) collective-permute-start(bf16[512,128]{1,0:T(8,128)(2,1)S(1)} %get-tuple-element.28), channel_id=1, source_target_pairs={{0,16},{16,0},{1,17},{17,1},{2,18},{18,2},{3,19},{19,3},{4,20},{20... | collective-permute-start | bytes 393224 | tf_op jit(solution)/shard_map/ppermute | solution.py:293
  32.6 3.4 %collective-permute-done.7 = bf16[512,128]{1,0:T(8,128)(2,1)S(1)} collective-permute-done((bf16[512,128]{1,0:T(8,128)(2,1)S(1)}, bf16[512,128]{1,0:T(8,128)(2,1)S(1)}, u32[]{:S(2)}, u32[]{:S(2)}) %collective-permute-start.7) | collective-permute-done | bytes 131104 | tf_op jit(solution)/shard_map/ppermute | solution.py:293
  36.1 0.1 collective-permute-start.9
  36.2 1.6 %collective-permute-start.10 = (bf16[512,128]{1,0:T(8,128)(2,1)S(1)}, bf16[512,128]{1,0:T(8,128)(2,1)S(1)}, u32[]{:S(2)}, u32[]{:S(2)}) collective-permute-start(bf16[512,128]{1,0:T(8,128)(2,1)S(1)} %get-tuple-element.39), channel_id=1, source_target_pairs={{0,16},{16,0},{1,17},{17,1},{2,18},{18,2},{3,19},{19,3},{4,20},{20... | collective-permute-start | bytes 393224 | tf_op jit(solution)/shard_map/ppermute | solution.py:293
  37.8 0.5 collective-permute-start.12
  38.3 1.3 %collective-permute-start.8 = (bf16[512,128]{1,0:T(8,128)(2,1)S(1)}, bf16[512,128]{1,0:T(8,128)(2,1)S(1)}, u32[]{:S(2)}, u32[]{:S(2)}) collective-permute-start(bf16[512,128]{1,0:T(8,128)(2,1)S(1)} %add_convert_fusion.2), channel_id=1, source_target_pairs={{4,0},{5,1},{6,2},{7,3},{12,8},{13,9},{14,10},{15,11},{20,16},{21,... | collective-permute-start | bytes 393224 | tf_op jit(solution)/shard_map/ppermute | solution.py:290
  39.6 3.0 %collective-permute-done.10 = bf16[512,128]{1,0:T(8,128)(2,1)S(1)} collective-permute-done((bf16[512,128]{1,0:T(8,128)(2,1)S(1)}, bf16[512,128]{1,0:T(8,128)(2,1)S(1)}, u32[]{:S(2)}, u32[]{:S(2)}) %collective-permute-start.10) | collective-permute-done | bytes 131104 | tf_op jit(solution)/shard_map/ppermute | solution.py:293
  42.6 1.3 %collective-permute-start.11 = (bf16[512,128]{1,0:T(8,128)(2,1)S(1)}, bf16[512,128]{1,0:T(8,128)(2,1)S(1)}, u32[]{:S(2)}, u32[]{:S(2)}) collective-permute-start(bf16[512,128]{1,0:T(8,128)(2,1)S(1)} %add_convert_fusion.1), channel_id=1, source_target_pairs={{2,0},{3,1},{4,2},{5,3},{6,4},{7,5},{10,8},{11,9},{12,10},{13,11},... | collective-permute-start | bytes 393224 | tf_op jit(solution)/shard_map/ppermute | solution.py:290
  43.9 0.0 collective-permute-done.9.side_ref
  43.9 0.0 copy-start.3
  43.9 0.8 %copy-done.3 = bf16[256,1024]{1,0:T(8,128)(2,1)} copy-done((bf16[256,1024]{1,0:T(8,128)(2,1)}, bf16[256,1024]{1,0:T(8,128)(2,1)S(1)}, u32[]{:S(2)}) %copy-start.3) | copy-done | bytes 524312
  44.7 2.2 %shard_map.96 = (bf16[128,2048]{1,0:T(8,128)(2,1)}, bf16[128,2048]{1,0:T(8,128)(2,1)}) custom-call(bf16[256,1024]{1,0:T(8,128)(2,1)} %copy-done.2, bf16[256,1024]{1,0:T(8,128)(2,1)} %copy-done.3), custom_call_target="tpu_custom_call" | custom-call | tf_op jit(solution)/shard_map/pallas_call | solution.py:362
  47.0 3.2 %collective-permute-done.8 = bf16[512,128]{1,0:T(8,128)(2,1)S(1)} collective-permute-done((bf16[512,128]{1,0:T(8,128)(2,1)S(1)}, bf16[512,128]{1,0:T(8,128)(2,1)S(1)}, u32[]{:S(2)}, u32[]{:S(2)}) %collective-permute-start.8) | collective-permute-done | bytes 131104 | tf_op jit(solution)/shard_map/ppermute | solution.py:290
  50.2 0.0 collective-permute-done.12
  50.2 0.8 %collective-permute-done.11 = bf16[512,128]{1,0:T(8,128)(2,1)S(1)} collective-permute-done((bf16[512,128]{1,0:T(8,128)(2,1)S(1)}, bf16[512,128]{1,0:T(8,128)(2,1)S(1)}, u32[]{:S(2)}, u32[]{:S(2)}) %collective-permute-start.11) | collective-permute-done | bytes 131104 | tf_op jit(solution)/shard_map/ppermute | solution.py:290
  51.0 0.1 add_convert_fusion
  51.1 0.1 collective-permute-start.13
  51.2 1.2 %collective-permute-done.13 = bf16[256,128]{1,0:T(8,128)(2,1)S(1)} collective-permute-done((bf16[256,128]{1,0:T(8,128)(2,1)S(1)}, bf16[256,128]{1,0:T(8,128)(2,1)S(1)}, u32[]{:S(2)}, u32[]{:S(2)}) %collective-permute-start.13) | collective-permute-done | bytes 65568 | tf_op jit(solution)/shard_map/ppermute | solution.py:296
  52.4 0.7 %fusion.2 = (bf16[1,128,256]{2,1,0:T(8,128)(2,1)}, bf16[1,128,256]{2,1,0:T(8,128)(2,1)}) fusion(bf16[256,128]{1,0:T(8,128)(2,1)S(1)} %get-tuple-element.42, bf16[256,128]{1,0:T(8,128)(2,1)S(1)} %get-tuple-element.43), kind=kLoop, calls=%fused_computation.9 | loop fusion | flops 262144 | bytes 262144 | tf_op jit(solution)/shard_map/broadcast_in_dim | solution.py:376
  (5 shorter events, 0.1 us)
Async XLA Ops:
  1.6 1.7 %collective-permute-start = (bf16[272,128]{1,0:T(8,128)(2,1)S(1)}, bf16[272,128]{1,0:T(8,128)(2,1)S(1)}, u32[]{:S(2)}, u32[]{:S(2)}) collective-permute-start(bf16[272,128]{1,0:T(8,128)(2,1)S(1)} %get-tuple-element.24), channel_id=1, source_target_pairs={{0,1},{1,0},{2,3},{3,2},{4,5},{5,4},{6,7},{7,6},{8,9},{9,8},{10,11... | collective-permute-start | bytes 208904 | tf_op jit(solution)/shard_map/ppermute | solution.py:296
  2.1 21.9 %copy-start = (bf16[1,128,2048]{2,1,0:T(8,128)(2,1)S(1)}, bf16[1,128,2048]{2,1,0:T(8,128)(2,1)}, u32[]{:S(2)}) copy-start(bf16[1,128,2048]{2,1,0:T(8,128)(2,1)} %param.6) | copy-start | bytes 1572868
  2.1 21.9 %copy-start.1 = (bf16[1,128,2048]{2,1,0:T(8,128)(2,1)S(1)}, bf16[1,128,2048]{2,1,0:T(8,128)(2,1)}, u32[]{:S(2)}) copy-start(bf16[1,128,2048]{2,1,0:T(8,128)(2,1)} %param.9) | copy-start | bytes 1572868
  3.3 20.7 %collective-permute-start.1 = (bf16[256,1024]{1,0:T(8,128)(2,1)S(1)}, bf16[256,1024]{1,0:T(8,128)(2,1)S(1)}, u32[]{:S(2)}, u32[]{:S(2)}) collective-permute-start(bf16[256,1024]{1,0:T(8,128)(2,1)S(1)} %shard_map.94), channel_id=1, source_target_pairs={{0,1},{1,0},{2,3},{3,2},{4,5},{5,4},{6,7},{7,6},{8,9},{9,8},{10,11... | collective-permute-start | bytes 1572872 | tf_op jit(solution)/shard_map/ppermute | solution.py:296
  3.4 11.0 %collective-permute-start.2 = (bf16[544,128]{1,0:T(8,128)(2,1)S(1)}, bf16[544,128]{1,0:T(8,128)(2,1)S(1)}, u32[]{:S(2)}, u32[]{:S(2)}) collective-permute-start(bf16[544,128]{1,0:T(8,128)(2,1)S(1)} %pad_maximum_fusion.refs_0_), channel_id=1, source_target_pairs={{0,2},{1,3},{2,4},{3,5},{4,6},{5,7},{8,10},{9,11},{10,12},{11,13},... | collective-permute-start | bytes 417800 | tf_op jit(solution)/shard_map/ppermute | solution.py:287
  8.3 7.4 %collective-permute-start.3 = (bf16[544,128]{1,0:T(8,128)(2,1)S(1)}, bf16[544,128]{1,0:T(8,128)(2,1)S(1)}, u32[]{:S(2)}, u32[]{:S(2)}) collective-permute-start(bf16[544,128]{1,0:T(8,128)(2,1)S(1)} %pad_maximum_fusion.refs_0_), channel_id=1, source_target_pairs={{0,4},{1,5},{2,6},{3,7},{8,12},{9,13},{10,14},{11,15},{16,20},{17,... | collective-permute-start | bytes 417800 | tf_op jit(solution)/shard_map/ppermute | solution.py:287
  12.8 6.7 %collective-permute-start.4 = (bf16[544,128]{1,0:T(8,128)(2,1)S(1)}, bf16[544,128]{1,0:T(8,128)(2,1)S(1)}, u32[]{:S(2)}, u32[]{:S(2)}) collective-permute-start(bf16[544,128]{1,0:T(8,128)(2,1)S(1)} %pad_maximum_fusion.refs_0_), channel_id=1, source_target_pairs={{0,16},{16,0},{1,17},{17,1},{2,18},{18,2},{3,19},{19,3},{4,20},{20... | collective-permute-start | bytes 417800 | tf_op jit(solution)/shard_map/ppermute | solution.py:293
  14.4 8.1 %collective-permute-start.5 = (bf16[544,128]{1,0:T(8,128)(2,1)S(1)}, bf16[544,128]{1,0:T(8,128)(2,1)S(1)}, u32[]{:S(2)}, u32[]{:S(2)}) collective-permute-start(bf16[544,128]{1,0:T(8,128)(2,1)S(1)} %collective-permute-done.2.refs_1_), channel_id=1, source_target_pairs={{0,16},{16,0},{1,17},{17,1},{2,18},{18,2},{3,19},{19,3},{4,20},{20... | collective-permute-start | bytes 417800 | tf_op jit(solution)/shard_map/ppermute | solution.py:293
  15.7 8.2 %collective-permute-start.6 = (bf16[544,128]{1,0:T(8,128)(2,1)S(1)}, bf16[544,128]{1,0:T(8,128)(2,1)S(1)}, u32[]{:S(2)}, u32[]{:S(2)}) collective-permute-start(bf16[544,128]{1,0:T(8,128)(2,1)S(1)} %collective-permute-done.3.refs_2_), channel_id=1, source_target_pairs={{0,16},{16,0},{1,17},{17,1},{2,18},{18,2},{3,19},{19,3},{4,20},{20... | collective-permute-start | bytes 417800 | tf_op jit(solution)/shard_map/ppermute | solution.py:293
  30.3 0.8 %copy-start.2 = (bf16[256,1024]{1,0:T(8,128)(2,1)}, bf16[256,1024]{1,0:T(8,128)(2,1)S(1)}, u32[]{:S(2)}) copy-start(bf16[256,1024]{1,0:T(8,128)(2,1)S(1)} %get-tuple-element.31.own_ref) | copy-start | bytes 1572868
  31.1 5.0 %collective-permute-start.7 = (bf16[512,128]{1,0:T(8,128)(2,1)S(1)}, bf16[512,128]{1,0:T(8,128)(2,1)S(1)}, u32[]{:S(2)}, u32[]{:S(2)}) collective-permute-start(bf16[512,128]{1,0:T(8,128)(2,1)S(1)} %get-tuple-element.28), channel_id=1, source_target_pairs={{0,16},{16,0},{1,17},{17,1},{2,18},{18,2},{3,19},{19,3},{4,20},{20... | collective-permute-start | bytes 393224 | tf_op jit(solution)/shard_map/ppermute | solution.py:293
  36.1 7.8 %collective-permute-start.9 = (bf16[256,1024]{1,0:T(8,128)(2,1)S(1)}, bf16[256,1024]{1,0:T(8,128)(2,1)S(1)}, u32[]{:S(2)}, u32[]{:S(2)}) collective-permute-start(bf16[256,1024]{1,0:T(8,128)(2,1)S(1)} %get-tuple-element.32), channel_id=1, source_target_pairs={{0,1},{1,0},{2,3},{3,2},{4,5},{5,4},{6,7},{7,6},{8,9},{9,8},{10,11... | collective-permute-start | bytes 1572872 | tf_op jit(solution)/shard_map/ppermute | solution.py:296
  36.2 6.4 %collective-permute-start.10 = (bf16[512,128]{1,0:T(8,128)(2,1)S(1)}, bf16[512,128]{1,0:T(8,128)(2,1)S(1)}, u32[]{:S(2)}, u32[]{:S(2)}) collective-permute-start(bf16[512,128]{1,0:T(8,128)(2,1)S(1)} %get-tuple-element.39), channel_id=1, source_target_pairs={{0,16},{16,0},{1,17},{17,1},{2,18},{18,2},{3,19},{19,3},{4,20},{20... | collective-permute-start | bytes 393224 | tf_op jit(solution)/shard_map/ppermute | solution.py:293
  37.8 12.4 %collective-permute-start.12 = (bf16[512,128]{1,0:T(8,128)(2,1)S(1)}, bf16[512,128]{1,0:T(8,128)(2,1)S(1)}, u32[]{:S(2)}, u32[]{:S(2)}) collective-permute-start(bf16[512,128]{1,0:T(8,128)(2,1)S(1)} %get-tuple-element.41), channel_id=1, source_target_pairs={{0,16},{16,0},{1,17},{17,1},{2,18},{18,2},{3,19},{19,3},{4,20},{20... | collective-permute-start | bytes 393224 | tf_op jit(solution)/shard_map/ppermute | solution.py:293
  38.3 11.9 %collective-permute-start.8 = (bf16[512,128]{1,0:T(8,128)(2,1)S(1)}, bf16[512,128]{1,0:T(8,128)(2,1)S(1)}, u32[]{:S(2)}, u32[]{:S(2)}) collective-permute-start(bf16[512,128]{1,0:T(8,128)(2,1)S(1)} %add_convert_fusion.2), channel_id=1, source_target_pairs={{4,0},{5,1},{6,2},{7,3},{12,8},{13,9},{14,10},{15,11},{20,16},{21,... | collective-permute-start | bytes 393224 | tf_op jit(solution)/shard_map/ppermute | solution.py:290
  42.6 8.4 %collective-permute-start.11 = (bf16[512,128]{1,0:T(8,128)(2,1)S(1)}, bf16[512,128]{1,0:T(8,128)(2,1)S(1)}, u32[]{:S(2)}, u32[]{:S(2)}) collective-permute-start(bf16[512,128]{1,0:T(8,128)(2,1)S(1)} %add_convert_fusion.1), channel_id=1, source_target_pairs={{2,0},{3,1},{4,2},{5,3},{6,4},{7,5},{10,8},{11,9},{12,10},{13,11},... | collective-permute-start | bytes 393224 | tf_op jit(solution)/shard_map/ppermute | solution.py:290
  43.9 0.8 %copy-start.3 = (bf16[256,1024]{1,0:T(8,128)(2,1)}, bf16[256,1024]{1,0:T(8,128)(2,1)S(1)}, u32[]{:S(2)}) copy-start(bf16[256,1024]{1,0:T(8,128)(2,1)S(1)} %collective-permute-done.9.side_ref) | copy-start | bytes 1572868
  51.1 1.3 %collective-permute-start.13 = (bf16[256,128]{1,0:T(8,128)(2,1)S(1)}, bf16[256,128]{1,0:T(8,128)(2,1)S(1)}, u32[]{:S(2)}, u32[]{:S(2)}) collective-permute-start(bf16[256,128]{1,0:T(8,128)(2,1)S(1)} %slice.17), channel_id=1, source_target_pairs={{0,1},{1,0},{2,3},{3,2},{4,5},{5,4},{6,7},{7,6},{8,9},{9,8},{10,11... | collective-permute-start | bytes 196616 | tf_op jit(solution)/shard_map/ppermute | solution.py:296

commit v5 on v4

--- a/solution.py
+++ b/solution.py
@@ -60,13 +60,19 @@
         copy.wait()
 
 
-def finish_kernel(own_ref, side_ref, out_ref, query_grad_ref):
+def finish_kernel(side_ref, out_held, query_grad_held, out_ref, query_grad_ref, sems):
     rows = out_ref.shape[0]
-    core = core_index()
-    for source, head in ((own_ref, core), (side_ref, 1 - core)):
-        lanes = pl.ds(pl.multiple_of(head * HALF, HALF), HALF)
-        out_ref[:, lanes] = source[:rows, :]
-        query_grad_ref[:, lanes] = source[rows:, :]
+    away = pl.ds(pl.multiple_of((1 - core_index()) * HALF, HALF), HALF)
+    copies = [
+        pltpu.make_async_copy(
+            side_ref.at[pl.ds(part * rows, rows), :], target.at[:, away], sems.at[part]
+        )
+        for part, target in enumerate((out_ref, query_grad_ref))
+    ]
+    for copy in copies:
+        copy.start()
+    for copy in copies:
+        copy.wait()
 
 
 def attention_kernel(hops, query_ref, grad_ref, side_rows_ref, *refs):
@@ -74,9 +80,9 @@
     slots = 2 * count
     window = slots - 1
     homes, aways = refs[:count], refs[count : 2 * count]
-    own_out_ref, side_out_ref = refs[2 * count : 2 * count + 2]
-    home_outs = refs[2 * count + 2 : 3 * count + 2]
-    away_outs = refs[3 * count + 2 : 4 * count + 2]
+    out_ref, query_grad_ref, side_out_ref = refs[2 * count : 2 * count + 3]
+    home_outs = refs[2 * count + 3 : 3 * count + 3]
+    away_outs = refs[3 * count + 3 : 4 * count + 3]
     (
         query_all,
         grad_all,
@@ -87,12 +93,13 @@
         value_turned,
         doc_window,
         starts,
+        flag_rows,
         key_total,
         value_total,
         logical_of,
         needed_of,
         sems,
-    ) = refs[4 * count + 2 :]
+    ) = refs[4 * count + 3 :]
     rows = query_ref.shape[0]
     per_block = rows // NBLK
     lanes = QUERY_PER_KEY * per_block
@@ -165,12 +172,20 @@
                 tiled = jnp.broadcast_to(tiled[:1], lower.shape)
                 start = jnp.sum(jnp.where(tiled == values_down, lower, 0.0), axis=0, keepdims=True)
                 starts[logical, who * NBLK + block : who * NBLK + block + 1, :] = start.astype(I32)
+    for who in range(2):
+        flag_rows[who * NBLK : (who + 1) * NBLK, :] = meta_rows[who][:NBLK, :]
+    flags = flag_rows[...]
+    firsts = [
+        jnp.broadcast_to(
+            jnp.min(starts[logical].astype(F32), axis=1, keepdims=True), flags.shape
+        )
+        for logical in range(2)
+    ]
+    first = jnp.where(flags > 0.5, firsts[1], firsts[0]).astype(I32)
+    flags = flags.astype(I32)
     for unit_index in range(2 * NBLK):
-        who, block = unit_index // NBLK, unit_index % NBLK
-        flag = jnp.max(meta_rows[who][block : block + 1, :]).astype(I32)
-        logical_of[unit_index] = flag
-        first = jnp.min(starts[flag, unit_index : unit_index + 1, :].astype(F32)).astype(I32)
-        needed_of[unit_index] = window + parity[who] - first // rows
+        logical_of[unit_index] = flags[unit_index, 0]
+        needed_of[unit_index] = window + parity[unit_index // NBLK] - first[unit_index, 0] // rows
     for copy in copies:
         copy.wait()
 
@@ -247,11 +262,10 @@
 
     lax.fori_loop(0, 2 * NBLK // GROUPED, step, 0)
     copies = [
-        pltpu.make_async_copy(
-            out_all.at[who, which], target.at[pl.ds(which * rows, rows), :], sems.at[2 * who + which]
-        )
-        for who, target in enumerate((own_out_ref, side_out_ref))
-        for which in range(2)
+        pltpu.make_async_copy(out_all.at[1, 0], side_out_ref.at[pl.ds(0, rows), :], sems.at[0]),
+        pltpu.make_async_copy(out_all.at[1, 1], side_out_ref.at[pl.ds(rows, rows), :], sems.at[1]),
+        pltpu.make_async_copy(out_all.at[0, 0], out_ref.at[:, mine], sems.at[2]),
+        pltpu.make_async_copy(out_all.at[0, 1], query_grad_ref.at[:, mine], sems.at[3]),
     ]
     for copy in copies:
         copy.start()
@@ -283,11 +297,11 @@
     size = 2 * rows + META
     queries, out_grad = queries[0], out_grad[0]
 
-    def up(block, k):
-        return lax.ppermute(block, "ctx", [(i, i + 2 * k) for i in range(ranks - 2 * k)])
-
-    def down(block, k):
-        return lax.ppermute(block, "ctx", [(i + 2 * k, i) for i in range(ranks - 2 * k)])
+    def up(block):
+        return lax.ppermute(block, "ctx", [(i, i + 2) for i in range(ranks - 2)])
+
+    def down(block):
+        return lax.ppermute(block, "ctx", [(i + 2, i) for i in range(ranks - 2)])
 
     def to_partner(block):
         return lax.ppermute(block, "half", [(0, 1), (1, 0)])
@@ -312,14 +326,18 @@
     both = jnp.concatenate([payload, from_side], axis=0)
     both, rows_side = lax.optimization_barrier((both, rows_side))
     rows_got = to_side(rows_side)
-    home = [both] + [up(both, k) for k in range(1, count)]
+    home = [both]
+    for _ in range(hops):
+        home.append(up(home[-1]))
     away = [to_partner(block) for block in home]
     chunk = pltpu.VMEM((4 * rows, HEAD_SIZE), BF16)
     outs = pl.pallas_call(
         functools.partial(attention_kernel, hops),
-        out_shape=[jax.ShapeDtypeStruct((2 * rows, HALF), BF16)] * 2 + [chunk] * (2 * count),
+        out_shape=[jax.ShapeDtypeStruct(queries.shape, BF16)] * 2
+        + [pltpu.VMEM((2 * rows, HALF), BF16)]
+        + [chunk] * (2 * count),
         in_specs=[HBM, HBM, pl.BlockSpec(memory_space=pl.ANY)] + [VMEM] * (2 * count),
-        out_specs=[HBM] * 2 + [VMEM] * (2 * count),
+        out_specs=[HBM] * 2 + [VMEM] * (1 + 2 * count),
         scratch_shapes=[
             pltpu.VMEM((2, rows, HALF), BF16),
             pltpu.VMEM((2, rows, HALF), BF16),
@@ -330,6 +348,7 @@
             pltpu.VMEM((2, HEAD_SIZE, keys), BF16),
             pltpu.VMEM((2, 16, rows), F32),
             pltpu.VMEM((2, 8, rows), I32),
+            pltpu.VMEM((8, rows), F32),
             pltpu.VMEM((2, keys, HEAD_SIZE), F32),
             pltpu.VMEM((2, keys, HEAD_SIZE), F32),
             pltpu.SMEM((2 * NBLK,), I32),
@@ -343,30 +362,32 @@
             transcendentals=rows * keys * 16,
         ),
     )(queries, out_grad, rows_got, *home, *away)
-    own_out, side_out = outs[:2]
-    home_sum, away_sum = outs[2 : 2 + count], outs[2 + count :]
-
-    crossed = [None] * count
+    out, query_grad, side_out = outs[:3]
+    home_sum, away_sum = outs[3 : 3 + count], list(outs[3 + count :])
+
+    total = None
     for k in reversed(range(count)):
-        crossed[k] = to_partner(away_sum[k])
-    parts = []
-    for k in reversed(range(count)):
-        part = home_sum[k].astype(F32) + crossed[k].astype(F32)
+        part = home_sum[k].astype(F32) + to_partner(away_sum[k]).astype(F32)
+        if total is not None:
+            part = part + total.astype(F32)
+        total = part.astype(BF16)
+        if k == hops:
+            total, side_out, *away_sum[:k] = lax.optimization_barrier(
+                (total, side_out, *away_sum[:k])
+            )
+            out_got = to_side(side_out)
         if k:
-            part = part.astype(BF16)
-            if k == hops:
-                part, side_out = lax.optimization_barrier((part, side_out))
-            part = down(part, k)
-        parts.append(part)
-    out_got = to_side(side_out)
-    out, query_grad = pl.pallas_call(
-        finish_kernel,
-        out_shape=[jax.ShapeDtypeStruct(queries.shape, BF16)] * 2,
-        in_specs=[VMEM] * 2,
-        out_specs=[VMEM] * 2,
-    )(own_out, out_got)
-    parts[0], out, query_grad = lax.optimization_barrier((parts[0], out, query_grad))
-    total = sum(part.astype(F32) for part in parts).astype(BF16)
+            total = down(total)
+        if k == 1:
+            out, query_grad = pl.pallas_call(
+                finish_kernel,
+                out_shape=[jax.ShapeDtypeStruct(queries.shape, BF16)] * 2,
+                in_specs=[VMEM, HBM, HBM],
+                out_specs=[HBM] * 2,
+                input_output_aliases={1: 0, 2: 1},
+                scratch_shapes=[pltpu.SemaphoreType.DMA((2,))],
+            )(out_got, out, query_grad)
+            total, out, query_grad = lax.optimization_barrier((total, out, query_grad))
     grads_got = to_side(total[2 * rows :])
     grads = total[: 2 * rows]
     first = core_index() == 0

time: 53.2 us -> 59.1 us (1.11); the launches traced: 53.1 us -> 58.2 us
  waiting for transfers between devices: 19.3 us -> 24.4 us
  starting transfers between devices: 20 us -> 21.2 us
  local copies, waits for them, and re-layouts: 1.6 us -> 0.82 us
    ppermute x4, waiting for transfers between devices: 4.89 us -> 10.2 us  [the longest x2 6.53 us: down(): return lax.ppermute(block, 'ctx', [(i + 2, i) for i in range(ranks - 2)])]
    ppermute x6, starting transfers between devices: 7.22 us -> 8.51 us  [to_partner(): return lax.ppermute(block, 'half', [(0, 1), (1, 0)])]
    unnamed x8 -> x6, local copies, waits for them, and re-layouts: 1.6 us -> 0.81 us
  transfers between devices with their start and end apart: 14 -> 14, of which waited for: 9 -> 10; matrix products, arithmetic and copies ran while one was open for 0% -> 0% of each run, Pallas kernels for 6% -> 5%
where the time goes in v5:
time: 59.1 us; the launch traced here: 58.2 us
  waiting for transfers between devices  24.4 us (41%)
  starting transfers between devices  21.2 us (36%)
  Pallas kernels  10.2 us (17%)
  other arithmetic  0.84 us (1%)
  local copies, waits for them, and re-layouts  0.82 us (1%)
  between operations  0.77 us (1%)
    ppermute x6, waiting for transfers between devices, to_partner(): return lax.ppermute(block, 'half', [(0, 1), (1, 0)])  13 us
    ppermute x2, starting transfers between devices, up(): return lax.ppermute(block, 'ctx', [(i, i + 2) for i in range(ranks - 2)])  9.26 us
    ppermute x6, starting transfers between devices, to_partner(): return lax.ppermute(block, 'half', [(0, 1), (1, 0)])  8.51 us
    ppermute x2, waiting for transfers between devices, down(): return lax.ppermute(block, 'ctx', [(i + 2, i) for i in range(ranks - 2)])  6.53 us
    pallas_call x1, Pallas kernels, local(): pl.pallas_call(functools.partial(attention_kernel, hops), out_shape=[jax....  6.31 us
    ppermute x2, waiting for transfers between devices, up(): return lax.ppermute(block, 'ctx', [(i, i + 2) for i in range(ranks - 2)])  3.65 us
    ppermute x2, starting transfers between devices, down(): return lax.ppermute(block, 'ctx', [(i + 2, i) for i in range(ranks - 2)])  2.57 us
    pallas_call x1, Pallas kernels, local(): pl.pallas_call(finish_kernel, out_shape=[jax.ShapeDtypeStruct(queries.sha...  1.85 us
  transfers between devices with their start and end apart: 14, of which 10 were waited for; matrix products, arithmetic and copies ran while one was open for 0% of the time, Pallas kernels for 5%

profile of v5, /device:TPU:0, one launch (start us, length us, event | category | flops | bytes accessed | tf_op | source)
XLA Modules:
  0.0 58.2 jit_solution(3568932795149493611)
XLA Ops:
  0.6 0.9 %shard_map.93 = (bf16[272,128]{1,0:T(8,128)(2,1)S(1)}, bf16[272,128]{1,0:T(8,128)(2,1)S(1)}) custom-call(s32[4]{0:T(128)} %bitcast.19, bf16[128,256]{1,0:T(8,128)(2,1)} %bitcast.17, bf16[128,256]{1,0:T(8,128)(2,1)} %bitcast.18, s32[1,128]{1,0:T(1,128)} %docs_ref.1), custom_call_target="tpu_custom_call" | custom-call | tf_op jit(solution)/shard_map/pallas_call | solution.py:312
  1.6 0.5 collective-permute-start
  2.1 0.0 copy-start
  2.1 0.0 copy-start.1
  2.1 1.1 %shard_map.94 = bf16[256,1024]{1,0:T(8,128)(2,1)S(1)} custom-call(bf16[128,2048]{1,0:T(8,128)(2,1)} %bitcast.11, bf16[128,2048]{1,0:T(8,128)(2,1)} %bitcast.13), custom_call_target="tpu_custom_call" | custom-call | tf_op jit(solution)/shard_map/pallas_call | solution.py:319
  3.2 0.0 collective-permute-done
  3.3 0.2 collective-permute-start.1
  3.4 4.9 %collective-permute-start.2 = (bf16[544,128]{1,0:T(8,128)(2,1)S(1)}, bf16[544,128]{1,0:T(8,128)(2,1)S(1)}, u32[]{:S(2)}, u32[]{:S(2)}) collective-permute-start(bf16[544,128]{1,0:T(8,128)(2,1)S(1)} %pad_maximum_fusion.refs_0_), channel_id=1, source_target_pairs={{0,2},{1,3},{2,4},{3,5},{4,6},{5,7},{8,10},{9,11},{10,12},{11,13},... | collective-permute-start | bytes 417800 | tf_op jit(solution)/shard_map/ppermute | solution.py:301
  8.3 3.2 %collective-permute-done.2.refs_1_ = bf16[544,128]{1,0:T(8,128)(2,1)S(1)} collective-permute-done((bf16[544,128]{1,0:T(8,128)(2,1)S(1)}, bf16[544,128]{1,0:T(8,128)(2,1)S(1)}, u32[]{:S(2)}, u32[]{:S(2)}) %collective-permute-start.2) | collective-permute-done | bytes 139296 | tf_op jit(solution)/shard_map/ppermute | solution.py:301
  11.5 4.4 %collective-permute-start.3 = (bf16[544,128]{1,0:T(8,128)(2,1)S(1)}, bf16[544,128]{1,0:T(8,128)(2,1)S(1)}, u32[]{:S(2)}, u32[]{:S(2)}) collective-permute-start(bf16[544,128]{1,0:T(8,128)(2,1)S(1)} %collective-permute-done.2.refs_1_), channel_id=1, source_target_pairs={{0,2},{1,3},{2,4},{3,5},{4,6},{5,7},{8,10},{9,11},{10,12},{11,13},... | collective-permute-start | bytes 417800 | tf_op jit(solution)/shard_map/ppermute | solution.py:301
  15.9 1.6 %collective-permute-start.4 = (bf16[544,128]{1,0:T(8,128)(2,1)S(1)}, bf16[544,128]{1,0:T(8,128)(2,1)S(1)}, u32[]{:S(2)}, u32[]{:S(2)}) collective-permute-start(bf16[544,128]{1,0:T(8,128)(2,1)S(1)} %pad_maximum_fusion.refs_0_), channel_id=1, source_target_pairs={{0,16},{16,0},{1,17},{17,1},{2,18},{18,2},{3,19},{19,3},{4,20},{20... | collective-permute-start | bytes 417800 | tf_op jit(solution)/shard_map/ppermute | solution.py:307
  17.4 0.5 collective-permute-start.5
  18.0 0.5 collective-permute-done.3.refs_2_
  18.4 1.5 %collective-permute-start.6 = (bf16[544,128]{1,0:T(8,128)(2,1)S(1)}, bf16[544,128]{1,0:T(8,128)(2,1)S(1)}, u32[]{:S(2)}, u32[]{:S(2)}) collective-permute-start(bf16[544,128]{1,0:T(8,128)(2,1)S(1)} %collective-permute-done.3.refs_2_), channel_id=1, source_target_pairs={{0,16},{16,0},{1,17},{17,1},{2,18},{18,2},{3,19},{19,3},{4,20},{20... | collective-permute-start | bytes 417800 | tf_op jit(solution)/shard_map/ppermute | solution.py:307
  20.0 2.6 %collective-permute-done.4.refs_3_ = bf16[544,128]{1,0:T(8,128)(2,1)S(1)} collective-permute-done((bf16[544,128]{1,0:T(8,128)(2,1)S(1)}, bf16[544,128]{1,0:T(8,128)(2,1)S(1)}, u32[]{:S(2)}, u32[]{:S(2)}) %collective-permute-start.4) | collective-permute-done | bytes 139296 | tf_op jit(solution)/shard_map/ppermute | solution.py:307
  22.5 2.4 %collective-permute-done.5.refs_4_ = bf16[544,128]{1,0:T(8,128)(2,1)S(1)} collective-permute-done((bf16[544,128]{1,0:T(8,128)(2,1)S(1)}, bf16[544,128]{1,0:T(8,128)(2,1)S(1)}, u32[]{:S(2)}, u32[]{:S(2)}) %collective-permute-start.5) | collective-permute-done | bytes 139296 | tf_op jit(solution)/shard_map/ppermute | solution.py:307
  25.0 1.5 %collective-permute-done.6.refs_5_ = bf16[544,128]{1,0:T(8,128)(2,1)S(1)} collective-permute-done((bf16[544,128]{1,0:T(8,128)(2,1)S(1)}, bf16[544,128]{1,0:T(8,128)(2,1)S(1)}, u32[]{:S(2)}, u32[]{:S(2)}) %collective-permute-start.6) | collective-permute-done | bytes 139296 | tf_op jit(solution)/shard_map/ppermute | solution.py:307
  26.5 0.0 collective-permute-done.1.side_rows_ref
  26.5 0.0 copy-done
  26.5 0.0 copy-done.1
  26.5 6.3 %shard_map.95 = (bf16[128,2048]{1,0:T(8,128)(2,1)}, bf16[128,2048]{1,0:T(8,128)(2,1)}, bf16[256,1024]{1,0:T(8,128)(2,1)S(1)}, bf16[512,128]{1,0:T(8,128)(2,1)S(1...) custom-call(bf16[128,2048]{1,0:T(8,128)(2,1)S(1)} %bitcast.12, ...), custom_call_target="tpu_custom_call" | custom-call | flops 2415919104 | bytes 4194304 | tf_op jit(solution)/shard_map/pallas_call | solution.py:334
  32.8 1.6 %collective-permute-start.7 = (bf16[512,128]{1,0:T(8,128)(2,1)S(1)}, bf16[512,128]{1,0:T(8,128)(2,1)S(1)}, u32[]{:S(2)}, u32[]{:S(2)}) collective-permute-start(bf16[512,128]{1,0:T(8,128)(2,1)S(1)} %get-tuple-element.32), channel_id=1, source_target_pairs={{0,16},{16,0},{1,17},{17,1},{2,18},{18,2},{3,19},{19,3},{4,20},{20... | collective-permute-start | bytes 393224 | tf_op jit(solution)/shard_map/ppermute | solution.py:307
  34.4 3.4 %collective-permute-done.7 = bf16[512,128]{1,0:T(8,128)(2,1)S(1)} collective-permute-done((bf16[512,128]{1,0:T(8,128)(2,1)S(1)}, bf16[512,128]{1,0:T(8,128)(2,1)S(1)}, u32[]{:S(2)}, u32[]{:S(2)}) %collective-permute-start.7) | collective-permute-done | bytes 131104 | tf_op jit(solution)/shard_map/ppermute | solution.py:307
  37.9 0.1 collective-permute-start.11
  37.9 1.6 %collective-permute-start.8 = (bf16[512,128]{1,0:T(8,128)(2,1)S(1)}, bf16[512,128]{1,0:T(8,128)(2,1)S(1)}, u32[]{:S(2)}, u32[]{:S(2)}) collective-permute-start(bf16[512,128]{1,0:T(8,128)(2,1)S(1)} %get-tuple-element.36), channel_id=1, source_target_pairs={{0,16},{16,0},{1,17},{17,1},{2,18},{18,2},{3,19},{19,3},{4,20},{20... | collective-permute-start | bytes 393224 | tf_op jit(solution)/shard_map/ppermute | solution.py:307
  39.5 1.3 %collective-permute-start.9 = (bf16[512,128]{1,0:T(8,128)(2,1)S(1)}, bf16[512,128]{1,0:T(8,128)(2,1)S(1)}, u32[]{:S(2)}, u32[]{:S(2)}) collective-permute-start(bf16[512,128]{1,0:T(8,128)(2,1)S(1)} %add_convert_fusion.2), channel_id=1, source_target_pairs={{2,0},{3,1},{4,2},{5,3},{6,4},{7,5},{10,8},{11,9},{12,10},{13,11},... | collective-permute-start | bytes 393224 | tf_op jit(solution)/shard_map/ppermute | solution.py:304
  40.8 3.0 %collective-permute-done.8 = bf16[512,128]{1,0:T(8,128)(2,1)S(1)} collective-permute-done((bf16[512,128]{1,0:T(8,128)(2,1)S(1)}, bf16[512,128]{1,0:T(8,128)(2,1)S(1)}, u32[]{:S(2)}, u32[]{:S(2)}) %collective-permute-start.8) | collective-permute-done | bytes 131104 | tf_op jit(solution)/shard_map/ppermute | solution.py:307
  43.9 4.3 %collective-permute-done.9 = bf16[512,128]{1,0:T(8,128)(2,1)S(1)} collective-permute-done((bf16[512,128]{1,0:T(8,128)(2,1)S(1)}, bf16[512,128]{1,0:T(8,128)(2,1)S(1)}, u32[]{:S(2)}, u32[]{:S(2)}) %collective-permute-start.9) | collective-permute-done | bytes 131104 | tf_op jit(solution)/shard_map/ppermute | solution.py:304
  48.1 0.1 add_convert_fusion.1
  48.2 1.3 %collective-permute-start.10 = (bf16[512,128]{1,0:T(8,128)(2,1)S(1)}, bf16[512,128]{1,0:T(8,128)(2,1)S(1)}, u32[]{:S(2)}, u32[]{:S(2)}) collective-permute-start(bf16[512,128]{1,0:T(8,128)(2,1)S(1)} %add_convert_fusion.1), channel_id=1, source_target_pairs={{2,0},{3,1},{4,2},{5,3},{6,4},{7,5},{10,8},{11,9},{12,10},{13,11},... | collective-permute-start | bytes 393224 | tf_op jit(solution)/shard_map/ppermute | solution.py:304
  49.5 1.7 %collective-permute-start.12 = (bf16[512,128]{1,0:T(8,128)(2,1)S(1)}, bf16[512,128]{1,0:T(8,128)(2,1)S(1)}, u32[]{:S(2)}, u32[]{:S(2)}) collective-permute-start(bf16[512,128]{1,0:T(8,128)(2,1)S(1)} %get-tuple-element.46), channel_id=1, source_target_pairs={{0,16},{16,0},{1,17},{17,1},{2,18},{18,2},{3,19},{19,3},{4,20},{20... | collective-permute-start | bytes 393224 | tf_op jit(solution)/shard_map/ppermute | solution.py:307
  51.2 0.0 collective-permute-done.11.side_ref
  51.2 0.0 copy-start.2
  51.2 0.8 %copy-done.2 = bf16[256,1024]{1,0:T(8,128)(2,1)} copy-done((bf16[256,1024]{1,0:T(8,128)(2,1)}, bf16[256,1024]{1,0:T(8,128)(2,1)S(1)}, u32[]{:S(2)}) %copy-start.2) | copy-done | bytes 524312
  52.0 1.8 %shard_map.96 = (bf16[128,2048]{1,0:T(8,128)(2,1)}, bf16[128,2048]{1,0:T(8,128)(2,1)}) custom-call(bf16[256,1024]{1,0:T(8,128)(2,1)} %copy-done.2, bf16[128,2048]{1,0:T(8,128)(2,1)} %get-tuple-element.39.out_held, bf16[128,2048]{1,0:T(8,128)(2,1)} %get-tuple-element.40.query_grad_held), custom_call_target="tpu_custom_call", output_to_operand_aliasing={{0}: (1, {}), {1}: (2, {})} | custom-call | tf_op jit(solution)/shard_map/pallas_call | solution.py:382
  53.9 2.2 %collective-permute-done.10 = bf16[512,128]{1,0:T(8,128)(2,1)S(1)} collective-permute-done((bf16[512,128]{1,0:T(8,128)(2,1)S(1)}, bf16[512,128]{1,0:T(8,128)(2,1)S(1)}, u32[]{:S(2)}, u32[]{:S(2)}) %collective-permute-start.10) | collective-permute-done | bytes 131104 | tf_op jit(solution)/shard_map/ppermute | solution.py:304
  56.1 0.0 collective-permute-done.12
  56.2 0.1 add_convert_fusion
  56.2 0.1 collective-permute-start.13
  56.3 1.2 %collective-permute-done.13 = bf16[256,128]{1,0:T(8,128)(2,1)S(1)} collective-permute-done((bf16[256,128]{1,0:T(8,128)(2,1)S(1)}, bf16[256,128]{1,0:T(8,128)(2,1)S(1)}, u32[]{:S(2)}, u32[]{:S(2)}) %collective-permute-start.13) | collective-permute-done | bytes 65568 | tf_op jit(solution)/shard_map/ppermute | solution.py:310
  57.6 0.7 %fusion.2 = (bf16[1,128,256]{2,1,0:T(8,128)(2,1)}, bf16[1,128,256]{2,1,0:T(8,128)(2,1)}) fusion(bf16[256,128]{1,0:T(8,128)(2,1)S(1)} %get-tuple-element.48, bf16[256,128]{1,0:T(8,128)(2,1)S(1)} %get-tuple-element.49), kind=kLoop, calls=%fused_computation.9 | loop fusion | flops 262144 | bytes 262144 | tf_op jit(solution)/shard_map/broadcast_in_dim | solution.py:397
  (4 shorter events, 0.1 us)
Async XLA Ops:
  1.6 1.7 %collective-permute-start = (bf16[272,128]{1,0:T(8,128)(2,1)S(1)}, bf16[272,128]{1,0:T(8,128)(2,1)S(1)}, u32[]{:S(2)}, u32[]{:S(2)}) collective-permute-start(bf16[272,128]{1,0:T(8,128)(2,1)S(1)} %get-tuple-element.27), channel_id=1, source_target_pairs={{0,1},{1,0},{2,3},{3,2},{4,5},{5,4},{6,7},{7,6},{8,9},{9,8},{10,11... | collective-permute-start | bytes 208904 | tf_op jit(solution)/shard_map/ppermute | solution.py:310
  2.1 24.4 %copy-start = (bf16[1,128,2048]{2,1,0:T(8,128)(2,1)S(1)}, bf16[1,128,2048]{2,1,0:T(8,128)(2,1)}, u32[]{:S(2)}) copy-start(bf16[1,128,2048]{2,1,0:T(8,128)(2,1)} %param.6) | copy-start | bytes 1572868
  2.1 24.4 %copy-start.1 = (bf16[1,128,2048]{2,1,0:T(8,128)(2,1)S(1)}, bf16[1,128,2048]{2,1,0:T(8,128)(2,1)}, u32[]{:S(2)}) copy-start(bf16[1,128,2048]{2,1,0:T(8,128)(2,1)} %param.9) | copy-start | bytes 1572868
  3.3 23.2 %collective-permute-start.1 = (bf16[256,1024]{1,0:T(8,128)(2,1)S(1)}, bf16[256,1024]{1,0:T(8,128)(2,1)S(1)}, u32[]{:S(2)}, u32[]{:S(2)}) collective-permute-start(bf16[256,1024]{1,0:T(8,128)(2,1)S(1)} %shard_map.94), channel_id=1, source_target_pairs={{0,1},{1,0},{2,3},{3,2},{4,5},{5,4},{6,7},{7,6},{8,9},{9,8},{10,11... | collective-permute-start | bytes 1572872 | tf_op jit(solution)/shard_map/ppermute | solution.py:310
  3.4 8.1 %collective-permute-start.2 = (bf16[544,128]{1,0:T(8,128)(2,1)S(1)}, bf16[544,128]{1,0:T(8,128)(2,1)S(1)}, u32[]{:S(2)}, u32[]{:S(2)}) collective-permute-start(bf16[544,128]{1,0:T(8,128)(2,1)S(1)} %pad_maximum_fusion.refs_0_), channel_id=1, source_target_pairs={{0,2},{1,3},{2,4},{3,5},{4,6},{5,7},{8,10},{9,11},{10,12},{11,13},... | collective-permute-start | bytes 417800 | tf_op jit(solution)/shard_map/ppermute | solution.py:301
  11.5 7.0 %collective-permute-start.3 = (bf16[544,128]{1,0:T(8,128)(2,1)S(1)}, bf16[544,128]{1,0:T(8,128)(2,1)S(1)}, u32[]{:S(2)}, u32[]{:S(2)}) collective-permute-start(bf16[544,128]{1,0:T(8,128)(2,1)S(1)} %collective-permute-done.2.refs_1_), channel_id=1, source_target_pairs={{0,2},{1,3},{2,4},{3,5},{4,6},{5,7},{8,10},{9,11},{10,12},{11,13},... | collective-permute-start | bytes 417800 | tf_op jit(solution)/shard_map/ppermute | solution.py:301
  15.9 6.7 %collective-permute-start.4 = (bf16[544,128]{1,0:T(8,128)(2,1)S(1)}, bf16[544,128]{1,0:T(8,128)(2,1)S(1)}, u32[]{:S(2)}, u32[]{:S(2)}) collective-permute-start(bf16[544,128]{1,0:T(8,128)(2,1)S(1)} %pad_maximum_fusion.refs_0_), channel_id=1, source_target_pairs={{0,16},{16,0},{1,17},{17,1},{2,18},{18,2},{3,19},{19,3},{4,20},{20... | collective-permute-start | bytes 417800 | tf_op jit(solution)/shard_map/ppermute | solution.py:307
  17.4 7.5 %collective-permute-start.5 = (bf16[544,128]{1,0:T(8,128)(2,1)S(1)}, bf16[544,128]{1,0:T(8,128)(2,1)S(1)}, u32[]{:S(2)}, u32[]{:S(2)}) collective-permute-start(bf16[544,128]{1,0:T(8,128)(2,1)S(1)} %collective-permute-done.2.refs_1_), channel_id=1, source_target_pairs={{0,16},{16,0},{1,17},{17,1},{2,18},{18,2},{3,19},{19,3},{4,20},{20... | collective-permute-start | bytes 417800 | tf_op jit(solution)/shard_map/ppermute | solution.py:307
  18.4 8.0 %collective-permute-start.6 = (bf16[544,128]{1,0:T(8,128)(2,1)S(1)}, bf16[544,128]{1,0:T(8,128)(2,1)S(1)}, u32[]{:S(2)}, u32[]{:S(2)}) collective-permute-start(bf16[544,128]{1,0:T(8,128)(2,1)S(1)} %collective-permute-done.3.refs_2_), channel_id=1, source_target_pairs={{0,16},{16,0},{1,17},{17,1},{2,18},{18,2},{3,19},{19,3},{4,20},{20... | collective-permute-start | bytes 417800 | tf_op jit(solution)/shard_map/ppermute | solution.py:307
  32.8 5.0 %collective-permute-start.7 = (bf16[512,128]{1,0:T(8,128)(2,1)S(1)}, bf16[512,128]{1,0:T(8,128)(2,1)S(1)}, u32[]{:S(2)}, u32[]{:S(2)}) collective-permute-start(bf16[512,128]{1,0:T(8,128)(2,1)S(1)} %get-tuple-element.32), channel_id=1, source_target_pairs={{0,16},{16,0},{1,17},{17,1},{2,18},{18,2},{3,19},{19,3},{4,20},{20... | collective-permute-start | bytes 393224 | tf_op jit(solution)/shard_map/ppermute | solution.py:307
  37.9 13.4 %collective-permute-start.11 = (bf16[256,1024]{1,0:T(8,128)(2,1)S(1)}, bf16[256,1024]{1,0:T(8,128)(2,1)S(1)}, u32[]{:S(2)}, u32[]{:S(2)}) collective-permute-start(bf16[256,1024]{1,0:T(8,128)(2,1)S(1)} %get-tuple-element.38), channel_id=1, source_target_pairs={{0,1},{1,0},{2,3},{3,2},{4,5},{5,4},{6,7},{7,6},{8,9},{9,8},{10,11... | collective-permute-start | bytes 1572872 | tf_op jit(solution)/shard_map/ppermute | solution.py:310
  37.9 5.9 %collective-permute-start.8 = (bf16[512,128]{1,0:T(8,128)(2,1)S(1)}, bf16[512,128]{1,0:T(8,128)(2,1)S(1)}, u32[]{:S(2)}, u32[]{:S(2)}) collective-permute-start(bf16[512,128]{1,0:T(8,128)(2,1)S(1)} %get-tuple-element.36), channel_id=1, source_target_pairs={{0,16},{16,0},{1,17},{17,1},{2,18},{18,2},{3,19},{19,3},{4,20},{20... | collective-permute-start | bytes 393224 | tf_op jit(solution)/shard_map/ppermute | solution.py:307
  39.5 8.6 %collective-permute-start.9 = (bf16[512,128]{1,0:T(8,128)(2,1)S(1)}, bf16[512,128]{1,0:T(8,128)(2,1)S(1)}, u32[]{:S(2)}, u32[]{:S(2)}) collective-permute-start(bf16[512,128]{1,0:T(8,128)(2,1)S(1)} %add_convert_fusion.2), channel_id=1, source_target_pairs={{2,0},{3,1},{4,2},{5,3},{6,4},{7,5},{10,8},{11,9},{12,10},{13,11},... | collective-permute-start | bytes 393224 | tf_op jit(solution)/shard_map/ppermute | solution.py:304
  48.2 7.9 %collective-permute-start.10 = (bf16[512,128]{1,0:T(8,128)(2,1)S(1)}, bf16[512,128]{1,0:T(8,128)(2,1)S(1)}, u32[]{:S(2)}, u32[]{:S(2)}) collective-permute-start(bf16[512,128]{1,0:T(8,128)(2,1)S(1)} %add_convert_fusion.1), channel_id=1, source_target_pairs={{2,0},{3,1},{4,2},{5,3},{6,4},{7,5},{10,8},{11,9},{12,10},{13,11},... | collective-permute-start | bytes 393224 | tf_op jit(solution)/shard_map/ppermute | solution.py:304
  49.5 6.6 %collective-permute-start.12 = (bf16[512,128]{1,0:T(8,128)(2,1)S(1)}, bf16[512,128]{1,0:T(8,128)(2,1)S(1)}, u32[]{:S(2)}, u32[]{:S(2)}) collective-permute-start(bf16[512,128]{1,0:T(8,128)(2,1)S(1)} %get-tuple-element.46), channel_id=1, source_target_pairs={{0,16},{16,0},{1,17},{17,1},{2,18},{18,2},{3,19},{19,3},{4,20},{20... | collective-permute-start | bytes 393224 | tf_op jit(solution)/shard_map/ppermute | solution.py:307
  51.2 0.8 %copy-start.2 = (bf16[256,1024]{1,0:T(8,128)(2,1)}, bf16[256,1024]{1,0:T(8,128)(2,1)S(1)}, u32[]{:S(2)}) copy-start(bf16[256,1024]{1,0:T(8,128)(2,1)S(1)} %collective-permute-done.11.side_ref) | copy-start | bytes 1572868
  56.2 1.3 %collective-permute-start.13 = (bf16[256,128]{1,0:T(8,128)(2,1)S(1)}, bf16[256,128]{1,0:T(8,128)(2,1)S(1)}, u32[]{:S(2)}, u32[]{:S(2)}) collective-permute-start(bf16[256,128]{1,0:T(8,128)(2,1)S(1)} %slice.17), channel_id=1, source_target_pairs={{0,1},{1,0},{2,3},{3,2},{4,5},{5,4},{6,7},{7,6},{8,9},{9,8},{10,11... | collective-permute-start | bytes 196616 | tf_op jit(solution)/shard_map/ppermute | solution.py:310
